TPU v7x, 32 devices: a whole 2x2x4 slice. The times are simulated.
32 devices in a mesh: groups: 2 (over x), lon: 16 (over z, y, core).
Axes of the slice: x: 2, y: 2, z: 4, core: 2. Of those that a mesh axis runs over, the one named last changes fastest.
Arguments:
- inputs: bfloat16 [16, 896, 512], P('groups', 'lon'), parts along dimension 0, may hold values from -6 to 6
- support: int32 [16], P('groups'), parts along dimension 0, may hold values from 1 to 4, as said below
- basis_table: bfloat16 [9, 16, 3, 449], P(None, 'groups'), parts along dimension 1, may hold values from -0.15625 to 0.15625
- mixing: bfloat16 [4608, 512], P('lon'), may hold values from -0.09375 to 0.09375
Outputs:
- output_field: bfloat16 [16, 896, 512], P('groups', 'lon'), parts along dimension 0
There are 2 independent parts, one for each index of `groups`. A program takes and returns all parts, laid end to end along the dimension named above; an argument that names none is the same for every part. Nothing has to cross between parts.
Inputs may be any that keep to these rules, and one draw needn't show every extreme that they name: `support`: in the first slab some band reaches 4.
All inputs are finite; a program needn't handle non-finite values.
Results may differ from a plain program's by a relative error of at most 0.0051.
Values may be sent and summed in bfloat16 or wider, within the bound.
No kernel may reach another device: no remote copies, remote signals or barrier semaphores. Data moves between devices by JAX's collectives and lax.ppermute only.
A program may use at most 64 MiB of HBM per device.

v0:
```python
import jax
import jax.numpy as jnp
from jax import lax
from jax.sharding import PartitionSpec as P

MAXS = 4


def shifted(value, axis, steps):
    count = lax.axis_size(axis)
    pairs = [(source, (source + steps) % count) for source in range(count)]
    return lax.ppermute(value, axis, pairs)


def band_basis(basis_table, support, band, longitudes, reach):
    span = (2 * reach + 1) * longitudes
    table_rows = lax.dynamic_index_in_dim(basis_table, band, 1, False)
    filters = table_rows.shape[0]
    widened = jnp.pad(table_rows, ((0, 0), (0, 0), (0, span + 1 - table_rows.shape[2])))
    tiled = jnp.broadcast_to(widened[:, :, None, :], (filters, 3, longitudes, span + 1))
    tiled = tiled.reshape(filters, 3, longitudes * (span + 1))[:, :, : longitudes * span]
    picked = tiled.reshape(filters, 3, longitudes, span)
    out_pos = jnp.arange(longitudes)[:, None]
    win_pos = jnp.arange(span)[None, :]
    offsets = win_pos - reach * longitudes - out_pos
    width = lax.dynamic_index_in_dim(support, band, 0, False)
    within = jnp.abs(offsets) <= width * longitudes
    picked = jnp.where(within[None, None], picked, jnp.zeros_like(picked))
    return picked.transpose(0, 2, 1, 3).reshape(filters * longitudes, 3 * span)


def convolve(window, basis_table, support, longitudes):
    bands, span, channels = window.shape
    filters = basis_table.shape[0]
    padded = jnp.pad(window, ((1, 1), (0, 0), (0, 0)))

    def one_band(band):
        rows = lax.dynamic_slice_in_dim(padded, band, 3, 0).reshape(3 * span, channels)
        toeplitz = band_basis(basis_table, support, band, longitudes, MAXS)
        product = jnp.dot(toeplitz, rows, preferred_element_type=jnp.float32)
        return (
            product.reshape(filters, longitudes, channels).transpose(1, 0, 2).astype(jnp.bfloat16)
        )

    return lax.map(one_band, jnp.arange(bands))


def west_start(block, reach):
    return shifted(block, "lon", reach)


def east_step(block):
    return shifted(block, "lon", -1)


def on_device(inputs, support, basis_table, mixing):
    bands, longitudes, channels = inputs.shape
    filters = basis_table.shape[0]
    current = west_start(inputs, MAXS)
    received = [current]
    for step in range(1, 2 * MAXS + 1):
        current = east_step(current)
        received.append(current)
    window = jnp.concatenate(received, axis=1)
    convolved = convolve(window, basis_table, support, longitudes)
    flattened = convolved.reshape(bands * longitudes, filters * channels)
    summed = jnp.dot(
        flattened,
        lax.all_gather(mixing, "lon", axis=0, tiled=True),
        preferred_element_type=jnp.float32,
    )
    return jax.nn.gelu(summed).astype(jnp.bfloat16).reshape(bands, longitudes, mixing.shape[1])


def solution(mesh):
    placed = (P("groups", "lon", None), P("groups"), P(None, "groups", None, None), P("lon", None))
    return jax.shard_map(
        on_device, mesh=mesh, in_specs=placed, out_specs=P("groups", "lon", None), check_vma=False
    )
```

profile of v0, /device:TPU:0, one launch (start us, length us, event | category | flops | bytes accessed | tf_op | source)
XLA Modules:
  0.0 311.6 jit_solution(15892357495941110552)
XLA Ops:
  9.6 12.8 %collective-permute-done = bf16[8,56,512]{2,1,0:T(8,128)(2,1)S(1)} collective-permute-done((bf16[8,56,512]{2,1,0:T(8,128)(2,1)}, bf16[8,56,512]{2,1,0:T(8,128)(2,1)S(1)}, u32[]{:S(2)}, u32[]{:S(2)}) %collective-permute-start) | collective-permute-done | bytes 458784 | tf_op jit(solution)/shard_map/ppermute | solution.py:12
  23.6 6.0 %collective-permute-done.1 = bf16[8,56,512]{2,1,0:T(8,128)(2,1)S(1)} collective-permute-done((bf16[8,56,512]{2,1,0:T(8,128)(2,1)S(1)}, bf16[8,56,512]{2,1,0:T(8,128)(2,1)S(1)}, u32[]{:S(2)}, u32[]{:S(2)}) %collective-permute-start.1) | collective-permute-done | bytes 458784 | tf_op jit(solution)/shard_map/ppermute | solution.py:12
  29.6 4.6 %collective-permute-start.2 = (bf16[8,56,512]{2,1,0:T(8,128)(2,1)S(1)}, bf16[8,56,512]{2,1,0:T(8,128)(2,1)S(1)}, u32[]{:S(2)}, u32[]{:S(2)}) collective-permute-start(bf16[8,56,512]{2,1,0:T(8,128)(2,1)S(1)} %collective-permute-done.1), channel_id=1, source_target_pairs={{0,15},{1,0},{2,1},{3,2},{4,3},{5,4},{6,5},{7,6},{8,7},{9,8},{10,9... | collective-permute-start | bytes 1376264 | tf_op jit(solution)/shard_map/ppermute | solution.py:12
  34.2 6.0 %collective-permute-done.2 = bf16[8,56,512]{2,1,0:T(8,128)(2,1)S(1)} collective-permute-done((bf16[8,56,512]{2,1,0:T(8,128)(2,1)S(1)}, bf16[8,56,512]{2,1,0:T(8,128)(2,1)S(1)}, u32[]{:S(2)}, u32[]{:S(2)}) %collective-permute-start.2) | collective-permute-done | bytes 458784 | tf_op jit(solution)/shard_map/ppermute | solution.py:12
  40.2 4.6 %collective-permute-start.3 = (bf16[8,56,512]{2,1,0:T(8,128)(2,1)S(1)}, bf16[8,56,512]{2,1,0:T(8,128)(2,1)S(1)}, u32[]{:S(2)}, u32[]{:S(2)}) collective-permute-start(bf16[8,56,512]{2,1,0:T(8,128)(2,1)S(1)} %collective-permute-done.2), channel_id=1, source_target_pairs={{0,15},{1,0},{2,1},{3,2},{4,3},{5,4},{6,5},{7,6},{8,7},{9,8},{10,9... | collective-permute-start | bytes 1376264 | tf_op jit(solution)/shard_map/ppermute | solution.py:12
  44.8 6.0 %collective-permute-done.3 = bf16[8,56,512]{2,1,0:T(8,128)(2,1)S(1)} collective-permute-done((bf16[8,56,512]{2,1,0:T(8,128)(2,1)S(1)}, bf16[8,56,512]{2,1,0:T(8,128)(2,1)S(1)}, u32[]{:S(2)}, u32[]{:S(2)}) %collective-permute-start.3) | collective-permute-done | bytes 458784 | tf_op jit(solution)/shard_map/ppermute | solution.py:12
  55.4 11.5 %collective-permute-done.4 = bf16[8,56,512]{2,1,0:T(8,128)(2,1)S(1)} collective-permute-done((bf16[8,56,512]{2,1,0:T(8,128)(2,1)S(1)}, bf16[8,56,512]{2,1,0:T(8,128)(2,1)S(1)}, u32[]{:S(2)}, u32[]{:S(2)}) %collective-permute-start.4) | collective-permute-done | bytes 458784 | tf_op jit(solution)/shard_map/ppermute | solution.py:12
  71.5 15.5 %collective-permute-done.5 = bf16[8,56,512]{2,1,0:T(8,128)(2,1)S(1)} collective-permute-done((bf16[8,56,512]{2,1,0:T(8,128)(2,1)S(1)}, bf16[8,56,512]{2,1,0:T(8,128)(2,1)S(1)}, u32[]{:S(2)}, u32[]{:S(2)}) %collective-permute-start.5) | collective-permute-done | bytes 458784 | tf_op jit(solution)/shard_map/ppermute | solution.py:12
  87.0 4.6 %collective-permute-start.6 = (bf16[8,56,512]{2,1,0:T(8,128)(2,1)S(1)}, bf16[8,56,512]{2,1,0:T(8,128)(2,1)}, u32[]{:S(2)}, u32[]{:S(2)}) collective-permute-start(bf16[8,56,512]{2,1,0:T(8,128)(2,1)S(1)} %collective-permute-done.5), channel_id=1, source_target_pairs={{0,15},{1,0},{2,1},{3,2},{4,3},{5,4},{6,5},{7,6},{8,7},{9,8},{10,9... | collective-permute-start | bytes 1376264 | tf_op jit(solution)/shard_map/ppermute | solution.py:12
  92.8 8.9 %collective-permute-done.6 = bf16[8,56,512]{2,1,0:T(8,128)(2,1)} collective-permute-done((bf16[8,56,512]{2,1,0:T(8,128)(2,1)S(1)}, bf16[8,56,512]{2,1,0:T(8,128)(2,1)}, u32[]{:S(2)}, u32[]{:S(2)}) %collective-permute-start.6) | collective-permute-done | bytes 458784 | tf_op jit(solution)/shard_map/ppermute | solution.py:12
  101.7 4.8 %collective-permute-start.7 = (bf16[8,56,512]{2,1,0:T(8,128)(2,1)}, bf16[8,56,512]{2,1,0:T(8,128)(2,1)S(1)}, u32[]{:S(2)}, u32[]{:S(2)}) collective-permute-start(bf16[8,56,512]{2,1,0:T(8,128)(2,1)} %collective-permute-done.6), channel_id=1, source_target_pairs={{0,15},{1,0},{2,1},{3,2},{4,3},{5,4},{6,5},{7,6},{8,7},{9,8},{10,9... | collective-permute-start | bytes 1376264 | tf_op jit(solution)/shard_map/ppermute | solution.py:12
  106.6 6.2 %collective-permute-done.7 = bf16[8,56,512]{2,1,0:T(8,128)(2,1)S(1)} collective-permute-done((bf16[8,56,512]{2,1,0:T(8,128)(2,1)}, bf16[8,56,512]{2,1,0:T(8,128)(2,1)S(1)}, u32[]{:S(2)}, u32[]{:S(2)}) %collective-permute-start.7) | collective-permute-done | bytes 458784 | tf_op jit(solution)/shard_map/ppermute | solution.py:12
  118.4 4.8 %collective-permute-done.8 = bf16[8,56,512]{2,1,0:T(8,128)(2,1)S(1)} collective-permute-done((bf16[8,56,512]{2,1,0:T(8,128)(2,1)S(1)}, bf16[8,56,512]{2,1,0:T(8,128)(2,1)S(1)}, u32[]{:S(2)}, u32[]{:S(2)}) %collective-permute-start.8) | collective-permute-done | bytes 458784 | tf_op jit(solution)/shard_map/ppermute | solution.py:12
  126.0 160.8 %while.12 = (s32[]{:T(128)}, bf16[8,56,9,512]{3,1,2,0:T(8,128)(2,1)}, s32[8]{0:T(128)S(1)}, s32[8]{0:T(128)S(1)}, bf16[9,8,3,449]{3,2,0,1:T(4,128)(2,1)S(1)}, /*...) while((s32[]{:T(128)}, ...), condition=%wide.region_1.2_spmd, body=%wide.region_0.1_spmd.sunk | while | flops 781442432 | bytes 11430720 | solution.py:45
  131.3 5.1 %reshape.62 = bf16[9,3,28280]{2,1,0:T(4,128)(2,1)S(1)} reshape(bf16[9,3,56,505]{3,2,1,0:T(8,128)(2,1)} %broadcast_in_dim.50) | data formatting | bytes 3054240 | tf_op jit(solution)/shard_map/while/body/eval_jaxpr/reshape | solution.py:21
  151.4 5.1 %reshape.62 = bf16[9,3,28280]{2,1,0:T(4,128)(2,1)S(1)} reshape(bf16[9,3,56,505]{3,2,1,0:T(8,128)(2,1)} %broadcast_in_dim.50) | data formatting | bytes 3054240 | tf_op jit(solution)/shard_map/while/body/eval_jaxpr/reshape | solution.py:21
  171.5 5.1 %reshape.62 = bf16[9,3,28280]{2,1,0:T(4,128)(2,1)S(1)} reshape(bf16[9,3,56,505]{3,2,1,0:T(8,128)(2,1)} %broadcast_in_dim.50) | data formatting | bytes 3054240 | tf_op jit(solution)/shard_map/while/body/eval_jaxpr/reshape | solution.py:21
  191.6 5.1 %reshape.62 = bf16[9,3,28280]{2,1,0:T(4,128)(2,1)S(1)} reshape(bf16[9,3,56,505]{3,2,1,0:T(8,128)(2,1)} %broadcast_in_dim.50) | data formatting | bytes 3054240 | tf_op jit(solution)/shard_map/while/body/eval_jaxpr/reshape | solution.py:21
  211.6 5.1 %reshape.62 = bf16[9,3,28280]{2,1,0:T(4,128)(2,1)S(1)} reshape(bf16[9,3,56,505]{3,2,1,0:T(8,128)(2,1)} %broadcast_in_dim.50) | data formatting | bytes 3054240 | tf_op jit(solution)/shard_map/while/body/eval_jaxpr/reshape | solution.py:21
  231.8 5.1 %reshape.62 = bf16[9,3,28280]{2,1,0:T(4,128)(2,1)S(1)} reshape(bf16[9,3,56,505]{3,2,1,0:T(8,128)(2,1)} %broadcast_in_dim.50) | data formatting | bytes 3054240 | tf_op jit(solution)/shard_map/while/body/eval_jaxpr/reshape | solution.py:21
  251.9 5.1 %reshape.62 = bf16[9,3,28280]{2,1,0:T(4,128)(2,1)S(1)} reshape(bf16[9,3,56,505]{3,2,1,0:T(8,128)(2,1)} %broadcast_in_dim.50) | data formatting | bytes 3054240 | tf_op jit(solution)/shard_map/while/body/eval_jaxpr/reshape | solution.py:21
  272.0 5.1 %reshape.62 = bf16[9,3,28280]{2,1,0:T(4,128)(2,1)S(1)} reshape(bf16[9,3,56,505]{3,2,1,0:T(8,128)(2,1)} %broadcast_in_dim.50) | data formatting | bytes 3054240 | tf_op jit(solution)/shard_map/while/body/eval_jaxpr/reshape | solution.py:21
  291.2 6.7 %copy.9 = bf16[56,8,9,512]{3,1,2,0:T(8,128)(2,1)} copy(bf16[56,8,9,512]{3,2,1,0:T(8,128)(2,1)S(1)} %bitcast.67) | data formatting | bytes 8257536
  297.9 6.8 %fusion.36 = bf16[448,512]{1,0:T(8,128)(2,1)} fusion(bf16[448,4608]{1,0:T(8,128)(2,1)} %bitcast.68, bf16[4608,512]{1,0:T(8,128)(2,1)} %all-gather.2.cloned.1.call-done), kind=kOutput, calls=%fused_computation.24 | convolution fusion | flops 2115993600 | bytes 9306112 | tf_op jit(solution)/shard_map/dot_general | solution.py:67
  (96 shorter events, 114.9 us)
Async XLA Ops:
  6.5 291.4 %all-gather.2.cloned.1.call-start = ((), (), s32[]{:S(2)}) async-start(), calls=%async_computation | async-start | bytes 5013504 | tf_op jit(solution)/shard_map/all_gather | solution.py:69
  6.5 15.8 %collective-permute-start = (bf16[8,56,512]{2,1,0:T(8,128)(2,1)}, bf16[8,56,512]{2,1,0:T(8,128)(2,1)S(1)}, u32[]{:S(2)}, u32[]{:S(2)}) collective-permute-start(bf16[8,56,512]{2,1,0:T(8,128)(2,1)} %param.6), channel_id=1, source_target_pairs={{0,4},{1,5},{2,6},{3,7},{4,8},{5,9},{6,10},{7,11},{8,12},{9,13},{1... | collective-permute-start | bytes 1376264 | tf_op jit(solution)/shard_map/ppermute | solution.py:12
  22.3 7.3 %collective-permute-start.1 = (bf16[8,56,512]{2,1,0:T(8,128)(2,1)S(1)}, bf16[8,56,512]{2,1,0:T(8,128)(2,1)S(1)}, u32[]{:S(2)}, u32[]{:S(2)}) collective-permute-start(bf16[8,56,512]{2,1,0:T(8,128)(2,1)S(1)} %collective-permute-done), channel_id=1, source_target_pairs={{0,15},{1,0},{2,1},{3,2},{4,3},{5,4},{6,5},{7,6},{8,7},{9,8},{10,9... | collective-permute-start | bytes 1376264 | tf_op jit(solution)/shard_map/ppermute | solution.py:12
  29.6 10.6 %collective-permute-start.2 = (bf16[8,56,512]{2,1,0:T(8,128)(2,1)S(1)}, bf16[8,56,512]{2,1,0:T(8,128)(2,1)S(1)}, u32[]{:S(2)}, u32[]{:S(2)}) collective-permute-start(bf16[8,56,512]{2,1,0:T(8,128)(2,1)S(1)} %collective-permute-done.1), channel_id=1, source_target_pairs={{0,15},{1,0},{2,1},{3,2},{4,3},{5,4},{6,5},{7,6},{8,7},{9,8},{10,9... | collective-permute-start | bytes 1376264 | tf_op jit(solution)/shard_map/ppermute | solution.py:12
  40.2 10.6 %collective-permute-start.3 = (bf16[8,56,512]{2,1,0:T(8,128)(2,1)S(1)}, bf16[8,56,512]{2,1,0:T(8,128)(2,1)S(1)}, u32[]{:S(2)}, u32[]{:S(2)}) collective-permute-start(bf16[8,56,512]{2,1,0:T(8,128)(2,1)S(1)} %collective-permute-done.2), channel_id=1, source_target_pairs={{0,15},{1,0},{2,1},{3,2},{4,3},{5,4},{6,5},{7,6},{8,7},{9,8},{10,9... | collective-permute-start | bytes 1376264 | tf_op jit(solution)/shard_map/ppermute | solution.py:12
  50.8 16.1 %collective-permute-start.4 = (bf16[8,56,512]{2,1,0:T(8,128)(2,1)S(1)}, bf16[8,56,512]{2,1,0:T(8,128)(2,1)S(1)}, u32[]{:S(2)}, u32[]{:S(2)}) collective-permute-start(bf16[8,56,512]{2,1,0:T(8,128)(2,1)S(1)} %collective-permute-done.3), channel_id=1, source_target_pairs={{0,15},{1,0},{2,1},{3,2},{4,3},{5,4},{6,5},{7,6},{8,7},{9,8},{10,9... | collective-permute-start | bytes 1376264 | tf_op jit(solution)/shard_map/ppermute | solution.py:12
  66.9 20.2 %collective-permute-start.5 = (bf16[8,56,512]{2,1,0:T(8,128)(2,1)S(1)}, bf16[8,56,512]{2,1,0:T(8,128)(2,1)S(1)}, u32[]{:S(2)}, u32[]{:S(2)}) collective-permute-start(bf16[8,56,512]{2,1,0:T(8,128)(2,1)S(1)} %collective-permute-done.4), channel_id=1, source_target_pairs={{0,15},{1,0},{2,1},{3,2},{4,3},{5,4},{6,5},{7,6},{8,7},{9,8},{10,9... | collective-permute-start | bytes 1376264 | tf_op jit(solution)/shard_map/ppermute | solution.py:12
  87.0 14.7 %collective-permute-start.6 = (bf16[8,56,512]{2,1,0:T(8,128)(2,1)S(1)}, bf16[8,56,512]{2,1,0:T(8,128)(2,1)}, u32[]{:S(2)}, u32[]{:S(2)}) collective-permute-start(bf16[8,56,512]{2,1,0:T(8,128)(2,1)S(1)} %collective-permute-done.5), channel_id=1, source_target_pairs={{0,15},{1,0},{2,1},{3,2},{4,3},{5,4},{6,5},{7,6},{8,7},{9,8},{10,9... | collective-permute-start | bytes 1376264 | tf_op jit(solution)/shard_map/ppermute | solution.py:12
  101.7 11.1 %collective-permute-start.7 = (bf16[8,56,512]{2,1,0:T(8,128)(2,1)}, bf16[8,56,512]{2,1,0:T(8,128)(2,1)S(1)}, u32[]{:S(2)}, u32[]{:S(2)}) collective-permute-start(bf16[8,56,512]{2,1,0:T(8,128)(2,1)} %collective-permute-done.6), channel_id=1, source_target_pairs={{0,15},{1,0},{2,1},{3,2},{4,3},{5,4},{6,5},{7,6},{8,7},{9,8},{10,9... | collective-permute-start | bytes 1376264 | tf_op jit(solution)/shard_map/ppermute | solution.py:12
  112.8 10.5 %collective-permute-start.8 = (bf16[8,56,512]{2,1,0:T(8,128)(2,1)S(1)}, bf16[8,56,512]{2,1,0:T(8,128)(2,1)S(1)}, u32[]{:S(2)}, u32[]{:S(2)}) collective-permute-start(bf16[8,56,512]{2,1,0:T(8,128)(2,1)S(1)} %collective-permute-done.7), channel_id=1, source_target_pairs={{0,15},{1,0},{2,1},{3,2},{4,3},{5,4},{6,5},{7,6},{8,7},{9,8},{10,9... | collective-permute-start | bytes 1376264 | tf_op jit(solution)/shard_map/ppermute | solution.py:12
  123.3 2.7 copy-start
Sparse Core Ops, SparseCore 0:
  44.9 59.1 all-gather.1
where the time goes:
time: 313 us; the launch traced here: 312 us
  local copies, waits for them, and re-layouts  114 us (36%)
  waiting for transfers between devices  77.7 us (25%)
  starting transfers between devices  36.6 us (12%)
  matrix products  36.5 us (12%)
  loops' own time  32.6 us (10%)
  between operations  13.5 us (4%)
    ppermute x9, waiting for transfers between devices, shifted(): return lax.ppermute(value, axis, pairs)  77.7 us
    reshape x8, local copies, waits for them, and re-layouts, band_basis(): tiled.reshape(filters, 3, longitudes * (span + 1))[:, :, :longitudes * span]  40.8 us
    reshape x8, local copies, waits for them, and re-layouts, band_basis(): picked = tiled.reshape(filters, 3, longitudes, span)  36.8 us
    ppermute x9, starting transfers between devices, shifted(): return lax.ppermute(value, axis, pairs)  36.6 us
    another operation x1, loops' own time, convolve(): return lax.map(one_band, jnp.arange(bands))  32.6 us
    dot_general x8, matrix products, one_band(): product = jnp.dot(toeplitz, rows, preferred_element_type=jnp.float32)  29.7 us
    broadcast_in_dim x8, local copies, waits for them, and re-layouts, band_basis(): jnp.broadcast_to(widened[:, :, None, :], (filters, 3, longitudes, span + 1))  10.2 us
    unnamed x11, local copies, waits for them, and re-layouts  8.02 us
  transfers between devices with their start and end apart: 10, of which 9 were waited for; matrix products, arithmetic and copies ran while one was open for 46% of the time, Pallas kernels for 0%

commit v1 on v0

v1 whole, which is shorter than its diff:
```python
import jax
import jax.numpy as jnp
from jax import lax
from jax.experimental import pallas as pl
from jax.experimental.pallas import tpu as pltpu
from jax.sharding import PartitionSpec as P

MAXS = 4
UNIT = 16
VMEM = 48 << 20


def send(value, axis, target_of):
    count = lax.axis_size(axis)
    return lax.ppermute(value, axis, [(s, target_of(s)) for s in range(count)])


def round_up(value, step):
    return -(-value // step) * step


def packed_basis(basis_table, support, longitudes, segment):
    filters, bands, three, offsets = basis_table.shape
    distance = jnp.abs(jnp.arange(offsets) - MAXS * longitudes)
    within = distance[None, :] <= (support * longitudes)[:, None]
    rows = jnp.where(within[None, :, None, :], basis_table, jnp.zeros_like(basis_table))
    rows = jnp.pad(rows, ((0, 0), (0, 0), (0, 0), (0, segment - offsets)))
    rows = rows.transpose(1, 0, 2, 3).reshape(bands, filters, three * segment)
    return rows.astype(jnp.float32)


def toeplitz(packed, longitudes):
    bands, filters, lanes = packed.shape
    rows = round_up(filters * longitudes, UNIT)

    def body(packed_ref, out_ref):
        def block(k):
            row = jnp.broadcast_to(packed_ref[0, k : k + 1, :], (longitudes, lanes))
            return pltpu.roll(row, 0, 1, stride=1, stride_axis=0)

        for k in range(0, filters, 2):
            start = k * longitudes
            if k + 1 < filters:
                pair = jnp.concatenate([block(k), block(k + 1)], 0)
            else:
                tail = jnp.zeros((rows - start - longitudes, lanes), jnp.float32)
                pair = jnp.concatenate([block(k), tail], 0)
            out_ref[0, start : start + pair.shape[0], :] = pair.astype(jnp.bfloat16)

    return pl.pallas_call(
        body,
        grid=(bands,),
        in_specs=[pl.BlockSpec((1, filters, lanes), lambda i: (i, 0, 0))],
        out_specs=pl.BlockSpec((1, rows, lanes), lambda i: (i, 0, 0)),
        out_shape=jax.ShapeDtypeStruct((bands, rows, lanes), jnp.bfloat16),
        compiler_params=pltpu.CompilerParams(vmem_limit_bytes=VMEM),
        name="toeplitz",
    )(packed)


def convolve_and_mix(place, matrices, planes, weights, filters):
    _, bands, longitudes, chans = planes[0].shape
    rows, lanes = matrices.shape[1:]
    segment = lanes // 3
    span = 3 * MAXS * longitudes
    window = (2 * MAXS + 1) * longitudes
    outs = weights.shape[1]
    used = filters * longitudes

    def body(place_ref, t_ref, west_ref, own_ref, east_ref, w_ref, mine_ref, rest_ref, line, windows):
        band = pl.program_id(0)
        here = place_ref[0]

        def fill(b):
            for t, ref in enumerate((west_ref, own_ref, east_ref)):
                for p in range(MAXS):
                    start = (t * MAXS + p) * longitudes
                    line[start : start + longitudes, :] = ref[p ^ here, b].astype(jnp.float32)
            for r in range(MAXS):
                first = pl.multiple_of((r ^ here) * longitudes, 8)
                part = line[pl.ds(first, segment), :].astype(jnp.bfloat16)
                start = pl.multiple_of((b + 1) * segment, segment)
                windows[pl.ds(start, segment), r * chans : (r + 1) * chans] = part

        @pl.when(band == 0)
        def _():
            line[span:, :] = jnp.zeros((line.shape[0] - span, chans), jnp.float32)
            windows[0:segment, :] = jnp.zeros((segment, MAXS * chans), jnp.bfloat16)
            last = (bands + 1) * segment
            windows[last : last + segment, :] = jnp.zeros((segment, MAXS * chans), jnp.bfloat16)
            fill(0)

        @pl.when(band + 1 < bands)
        def _():
            fill(band + 1)

        start = pl.multiple_of(band * segment, segment)
        conv = jnp.dot(t_ref[0], windows[pl.ds(start, lanes), :], preferred_element_type=jnp.float32)
        conv = conv[:used]
        mixed_in = jnp.concatenate(
            [
                jnp.concatenate(
                    [
                        conv[k * longitudes : (k + 1) * longitudes, r * chans : (r + 1) * chans]
                        for k in range(filters)
                    ],
                    1,
                )
                for r in range(MAXS)
            ],
            0,
        ).astype(jnp.bfloat16)
        mixed = jnp.dot(mixed_in, w_ref[...], preferred_element_type=jnp.float32)
        mine_ref[0] = mixed[:longitudes]
        for r in range(1, MAXS):
            rest_ref[r - 1, 0] = mixed[r * longitudes : (r + 1) * longitudes].astype(jnp.bfloat16)

    whole = pl.BlockSpec((MAXS, bands, longitudes, chans), lambda i: (0, 0, 0, 0))
    return pl.pallas_call(
        body,
        grid=(bands,),
        in_specs=[
            pl.BlockSpec(memory_space=pltpu.SMEM),
            pl.BlockSpec((1, rows, lanes), lambda i: (i, 0, 0)),
            whole,
            whole,
            whole,
            pl.BlockSpec(weights.shape, lambda i: (0, 0)),
        ],
        out_specs=[
            pl.BlockSpec((1, longitudes, outs), lambda i: (i, 0, 0)),
            pl.BlockSpec((MAXS - 1, 1, longitudes, outs), lambda i: (0, i, 0, 0)),
        ],
        out_shape=[
            jax.ShapeDtypeStruct((bands, longitudes, outs), jnp.float32),
            jax.ShapeDtypeStruct((MAXS - 1, bands, longitudes, outs), jnp.bfloat16),
        ],
        scratch_shapes=[
            pltpu.VMEM((MAXS * longitudes + round_up(window, segment) + 2 * longitudes, chans), jnp.float32),
            pltpu.VMEM(((bands + 2) * segment, MAXS * chans), jnp.bfloat16),
        ],
        compiler_params=pltpu.CompilerParams(vmem_limit_bytes=VMEM),
        name="convolve_and_mix",
    )(place, matrices, *planes, weights)


def finish(mine, others):
    bands, longitudes, outs = mine.shape

    def body(mine_ref, a_ref, b_ref, c_ref, out_ref):
        total = mine_ref[...] + a_ref[...].astype(jnp.float32)
        total += b_ref[...].astype(jnp.float32) + c_ref[...].astype(jnp.float32)
        out_ref[...] = jax.nn.gelu(total).astype(jnp.bfloat16)

    block = pl.BlockSpec((2, longitudes, outs), lambda i: (i, 0, 0))
    return pl.pallas_call(
        body,
        grid=(bands // 2,),
        in_specs=[block] * MAXS,
        out_specs=block,
        out_shape=jax.ShapeDtypeStruct(mine.shape, jnp.bfloat16),
        compiler_params=pltpu.CompilerParams(vmem_limit_bytes=VMEM),
        name="finish",
    )(mine, *others)


def gather_weights(mixing, filters, channels):
    held, outs = mixing.shape
    chans = channels // MAXS
    devices = lax.axis_size("lon")
    groups = lax.axis_size("groups")
    lon = lax.axis_index("lon")
    place = lon % MAXS
    planes = devices // MAXS
    part = held // groups
    units = part // UNIT
    per_filter = channels // UNIT
    per_quarter = chans // UNIT
    plane_units = MAXS * held // UNIT
    fits = (
        groups == 2
        and planes == MAXS
        and part % UNIT == 0
        and (plane_units % per_filter) * MAXS % per_filter == 0
        and plane_units % per_filter == per_quarter
    )
    if not fits:
        whole = lax.all_gather(mixing, "lon", axis=0, tiled=True).reshape(filters, channels, outs)
        mine = lax.dynamic_slice_in_dim(whole, place * chans, chans, 1)
        return mine.reshape(filters * chans, outs)
    group = lax.axis_index("groups")
    plane = lon // MAXS
    rows = lax.dynamic_slice_in_dim(mixing, group * part, part, 0)[None]
    step = 1
    while step < planes:
        arrived = send(rows, "lon", lambda s, step=step: s ^ (step * MAXS))
        rows = jnp.concatenate([rows, arrived], 0)
        step *= 2
    rows = rows.reshape(planes, units, UNIT, outs)
    first = place * (held // UNIT) + group * units + jnp.arange(units)
    base = (first % per_filter) // per_quarter

    def for_quarter(quarter):
        entry = ((quarter - base) % MAXS) ^ plane
        picked = rows[0]
        for z in range(1, planes):
            picked = jnp.where((entry == z)[:, None, None], rows[z], picked)
        return picked

    pieces = [for_quarter(place)]
    for r in range(1, MAXS):
        pieces.append(send(for_quarter(place ^ r), "lon", lambda s, r=r: s ^ r))
    mine = jnp.stack(pieces)
    theirs = send(mine, "groups", lambda s: s ^ 1)
    mine = mine.reshape(MAXS * units, UNIT, outs)
    theirs = theirs.reshape(MAXS * units, UNIT, outs)
    wanted = jnp.arange(filters * per_quarter)
    source = wanted // per_quarter * per_filter + place * per_quarter + wanted % per_quarter
    device, index = source // (held // UNIT), source % (held // UNIT)
    position = ((device % MAXS) ^ place) * units + index % units
    swapped = (index // units) ^ group

    def body(position_ref, swapped_ref, mine_ref, theirs_ref, out_ref):
        for u in range(filters * per_quarter):
            at, other = position_ref[u], swapped_ref[u]
            value = jnp.where(other == 1, theirs_ref[at], mine_ref[at])
            out_ref[u * UNIT : (u + 1) * UNIT, :] = value

    return pl.pallas_call(
        body,
        in_specs=[pl.BlockSpec(memory_space=pltpu.SMEM)] * 2 + [pl.BlockSpec(memory_space=pltpu.VMEM)] * 2,
        out_specs=pl.BlockSpec(memory_space=pltpu.VMEM),
        out_shape=jax.ShapeDtypeStruct((filters * chans, outs), mixing.dtype),
        compiler_params=pltpu.CompilerParams(vmem_limit_bytes=VMEM),
        name="sort_weights",
    )(position.astype(jnp.int32), swapped.astype(jnp.int32), mine, theirs)


def on_device(inputs, support, basis_table, mixing):
    bands, longitudes, channels = inputs.shape
    filters = basis_table.shape[0]
    chans = channels // MAXS
    devices = lax.axis_size("lon")
    place = lax.axis_index("lon") % MAXS

    def quarter(r):
        return lax.dynamic_slice_in_dim(inputs, (place ^ r) * chans, chans, 2)

    pieces = [quarter(0)] + [send(quarter(r), "lon", lambda s, r=r: s ^ r) for r in range(1, MAXS)]
    own = jnp.stack(pieces)
    west = send(own, "lon", lambda s: (s + MAXS) % devices)
    east = send(own, "lon", lambda s: (s - MAXS) % devices)

    weights = gather_weights(mixing, filters, channels)
    segment = round_up((2 * MAXS + 1) * longitudes, 128)
    matrices = toeplitz(packed_basis(basis_table, support, longitudes, segment), longitudes)
    mine, rest = convolve_and_mix(
        place.reshape(1).astype(jnp.int32), matrices, (west, own, east), weights, filters
    )
    others = [send(rest[r - 1], "lon", lambda s, r=r: s ^ r) for r in range(1, MAXS)]
    return finish(mine, others)


def solution(mesh):
    placed = (P("groups", "lon", None), P("groups"), P(None, "groups", None, None), P("lon", None))
    return jax.shard_map(
        on_device, mesh=mesh, in_specs=placed, out_specs=P("groups", "lon", None), check_vma=False
    )
```

time: 313 us -> 96.7 us (0.31)
  local copies, waits for them, and re-layouts: 114 us -> 2.49 us
  matrix products: 36.5 us -> 0 us
  loops' own time: 32.6 us -> 0 us
  waiting for transfers between devices: 77.7 us -> 52.9 us
  Pallas kernels: 0 us -> 22.4 us
  starting transfers between devices: 36.6 us -> 17.1 us
  between operations: 13.5 us -> 0.16 us
    reshape x16 -> x0, local copies, waits for them, and re-layouts: 77.6 us -> none  [the longest x8 40.8 us: band_basis(): tiled.reshape(filters, 3, longitudes * (span + 1))[:, :, :longitudes * span]]
    dot_general x9 -> x0, matrix products: 36.5 us -> none  [the longest x8 29.7 us: one_band(): product = jnp.dot(toeplitz, rows, preferred_element_type=jnp.float32)]
    another operation x1 -> x0, loops' own time: 32.6 us -> none  [convolve(): return lax.map(one_band, jnp.arange(bands))]
    ppermute x9 -> x14, waiting for transfers between devices: 77.7 us -> 52.9 us  [send(): return lax.ppermute(value, axis, [(s, target_of(s)) for s in range(count)])]
    pallas_call x0 -> x4, Pallas kernels: none -> 22.4 us  [the longest x1 12.8 us: convolve_and_mix(): pl.pallas_call(body, grid=(bands,), in_specs=[pl.BlockSpec(memory_space=p...]
    ppermute x9 -> x14, starting transfers between devices: 36.6 us -> 17.1 us  [send(): return lax.ppermute(value, axis, [(s, target_of(s)) for s in range(count)])]
    broadcast_in_dim x8 -> x1, local copies, waits for them, and re-layouts: 10.2 us -> 0.01 us  [gather_weights(): rows = lax.dynamic_slice_in_dim(mixing, group * part, part, 0)[None]]
    dynamic_slice x16 -> x1, local copies, waits for them, and re-layouts: 10 us -> 0.01 us  [gather_weights(): rows = lax.dynamic_slice_in_dim(mixing, group * part, part, 0)[None]]
  transfers between devices with their start and end apart: 10 -> 14, of which waited for: 9 -> 10; matrix products, arithmetic and copies ran while one was open for 46% -> 3% of each run, Pallas kernels for 0% -> 8%
where the time goes in v1:
time: 96.7 us; the launch traced here: 96.4 us
  waiting for transfers between devices  52.9 us (55%)
  Pallas kernels  22.4 us (23%)
  starting transfers between devices  17.1 us (18%)
  local copies, waits for them, and re-layouts  2.49 us (3%)
  other arithmetic  1.35 us (1%)
    ppermute x14, waiting for transfers between devices, send(): return lax.ppermute(value, axis, [(s, target_of(s)) for s in range(count)])  52.9 us
    ppermute x14, starting transfers between devices, send(): return lax.ppermute(value, axis, [(s, target_of(s)) for s in range(count)])  17.1 us
    pallas_call x1, Pallas kernels, convolve_and_mix(): pl.pallas_call(body, grid=(bands,), in_specs=[pl.BlockSpec(memory_space=p...  12.8 us
    pallas_call x1, Pallas kernels, toeplitz(): pl.pallas_call(body, grid=(bands,), in_specs=[pl.BlockSpec((1, filters, l...  7.2 us
  transfers between devices with their start and end apart: 14, of which 10 were waited for; matrix products, arithmetic and copies ran while one was open for 3% of the time, Pallas kernels for 8%

profile of v1, /device:TPU:0, one launch (start us, length us, event | category | flops | bytes accessed | tf_op | source)
XLA Modules:
  0.0 96.4 jit_solution(13587566087730806545)
XLA Ops:
  0.0 1.0 copy-done
  1.0 3.1 %collective-permute-start.5 = (bf16[1,144,512]{2,1,0:T(8,128)(2,1)S(1)}, bf16[1,144,512]{2,1,0:T(8,128)(2,1)S(1)}, u32[]{:S(2)}, u32[]{:S(2)}) collective-permute-start(bf16[1,144,512]{2,1,0:T(8,128)(2,1)S(1)} %fusion.22), channel_id=1, source_target_pairs={{0,4},{1,5},{2,6},{3,7},{4,0},{5,1},{6,2},{7,3},{8,12},{9,13},{10,... | collective-permute-start | bytes 442376 | tf_op jit(solution)/shard_map/ppermute | solution.py:15
  4.1 1.1 %dynamic-slice_bitcast_fusion = (bf16[1,8,56,128]{3,2,1,0:T(8,128)(2,1)S(1)}, bf16[8,56,128]{2,1,0:T(8,128)(2,1)S(1)}, bf16[8,56,128]{2,1,0:T(8,128)(2,1)S(1)}, bf16[8,56,128]{2,1,0:T(8,128)(2,1)S(1)}) fusion(bf16[8,56,512]{2,1,0:T(8,128)(2,1)} %param.4, s32[]{:T(128)S(6)} %select_n.262, s32[]{:T(128)S(6)} %select_n.263, s32[]{:T(128)S(6)} %select_n.265, ...), kind=kLoop, calls=%fused_computation.12 | loop fusion | bytes 917520 | tf_op jit(solution)/shard_map/stack | solution.py:250
  5.3 1.6 %collective-permute-start.2 = (bf16[8,56,128]{2,1,0:T(8,128)(2,1)S(1)}, bf16[8,56,128]{2,1,0:T(8,128)(2,1)S(1)}, u32[]{:S(2)}, u32[]{:S(2)}) collective-permute-start(bf16[8,56,128]{2,1,0:T(8,128)(2,1)S(1)} %get-tuple-element.25), channel_id=1, source_target_pairs={{0,3},{1,2},{2,1},{3,0},{4,7},{5,6},{6,5},{7,4},{8,11},{9,10},{10,... | collective-permute-start | bytes 344072 | tf_op jit(solution)/shard_map/ppermute | solution.py:15
  7.0 0.7 broadcast_multiply_fusion
  7.9 2.8 %collective-permute-start.6 = (bf16[2,144,512]{2,1,0:T(8,128)(2,1)S(1)}, bf16[2,144,512]{2,1,0:T(8,128)(2,1)S(1)}, u32[]{:S(2)}, u32[]{:S(2)}) collective-permute-start(bf16[2,144,512]{2,1,0:T(8,128)(2,1)S(1)} %pad_maximum_fusion.2), channel_id=1, source_target_pairs={{0,8},{1,9},{2,10},{3,11},{4,12},{5,13},{6,14},{7,15},{8,0},{9,1},... | collective-permute-start | bytes 884744 | tf_op jit(solution)/shard_map/ppermute | solution.py:15
  10.8 13.2 %collective-permute-done.6 = bf16[2,144,512]{2,1,0:T(8,128)(2,1)S(1)} collective-permute-done((bf16[2,144,512]{2,1,0:T(8,128)(2,1)S(1)}, bf16[2,144,512]{2,1,0:T(8,128)(2,1)S(1)}, u32[]{:S(2)}, u32[]{:S(2)}) %collective-permute-start.6) | collective-permute-done | bytes 294944 | tf_op jit(solution)/shard_map/ppermute | solution.py:15
  24.3 0.9 collective-permute-start.9
  25.2 1.2 %collective-permute-start.8 = (bf16[9,16,512]{2,1,0:T(8,128)(2,1)S(1)}, bf16[9,16,512]{2,1,0:T(8,128)(2,1)S(1)}, u32[]{:S(2)}, u32[]{:S(2)}) collective-permute-start(bf16[9,16,512]{2,1,0:T(8,128)(2,1)S(1)} %get-tuple-element.22), channel_id=1, source_target_pairs={{0,2},{1,3},{2,0},{3,1},{4,6},{5,7},{6,4},{7,5},{8,10},{9,11},{10,... | collective-permute-start | bytes 442376 | tf_op jit(solution)/shard_map/ppermute | solution.py:15
  26.5 0.9 collective-permute-start.1
  27.4 2.5 %collective-permute-done.9 = bf16[9,16,512]{2,1,0:T(8,128)(2,1)S(1)} collective-permute-done((bf16[9,16,512]{2,1,0:T(8,128)(2,1)S(1)}, bf16[9,16,512]{2,1,0:T(8,128)(2,1)S(1)}, u32[]{:S(2)}, u32[]{:S(2)}) %collective-permute-start.9) | collective-permute-done | bytes 147488 | tf_op jit(solution)/shard_map/ppermute | solution.py:15
  29.9 4.3 %collective-permute-done.8 = bf16[9,16,512]{2,1,0:T(8,128)(2,1)S(1)} collective-permute-done((bf16[9,16,512]{2,1,0:T(8,128)(2,1)S(1)}, bf16[9,16,512]{2,1,0:T(8,128)(2,1)S(1)}, u32[]{:S(2)}, u32[]{:S(2)}) %collective-permute-start.8) | collective-permute-done | bytes 147488 | tf_op jit(solution)/shard_map/ppermute | solution.py:15
  34.3 1.6 %collective-permute-start.10 = (bf16[4,9,16,512]{3,2,1,0:T(8,128)(2,1)S(1)}, bf16[4,9,16,512]{3,2,1,0:T(8,128)(2,1)S(1)}, u32[]{:S(2)}, u32[]{:S(2)}) collective-permute-start(bf16[4,9,16,512]{3,2,1,0:T(8,128)(2,1)S(1)} %pad_maximum_fusion), channel_id=1, source_target_pairs={{0,16},{16,0},{1,17},{17,1},{2,18},{18,2},{3,19},{19,3},{4,20},{20... | collective-permute-start | bytes 1769480 | tf_op jit(solution)/shard_map/ppermute | solution.py:15
  36.2 2.9 %collective-permute-start.4 = (bf16[4,8,56,128]{3,2,1,0:T(8,128)(2,1)S(1)}, bf16[4,8,56,128]{3,2,1,0:T(8,128)(2,1)S(1)}, u32[]{:S(2)}, u32[]{:S(2)}) collective-permute-start(bf16[4,8,56,128]{3,2,1,0:T(8,128)(2,1)S(1)} %pad_maximum_fusion.1.own_ref), channel_id=1, source_target_pairs={{0,12},{1,13},{2,14},{3,15},{4,0},{5,1},{6,2},{7,3},{8,4},{9,5},{1... | collective-permute-start | bytes 1376264 | tf_op jit(solution)/shard_map/ppermute | solution.py:15
  39.5 7.2 %toeplitz.1.t_ref = bf16[8,512,1536]{2,1,0:T(8,128)(2,1)} custom-call(f32[8,9,1536]{2,1,0:T(8,128)S(1)} %copy.6.packed_ref), custom_call_target="tpu_custom_call" | custom-call | tf_op jit(solution)/shard_map/toeplitz/pallas_call | solution.py:50
  46.7 1.9 %collective-permute-done.10 = bf16[4,9,16,512]{3,2,1,0:T(8,128)(2,1)S(1)} collective-permute-done((bf16[4,9,16,512]{3,2,1,0:T(8,128)(2,1)S(1)}, bf16[4,9,16,512]{3,2,1,0:T(8,128)(2,1)S(1)}, u32[]{:S(2)}, u32[]{:S(2)}) %collective-permute-start.10) | collective-permute-done | bytes 589856 | tf_op jit(solution)/shard_map/ppermute | solution.py:15
  48.6 0.7 sort_weights.1.w_ref
  49.3 0.8 collective-permute-done.4.east_ref
  50.1 9.1 %collective-permute-done.3.west_ref = bf16[4,8,56,128]{3,2,1,0:T(8,128)(2,1)S(1)} collective-permute-done((bf16[4,8,56,128]{3,2,1,0:T(8,128)(2,1)S(1)}, bf16[4,8,56,128]{3,2,1,0:T(8,128)(2,1)S(1)}, u32[]{:S(2)}, u32[]{:S(2)}) %collective-permute-start.3) | collective-permute-done | bytes 458784 | tf_op jit(solution)/shard_map/ppermute | solution.py:15
  59.2 12.8 %convolve_and_mix.1 = (f32[8,56,512]{2,1,0:T(8,128)S(1)}, bf16[3,8,56,512]{3,2,1,0:T(8,128)(2,1)S(1)}) custom-call(s32[1]{0:T(128)} %bitcast.place_ref, bf16[8,512,1536]{2,1,0:T(8,128)(2,1)} %toeplitz.1.t_ref, bf16[4,8,56,128]{3,2,1,0:T(8,128)(2,1)S(1)} %collective-permute-done.3.west_ref, bf16[4,8,56,128]{3,2,1,0:T(8,128)(2,1)S(1)} %pad_maximum_fusion.1.own_ref, ...), custom_call_target="tpu_custom_call" | custom-call | tf_op jit(solution)/shard_map/convolve_and_mix/pallas_call | solution.py:119
  72.1 1.5 %collective-permute-start.12 = (bf16[8,56,512]{2,1,0:T(8,128)(2,1)S(1)}, bf16[8,56,512]{2,1,0:T(8,128)(2,1)S(1)}, u32[]{:S(2)}, u32[]{:S(2)}) collective-permute-start(bf16[8,56,512]{2,1,0:T(8,128)(2,1)S(1)} %get-tuple-element.18), channel_id=1, source_target_pairs={{0,2},{1,3},{2,0},{3,1},{4,6},{5,7},{6,4},{7,5},{8,10},{9,11},{10,... | collective-permute-start | bytes 1376264 | tf_op jit(solution)/shard_map/ppermute | solution.py:15
  74.0 11.0 %collective-permute-done.13.c_ref = bf16[8,56,512]{2,1,0:T(8,128)(2,1)S(1)} collective-permute-done((bf16[8,56,512]{2,1,0:T(8,128)(2,1)S(1)}, bf16[8,56,512]{2,1,0:T(8,128)(2,1)S(1)}, u32[]{:S(2)}, u32[]{:S(2)}) %collective-permute-start.13) | collective-permute-done | bytes 458784 | tf_op jit(solution)/shard_map/ppermute | solution.py:15
  84.9 9.8 %collective-permute-done.12.b_ref = bf16[8,56,512]{2,1,0:T(8,128)(2,1)S(1)} collective-permute-done((bf16[8,56,512]{2,1,0:T(8,128)(2,1)S(1)}, bf16[8,56,512]{2,1,0:T(8,128)(2,1)S(1)}, u32[]{:S(2)}, u32[]{:S(2)}) %collective-permute-start.12) | collective-permute-done | bytes 458784 | tf_op jit(solution)/shard_map/ppermute | solution.py:15
  94.7 1.7 %finish.1 = bf16[8,56,512]{2,1,0:T(8,128)(2,1)} custom-call(f32[8,56,512]{2,1,0:T(8,128)S(1)} %get-tuple-element.7.mine_ref, bf16[8,56,512]{2,1,0:T(8,128)(2,1)S(1)} %collective-permute-done.11.a_ref, bf16[8,56,512]{2,1,0:T(8,128)(2,1)S(1)} %collective-permute-done.12.b_ref, bf16[8,56,512]{2,1,0:T(8,128)(2,1)S(1)} %collective-permute-done.13.c_ref), custom_call_target="tpu_custom_call" | custom-call | tf_op jit(solution)/shard_map/finish/pallas_call | solution.py:156
  (35 shorter events, 2.2 us)
Async XLA Ops:
  0.0 1.0 copy-start
  1.0 6.9 %collective-permute-start.5 = (bf16[1,144,512]{2,1,0:T(8,128)(2,1)S(1)}, bf16[1,144,512]{2,1,0:T(8,128)(2,1)S(1)}, u32[]{:S(2)}, u32[]{:S(2)}) collective-permute-start(bf16[1,144,512]{2,1,0:T(8,128)(2,1)S(1)} %fusion.22), channel_id=1, source_target_pairs={{0,4},{1,5},{2,6},{3,7},{4,0},{5,1},{6,2},{7,3},{8,12},{9,13},{10,... | collective-permute-start | bytes 442376 | tf_op jit(solution)/shard_map/ppermute | solution.py:15
  5.2 30.7 %collective-permute-start = (bf16[8,56,128]{2,1,0:T(8,128)(2,1)S(1)}, bf16[8,56,128]{2,1,0:T(8,128)(2,1)S(1)}, u32[]{:S(2)}, u32[]{:S(2)}) collective-permute-start(bf16[8,56,128]{2,1,0:T(8,128)(2,1)S(1)} %get-tuple-element.24), channel_id=1, source_target_pairs={{0,1},{1,0},{2,3},{3,2},{4,5},{5,4},{6,7},{7,6},{8,9},{9,8},{10,11... | collective-permute-start | bytes 344072 | tf_op jit(solution)/shard_map/ppermute | solution.py:15
  5.3 30.6 %collective-permute-start.2 = (bf16[8,56,128]{2,1,0:T(8,128)(2,1)S(1)}, bf16[8,56,128]{2,1,0:T(8,128)(2,1)S(1)}, u32[]{:S(2)}, u32[]{:S(2)}) collective-permute-start(bf16[8,56,128]{2,1,0:T(8,128)(2,1)S(1)} %get-tuple-element.25), channel_id=1, source_target_pairs={{0,3},{1,2},{2,1},{3,0},{4,7},{5,6},{6,5},{7,4},{8,11},{9,10},{10,... | collective-permute-start | bytes 344072 | tf_op jit(solution)/shard_map/ppermute | solution.py:15
  7.9 16.1 %collective-permute-start.6 = (bf16[2,144,512]{2,1,0:T(8,128)(2,1)S(1)}, bf16[2,144,512]{2,1,0:T(8,128)(2,1)S(1)}, u32[]{:S(2)}, u32[]{:S(2)}) collective-permute-start(bf16[2,144,512]{2,1,0:T(8,128)(2,1)S(1)} %pad_maximum_fusion.2), channel_id=1, source_target_pairs={{0,8},{1,9},{2,10},{3,11},{4,12},{5,13},{6,14},{7,15},{8,0},{9,1},... | collective-permute-start | bytes 884744 | tf_op jit(solution)/shard_map/ppermute | solution.py:15
  24.2 2.3 %collective-permute-start.7 = (bf16[9,16,512]{2,1,0:T(8,128)(2,1)S(1)}, bf16[9,16,512]{2,1,0:T(8,128)(2,1)S(1)}, u32[]{:S(2)}, u32[]{:S(2)}) collective-permute-start(bf16[9,16,512]{2,1,0:T(8,128)(2,1)S(1)} %get-tuple-element.20), channel_id=1, source_target_pairs={{0,1},{1,0},{2,3},{3,2},{4,5},{5,4},{6,7},{7,6},{8,9},{9,8},{10,11... | collective-permute-start | bytes 442376 | tf_op jit(solution)/shard_map/ppermute | solution.py:15
  24.3 5.6 %collective-permute-start.9 = (bf16[9,16,512]{2,1,0:T(8,128)(2,1)S(1)}, bf16[9,16,512]{2,1,0:T(8,128)(2,1)S(1)}, u32[]{:S(2)}, u32[]{:S(2)}) collective-permute-start(bf16[9,16,512]{2,1,0:T(8,128)(2,1)S(1)} %get-tuple-element.21), channel_id=1, source_target_pairs={{0,3},{1,2},{2,1},{3,0},{4,7},{5,6},{6,5},{7,4},{8,11},{9,10},{10,... | collective-permute-start | bytes 442376 | tf_op jit(solution)/shard_map/ppermute | solution.py:15
  25.2 9.0 %collective-permute-start.8 = (bf16[9,16,512]{2,1,0:T(8,128)(2,1)S(1)}, bf16[9,16,512]{2,1,0:T(8,128)(2,1)S(1)}, u32[]{:S(2)}, u32[]{:S(2)}) collective-permute-start(bf16[9,16,512]{2,1,0:T(8,128)(2,1)S(1)} %get-tuple-element.22), channel_id=1, source_target_pairs={{0,2},{1,3},{2,0},{3,1},{4,6},{5,7},{6,4},{7,5},{8,10},{9,11},{10,... | collective-permute-start | bytes 442376 | tf_op jit(solution)/shard_map/ppermute | solution.py:15
  26.4 12.7 %copy-start.1 = (bf16[9,8,3,449]{3,1,2,0:T(8,128)(2,1)S(1)}, bf16[9,8,3,449]{3,1,2,0:T(8,128)(2,1)}, u32[]{:S(2)}) copy-start(bf16[9,8,3,449]{3,1,2,0:T(8,128)(2,1)} %param.6) | copy-start | bytes 581908
  26.5 9.6 %collective-permute-start.1 = (bf16[8,56,128]{2,1,0:T(8,128)(2,1)S(1)}, bf16[8,56,128]{2,1,0:T(8,128)(2,1)S(1)}, u32[]{:S(2)}, u32[]{:S(2)}) collective-permute-start(bf16[8,56,128]{2,1,0:T(8,128)(2,1)S(1)} %get-tuple-element.26), channel_id=1, source_target_pairs={{0,2},{1,3},{2,0},{3,1},{4,6},{5,7},{6,4},{7,5},{8,10},{9,11},{10,... | collective-permute-start | bytes 344072 | tf_op jit(solution)/shard_map/ppermute | solution.py:15
  34.3 14.3 %collective-permute-start.10 = (bf16[4,9,16,512]{3,2,1,0:T(8,128)(2,1)S(1)}, bf16[4,9,16,512]{3,2,1,0:T(8,128)(2,1)S(1)}, u32[]{:S(2)}, u32[]{:S(2)}) collective-permute-start(bf16[4,9,16,512]{3,2,1,0:T(8,128)(2,1)S(1)} %pad_maximum_fusion), channel_id=1, source_target_pairs={{0,16},{16,0},{1,17},{17,1},{2,18},{18,2},{3,19},{19,3},{4,20},{20... | collective-permute-start | bytes 1769480 | tf_op jit(solution)/shard_map/ppermute | solution.py:15
  36.2 13.9 %collective-permute-start.4 = (bf16[4,8,56,128]{3,2,1,0:T(8,128)(2,1)S(1)}, bf16[4,8,56,128]{3,2,1,0:T(8,128)(2,1)S(1)}, u32[]{:S(2)}, u32[]{:S(2)}) collective-permute-start(bf16[4,8,56,128]{3,2,1,0:T(8,128)(2,1)S(1)} %pad_maximum_fusion.1.own_ref), channel_id=1, source_target_pairs={{0,12},{1,13},{2,14},{3,15},{4,0},{5,1},{6,2},{7,3},{8,4},{9,5},{1... | collective-permute-start | bytes 1376264 | tf_op jit(solution)/shard_map/ppermute | solution.py:15
  39.1 20.1 %collective-permute-start.3 = (bf16[4,8,56,128]{3,2,1,0:T(8,128)(2,1)S(1)}, bf16[4,8,56,128]{3,2,1,0:T(8,128)(2,1)S(1)}, u32[]{:S(2)}, u32[]{:S(2)}) collective-permute-start(bf16[4,8,56,128]{3,2,1,0:T(8,128)(2,1)S(1)} %pad_maximum_fusion.1.own_ref), channel_id=1, source_target_pairs={{0,4},{1,5},{2,6},{3,7},{4,8},{5,9},{6,10},{7,11},{8,12},{9,13},{1... | collective-permute-start | bytes 1376264 | tf_op jit(solution)/shard_map/ppermute | solution.py:15
  72.0 12.9 %collective-permute-start.13 = (bf16[8,56,512]{2,1,0:T(8,128)(2,1)S(1)}, bf16[8,56,512]{2,1,0:T(8,128)(2,1)S(1)}, u32[]{:S(2)}, u32[]{:S(2)}) collective-permute-start(bf16[8,56,512]{2,1,0:T(8,128)(2,1)S(1)} %get-tuple-element.17), channel_id=1, source_target_pairs={{0,3},{1,2},{2,1},{3,0},{4,7},{5,6},{6,5},{7,4},{8,11},{9,10},{10,... | collective-permute-start | bytes 1376264 | tf_op jit(solution)/shard_map/ppermute | solution.py:15
  72.1 22.6 %collective-permute-start.12 = (bf16[8,56,512]{2,1,0:T(8,128)(2,1)S(1)}, bf16[8,56,512]{2,1,0:T(8,128)(2,1)S(1)}, u32[]{:S(2)}, u32[]{:S(2)}) collective-permute-start(bf16[8,56,512]{2,1,0:T(8,128)(2,1)S(1)} %get-tuple-element.18), channel_id=1, source_target_pairs={{0,2},{1,3},{2,0},{3,1},{4,6},{5,7},{6,4},{7,5},{8,10},{9,11},{10,... | collective-permute-start | bytes 1376264 | tf_op jit(solution)/shard_map/ppermute | solution.py:15
  73.6 21.1 %collective-permute-start.11 = (bf16[8,56,512]{2,1,0:T(8,128)(2,1)S(1)}, bf16[8,56,512]{2,1,0:T(8,128)(2,1)S(1)}, u32[]{:S(2)}, u32[]{:S(2)}) collective-permute-start(bf16[8,56,512]{2,1,0:T(8,128)(2,1)S(1)} %get-tuple-element.19), channel_id=1, source_target_pairs={{0,1},{1,0},{2,3},{3,2},{4,5},{5,4},{6,7},{7,6},{8,9},{9,8},{10,11... | collective-permute-start | bytes 1376264 | tf_op jit(solution)/shard_map/ppermute | solution.py:15

commit v2 on v0

v2 whole, which is shorter than its diff:
```python
import jax
import jax.numpy as jnp
from jax import lax
from jax.experimental import pallas as pl
from jax.experimental.pallas import tpu as pltpu
from jax.sharding import PartitionSpec as P

MAXS = 4
UNIT = 16
VMEM = 28 << 20


def send(value, axis, target_of):
    count = lax.axis_size(axis)
    return lax.ppermute(value, axis, [(s, target_of(s)) for s in range(count)])


def round_up(value, step):
    return -(-value // step) * step


def lay_out(pieces, first, last, ties):
    shape = (len(pieces), last - first, *pieces[0].shape[1:])

    def body(*refs):
        for n in range(len(pieces)):
            refs[-1][n] = refs[n][first:last]

    return pl.pallas_call(
        body,
        in_specs=[pl.BlockSpec(memory_space=pltpu.VMEM)] * len(pieces)
        + [pl.BlockSpec(memory_space=pl.ANY)] * len(ties),
        out_specs=pl.BlockSpec(memory_space=pltpu.VMEM),
        out_shape=jax.ShapeDtypeStruct(shape, pieces[0].dtype),
        compiler_params=pltpu.CompilerParams(vmem_limit_bytes=VMEM),
        name="lay_out",
    )(*pieces, *ties)


def packed_basis(basis_table, support, longitudes, segment):
    filters, bands, three, offsets = basis_table.shape
    distance = jnp.abs(jnp.arange(offsets) - MAXS * longitudes)
    within = distance[None, :] <= (support * longitudes)[:, None]
    rows = jnp.where(within[None, :, None, :], basis_table, jnp.zeros_like(basis_table))
    rows = jnp.pad(rows, ((0, 0), (0, 0), (0, 0), (0, segment - offsets)))
    rows = rows.transpose(1, 0, 2, 3).reshape(bands, filters, three * segment)
    return rows.astype(jnp.float32)


def fill_toeplitz(row_of, out_ref, filters, longitudes):
    rows, lanes = out_ref.shape

    def block(k):
        row = jnp.broadcast_to(row_of(k), (longitudes, lanes))
        return pltpu.roll(row, 0, 1, stride=1, stride_axis=0)

    for k in range(0, filters, 2):
        start = k * longitudes
        if k + 1 < filters:
            pair = jnp.concatenate([block(k), block(k + 1)], 0)
        else:
            tail = jnp.zeros((rows - start - longitudes, lanes), jnp.float32)
            pair = jnp.concatenate([block(k), tail], 0)
        out_ref[start : start + pair.shape[0], :] = pair.astype(jnp.bfloat16)


def convolve(place, packed, planes, first, bands):
    longitudes, chans = planes[0][0][1].shape[2:]
    count, filters, lanes = packed.shape
    rows = round_up(filters * longitudes, UNIT)
    segment = lanes // 3
    span = 3 * MAXS * longitudes
    step = round_up(longitudes, UNIT)
    low, high = max(first - 1, 0), min(first + count + 1, bands)
    arrays, found = [], [{}, {}, {}]
    for t in range(3):
        for start, array in planes[t]:
            for b in range(array.shape[1]):
                found[t][start + b] = (len(arrays), b)
            arrays.append(array)

    def body(place_ref, packed_ref, *refs):
        ins, (mixin, line, windows, toeplitz) = refs[: len(arrays)], refs[len(arrays) :]
        here = place_ref[0]
        line[:, span:, :] = jnp.zeros((2, line.shape[1] - span, chans), jnp.float32)
        for b in range(low, high):
            side = b % 2
            for t in range(3):
                which, at = found[t][b]
                for p in range(MAXS):
                    start = (t * MAXS + p) * longitudes
                    line[side, start : start + longitudes, :] = ins[which][p ^ here, at].astype(jnp.float32)
            start = (b - low) * segment
            for r in range(MAXS):
                begin = pl.multiple_of((r ^ here) * longitudes, 8)
                part = line[side, pl.ds(begin, segment), :].astype(jnp.bfloat16)
                windows[start : start + segment, r * chans : (r + 1) * chans] = part
        for c in range(count):
            i = first + c
            from_band, to_band = max(i - 1, 0), min(i + 2, bands)
            matrix = toeplitz.at[c % 2]
            fill_toeplitz(lambda k, c=c: packed_ref[c, k : k + 1, :], matrix, filters, longitudes)
            matrix = matrix[:, (from_band - i + 1) * segment : (to_band - i + 1) * segment]
            window = windows[(from_band - low) * segment : (to_band - low) * segment, :]
            conv = jnp.dot(matrix, window, preferred_element_type=jnp.float32)
            for r in range(MAXS):
                parts = [
                    conv[k * longitudes : (k + 1) * longitudes, r * chans : (r + 1) * chans]
                    for k in range(filters)
                ]
                part = jnp.concatenate(parts, 1)
                fill = jnp.zeros((step - longitudes, part.shape[1]), jnp.float32)
                start = (c * MAXS + r) * step
                mixin[start : start + step, :] = jnp.concatenate([part, fill], 0).astype(jnp.bfloat16)

    vmem = pl.BlockSpec(memory_space=pltpu.VMEM)
    return pl.pallas_call(
        body,
        in_specs=[pl.BlockSpec(memory_space=pltpu.SMEM)] + [vmem] * (1 + len(arrays)),
        out_specs=vmem,
        out_shape=jax.ShapeDtypeStruct((count * MAXS * step, filters * chans), jnp.bfloat16),
        scratch_shapes=[
            pltpu.VMEM((2, round_up((MAXS - 1) * longitudes + max(segment, span), 8), chans), jnp.float32),
            pltpu.VMEM(((high - low) * segment, MAXS * chans), jnp.bfloat16),
            pltpu.VMEM((2, rows, lanes), jnp.bfloat16),
        ],
        compiler_params=pltpu.CompilerParams(vmem_limit_bytes=VMEM),
        cost_estimate=pl.CostEstimate(
            flops=2 * count * rows * lanes * MAXS * chans, bytes_accessed=1, transcendentals=0
        ),
        name="convolve",
    )(place, packed, *arrays)


def mix(convolved, weights, longitudes):
    step = round_up(longitudes, UNIT)
    counts = [array.shape[0] // (MAXS * step) for array in convolved]
    outs = weights.shape[1]

    def body(w_ref, *refs):
        ins, (kept_ref, sent_ref) = refs[:-2], refs[-2:]
        first = 0
        for ref, count in zip(ins, counts):
            mixed = jnp.dot(ref[...], w_ref[...], preferred_element_type=jnp.float32)
            for c in range(count):
                for r in range(MAXS):
                    start = (c * MAXS + r) * step
                    value = mixed[start : start + longitudes]
                    if r % 2 == 0:
                        kept_ref[r // 2, first + c] = value
                    else:
                        sent_ref[r // 2, first + c] = value.astype(jnp.bfloat16)
            first += count

    vmem = pl.BlockSpec(memory_space=pltpu.VMEM)
    shape = (2, sum(counts), longitudes, outs)
    return pl.pallas_call(
        body,
        in_specs=[vmem] * (1 + len(convolved)),
        out_specs=[vmem, vmem],
        out_shape=[jax.ShapeDtypeStruct(shape, jnp.float32), jax.ShapeDtypeStruct(shape, jnp.bfloat16)],
        compiler_params=pltpu.CompilerParams(vmem_limit_bytes=VMEM),
        name="mix",
    )(weights, *convolved)


def finish(turned, sums, bands):
    longitudes, width = sums[0][1].shape[2:]

    def body(turned_ref, *refs):
        out_ref = refs[-1]
        reached = [0, 0]
        for n, (half, kept, _, _) in enumerate(sums):
            kept_ref, core_ref, across_ref = refs[3 * n : 3 * n + 3]
            column = pl.multiple_of((turned_ref[0] ^ half) * width, width)
            for band in range(kept.shape[1]):
                total = kept_ref[0, band] + core_ref[0, band].astype(jnp.float32)
                total += across_ref[band].astype(jnp.float32)
                out_ref[reached[half], :, pl.ds(column, width)] = jax.nn.gelu(total).astype(jnp.bfloat16)
                reached[half] += 1

    vmem = pl.BlockSpec(memory_space=pltpu.VMEM)
    return pl.pallas_call(
        body,
        in_specs=[pl.BlockSpec(memory_space=pltpu.SMEM)] + [vmem] * (3 * len(sums)),
        out_specs=vmem,
        out_shape=jax.ShapeDtypeStruct((bands, longitudes, 2 * width), jnp.bfloat16),
        compiler_params=pltpu.CompilerParams(vmem_limit_bytes=VMEM),
        name="finish",
    )(turned, *(array for entry in sums for array in entry[1:]))


def gather_weights(mixing, filters, channels):
    held, outs = mixing.shape
    chans = channels // MAXS
    width = outs // 2
    devices = lax.axis_size("lon")
    groups = lax.axis_size("groups")
    lon = lax.axis_index("lon")
    place = lon % MAXS
    planes = devices // MAXS
    units = held // UNIT
    per_filter = channels // UNIT
    per_quarter = chans // UNIT
    fits = (
        groups == 2
        and planes == MAXS
        and held % UNIT == 0
        and (MAXS * units) % per_filter == per_quarter
    )
    if not fits:
        whole = lax.all_gather(mixing, "lon", axis=0, tiled=True).reshape(filters, channels, outs)
        mine = lax.dynamic_slice_in_dim(whole, place * chans, chans, 1).reshape(filters * chans, outs)
        return (), lambda *_: (mine[:, :width], mine[:, width:], jnp.int32(0))
    group = lax.axis_index("groups")
    plane = lon // MAXS
    rows = lax.dynamic_slice_in_dim(mixing, group * width, width, 1)
    far = send(rows, "lon", lambda s: s ^ (2 * MAXS))
    near = send(rows, "lon", lambda s: s ^ MAXS)
    rows = jnp.stack([rows, near, far, send(far, "lon", lambda s: s ^ MAXS)])
    rows = rows.reshape(planes, units, UNIT, width)
    base = (place * units + jnp.arange(units)) % per_filter // per_quarter

    def for_quarter(quarter):
        entry = ((quarter - base) % MAXS) ^ plane
        picked = rows[0]
        for z in range(1, planes):
            picked = jnp.where((entry == z)[:, None, None], rows[z], picked)
        return picked

    pieces = {0: for_quarter(place)}
    for r in (3, 2, 1):
        pieces[r] = send(for_quarter(place ^ r), "lon", lambda s, r=r: s ^ r)
    def sort(*ties):
        mine = jnp.concatenate([pieces[r] for r in range(MAXS)])
        count = filters * per_quarter
        wanted = jnp.arange(count)
        source = wanted // per_quarter * per_filter + place * per_quarter + wanted % per_quarter
        position = (source // units % MAXS ^ place) * units + source % units

        def body(position_ref, mine_ref, *refs):
            for u in range(count):
                refs[-1][u * UNIT : (u + 1) * UNIT, :] = mine_ref[position_ref[u]]

        ours = pl.pallas_call(
            body,
            in_specs=[pl.BlockSpec(memory_space=pltpu.SMEM), pl.BlockSpec(memory_space=pltpu.VMEM)]
            + [pl.BlockSpec(memory_space=pl.ANY)] * len(ties),
            out_specs=pl.BlockSpec(memory_space=pltpu.VMEM),
            out_shape=jax.ShapeDtypeStruct((filters * chans, width), mixing.dtype),
            compiler_params=pltpu.CompilerParams(vmem_limit_bytes=VMEM),
            name="sort_weights",
        )(position.astype(jnp.int32), mine, *ties)
        return ours, send(ours, "groups", lambda s: s ^ 1), group

    return (pieces[1], pieces[2], pieces[3]), sort


def on_device(inputs, support, basis_table, mixing):
    bands, longitudes, channels = inputs.shape
    filters = basis_table.shape[0]
    chans = channels // MAXS
    devices = lax.axis_size("lon")
    place = lax.axis_index("lon") % MAXS
    segment = round_up((2 * MAXS + 1) * longitudes, 128)
    packed = packed_basis(basis_table, support, longitudes, segment)
    cuts = ((0, 4), (4, 8))

    def quarter(r):
        return lax.dynamic_slice_in_dim(inputs, (place ^ r) * chans, chans, 2)

    pieces = {0: quarter(0)}
    for r in (3, 2, 1):
        pieces[r] = send(quarter(r), "lon", lambda s, r=r: s ^ r)
    arrived, sort = gather_weights(mixing, filters, channels)
    planes = [[], [], []]
    reached = 0
    for index, (first, last) in enumerate(cuts):
        until = min(last + 1, bands)
        ties = list(arrived) if index else []
        own = lay_out([pieces[r] for r in range(MAXS)], reached, until, ties)
        west = send(own, "lon", lambda s: (s + MAXS) % devices)
        east = send(own, "lon", lambda s: (s - MAXS) % devices)
        for held, array in zip(planes, (west, own, east)):
            held.append((reached, array))
        reached = until
    ours, theirs, turned = sort()

    here = place.reshape(1).astype(jnp.int32)
    convolved = []
    for index, (first, last) in enumerate(cuts):
        low, high = max(first - 1, 0), min(last + 1, bands)
        needed = [[(s, a) for s, a in held if s < high and s + a.shape[1] > low] for held in planes]
        convolved.append(convolve(here, packed[first:last], needed, first, bands))

    def summed(half, arrays, weights):
        kept, sent = mix(arrays, weights, longitudes)
        core = send(sent, "lon", lambda s: s ^ 1)
        across = (kept[1] + core[1].astype(jnp.float32)).astype(jnp.bfloat16)
        return half, kept, core, send(across, "lon", lambda s: s ^ 2)

    sums = [summed(0, [array], ours) for array in convolved] + [summed(1, convolved, theirs)]
    return finish(turned.reshape(1).astype(jnp.int32), sums, bands)


def solution(mesh):
    placed = (P("groups", "lon", None), P("groups"), P(None, "groups", None, None), P("lon", None))
    return jax.shard_map(
        on_device, mesh=mesh, in_specs=placed, out_specs=P("groups", "lon", None), check_vma=False
    )
```

time: 313 us -> 70.9 us (0.23)
  local copies, waits for them, and re-layouts: 114 us -> 2.32 us
  waiting for transfers between devices: 77.7 us -> 24.4 us
  matrix products: 36.5 us -> 0 us
  loops' own time: 32.6 us -> 0 us
  between operations: 13.5 us -> 0.23 us
  Pallas kernels: 0 us -> 12.3 us
  starting transfers between devices: 36.6 us -> 29.1 us
    reshape x16 -> x0, local copies, waits for them, and re-layouts: 77.6 us -> none  [the longest x8 40.8 us: band_basis(): tiled.reshape(filters, 3, longitudes * (span + 1))[:, :, :longitudes * span]]
    ppermute x9 -> x20, waiting for transfers between devices: 77.7 us -> 24.4 us  [send(): return lax.ppermute(value, axis, [(s, target_of(s)) for s in range(count)])]
    dot_general x9 -> x0, matrix products: 36.5 us -> none  [the longest x8 29.7 us: one_band(): product = jnp.dot(toeplitz, rows, preferred_element_type=jnp.float32)]
    another operation x1 -> x0, loops' own time: 32.6 us -> none  [convolve(): return lax.map(one_band, jnp.arange(bands))]
    pallas_call x0 -> x9, Pallas kernels: none -> 12.3 us  [the longest x2 7.24 us: convolve(): pl.pallas_call(body, in_specs=[pl.BlockSpec(memory_space=pltpu.SMEM)] + [...]
    broadcast_in_dim x8 -> x0, local copies, waits for them, and re-layouts: 10.2 us -> none  [band_basis(): jnp.broadcast_to(widened[:, :, None, :], (filters, 3, longitudes, span + 1))]
    dynamic_slice x16 -> x2, local copies, waits for them, and re-layouts: 10 us -> 1.12 us  [the longest x1 1.11 us: quarter(): return lax.dynamic_slice_in_dim(inputs, (place ^ r) * chans, chans, 2)]
    ppermute x9 -> x20, starting transfers between devices: 36.6 us -> 29.1 us  [send(): return lax.ppermute(value, axis, [(s, target_of(s)) for s in range(count)])]
  transfers between devices with their start and end apart: 10 -> 20, of which waited for: 9 -> 9; matrix products, arithmetic and copies ran while one was open for 46% -> 5% of each run, Pallas kernels for 0% -> 16%
where the time goes in v2:
time: 70.9 us; the launch traced here: 70.7 us
  starting transfers between devices  29.1 us (41%)
  waiting for transfers between devices  24.4 us (34%)
  Pallas kernels  12.3 us (17%)
  local copies, waits for them, and re-layouts  2.32 us (3%)
  other arithmetic  2.31 us (3%)
    ppermute x20, starting transfers between devices, send(): return lax.ppermute(value, axis, [(s, target_of(s)) for s in range(count)])  29.1 us
    ppermute x20, waiting for transfers between devices, send(): return lax.ppermute(value, axis, [(s, target_of(s)) for s in range(count)])  24.4 us
    pallas_call x2, Pallas kernels, convolve(): pl.pallas_call(body, in_specs=[pl.BlockSpec(memory_space=pltpu.SMEM)] + [...  7.24 us
    pallas_call x3, Pallas kernels, mix(): pl.pallas_call(body, in_specs=[vmem] * (1 + len(convolved)), out_specs=[v...  3.2 us
  transfers between devices with their start and end apart: 20, of which 9 were waited for; matrix products, arithmetic and copies ran while one was open for 5% of the time, Pallas kernels for 16%

profile of v2, /device:TPU:0, one launch (start us, length us, event | category | flops | bytes accessed | tf_op | source)
XLA Modules:
  0.0 70.7 jit_solution(6133921335803448439)
XLA Ops:
  0.0 1.0 %copy-done = bf16[288,512]{1,0:T(8,128)(2,1)S(1)} copy-done((bf16[288,512]{1,0:T(8,128)(2,1)S(1)}, bf16[288,512]{1,0:T(8,128)(2,1)}, u32[]{:S(2)}) %copy-start) | copy-done | bytes 294936
  1.0 4.1 %collective-permute-start = (bf16[288,256]{1,0:T(8,128)(2,1)S(1)}, bf16[288,256]{1,0:T(8,128)(2,1)S(1)}, u32[]{:S(2)}, u32[]{:S(2)}) collective-permute-start(bf16[288,256]{1,0:T(8,128)(2,1)S(1)} %constant_dynamic-slice_fusion.4), channel_id=1, source_target_pairs={{0,8},{1,9},{2,10},{3,11},{4,12},{5,13},{6,14},{7,15},{8,0},{9,1},... | collective-permute-start | bytes 442376 | tf_op jit(solution)/shard_map/ppermute | solution.py:15
  5.1 1.6 %collective-permute-start.2 = (bf16[288,256]{1,0:T(8,128)(2,1)S(1)}, bf16[288,256]{1,0:T(8,128)(2,1)S(1)}, u32[]{:S(2)}, u32[]{:S(2)}) collective-permute-start(bf16[288,256]{1,0:T(8,128)(2,1)S(1)} %constant_dynamic-slice_fusion.4), channel_id=1, source_target_pairs={{0,4},{1,5},{2,6},{3,7},{4,0},{5,1},{6,2},{7,3},{8,12},{9,13},{10,... | collective-permute-start | bytes 442376 | tf_op jit(solution)/shard_map/ppermute | solution.py:15
  6.7 1.1 %constant_dynamic-slice_fusion = (bf16[8,56,128]{2,1,0:T(8,128)(2,1)S(1)}, bf16[8,56,128]{2,1,0:T(8,128)(2,1)S(1)}, bf16[8,56,128]{2,1,0:T(8,128)(2,1)S(1)}, bf16[8,56,128]{2,1,0:T(8,128)(2,1)S(1)}) fusion(bf16[8,56,512]{2,1,0:T(8,128)(2,1)} %param.4, s32[]{:T(128)S(6)} %select_n.262, s32[]{:T(128)S(6)} %select_n.260, s32[]{:T(128)S(6)} %select_n.259, ...), kind=kLoop, calls=%fused_computation.38 | loop fusion | bytes 917520 | tf_op jit(solution)/shard_map/dynamic_slice | solution.py:270
  7.9 1.6 %collective-permute-start.7 = (bf16[8,56,128]{2,1,0:T(8,128)(2,1)S(1)}, bf16[8,56,128]{2,1,0:T(8,128)(2,1)S(1)}, u32[]{:S(2)}, u32[]{:S(2)}) collective-permute-start(bf16[8,56,128]{2,1,0:T(8,128)(2,1)S(1)} %get-tuple-element.32), channel_id=1, source_target_pairs={{0,2},{1,3},{2,0},{3,1},{4,6},{5,7},{6,4},{7,5},{8,10},{9,11},{10,... | collective-permute-start | bytes 344072 | tf_op jit(solution)/shard_map/ppermute | solution.py:15
  10.6 1.0 %broadcast_select_fusion = bf16[9,8,3,449]{3,1,2,0:T(8,128)(2,1)S(1)} fusion(bf16[9,8,3,449]{3,1,2,0:T(8,128)(2,1)} %param.6, pred[8,449]{1,0:T(8,128)(4,1)S(1)} %broadcast_compare_fusion), kind=kLoop, calls=%fused_computation.6 | loop fusion | flops 96984 | bytes 391528 | tf_op jit(solution)/shard_map/jit(_where)/select_n | solution.py:44
  12.9 1.0 %collective-permute-done.7.refs_2_ = bf16[8,56,128]{2,1,0:T(8,128)(2,1)S(1)} collective-permute-done((bf16[8,56,128]{2,1,0:T(8,128)(2,1)S(1)}, bf16[8,56,128]{2,1,0:T(8,128)(2,1)S(1)}, u32[]{:S(2)}, u32[]{:S(2)}) %collective-permute-start.7) | collective-permute-done | bytes 114720 | tf_op jit(solution)/shard_map/ppermute | solution.py:15
  13.9 1.6 %collective-permute-done.8.refs_3_ = bf16[8,56,128]{2,1,0:T(8,128)(2,1)S(1)} collective-permute-done((bf16[8,56,128]{2,1,0:T(8,128)(2,1)S(1)}, bf16[8,56,128]{2,1,0:T(8,128)(2,1)S(1)}, u32[]{:S(2)}, u32[]{:S(2)}) %collective-permute-start.8) | collective-permute-done | bytes 114720 | tf_op jit(solution)/shard_map/ppermute | solution.py:15
  15.8 1.7 %collective-permute-start.9 = (bf16[4,5,56,128]{3,2,1,0:T(8,128)(2,1)S(1)}, bf16[4,5,56,128]{3,2,1,0:T(8,128)(2,1)S(1)}, u32[]{:S(2)}, u32[]{:S(2)}) collective-permute-start(bf16[4,5,56,128]{3,2,1,0:T(8,128)(2,1)S(1)} %lay_out.2.refs_1_.refs_2_), channel_id=1, source_target_pairs={{0,4},{1,5},{2,6},{3,7},{4,8},{5,9},{6,10},{7,11},{8,12},{9,13},{1... | collective-permute-start | bytes 860168 | tf_op jit(solution)/shard_map/ppermute | solution.py:15
  18.1 1.6 %collective-permute-start.4 = (bf16[18,16,256]{2,1,0:T(8,128)(2,1)S(1)}, bf16[18,16,256]{2,1,0:T(8,128)(2,1)S(1)}, u32[]{:S(2)}, u32[]{:S(2)}) collective-permute-start(bf16[18,16,256]{2,1,0:T(8,128)(2,1)S(1)} %get-tuple-element.27), channel_id=1, source_target_pairs={{0,2},{1,3},{2,0},{3,1},{4,6},{5,7},{6,4},{7,5},{8,10},{9,11},{10,... | collective-permute-start | bytes 442376 | tf_op jit(solution)/shard_map/ppermute | solution.py:15
  20.2 4.6 %collective-permute-done.4.refs_5_ = bf16[18,16,256]{2,1,0:T(8,128)(2,1)S(1)} collective-permute-done((bf16[18,16,256]{2,1,0:T(8,128)(2,1)S(1)}, bf16[18,16,256]{2,1,0:T(8,128)(2,1)S(1)}, u32[]{:S(2)}, u32[]{:S(2)}) %collective-permute-start.4) | collective-permute-done | bytes 147488 | tf_op jit(solution)/shard_map/ppermute | solution.py:15
  24.8 2.3 %collective-permute-done.5.refs_6_ = bf16[18,16,256]{2,1,0:T(8,128)(2,1)S(1)} collective-permute-done((bf16[18,16,256]{2,1,0:T(8,128)(2,1)S(1)}, bf16[18,16,256]{2,1,0:T(8,128)(2,1)S(1)}, u32[]{:S(2)}, u32[]{:S(2)}) %collective-permute-start.5) | collective-permute-done | bytes 147488 | tf_op jit(solution)/shard_map/ppermute | solution.py:15
  27.1 0.9 %collective-permute-start.13 = (bf16[4,3,56,128]{3,2,1,0:T(8,128)(2,1)S(1)}, bf16[4,3,56,128]{3,2,1,0:T(8,128)(2,1)S(1)}, u32[]{:S(2)}, u32[]{:S(2)}) collective-permute-start(bf16[4,3,56,128]{3,2,1,0:T(8,128)(2,1)S(1)} %lay_out.3.refs_3_), channel_id=1, source_target_pairs={{0,4},{1,5},{2,6},{3,7},{4,8},{5,9},{6,10},{7,11},{8,12},{9,13},{1... | collective-permute-start | bytes 516104 | tf_op jit(solution)/shard_map/ppermute | solution.py:15
  28.0 10.0 %collective-permute-start.14 = (bf16[4,3,56,128]{3,2,1,0:T(8,128)(2,1)S(1)}, bf16[4,3,56,128]{3,2,1,0:T(8,128)(2,1)S(1)}, u32[]{:S(2)}, u32[]{:S(2)}) collective-permute-start(bf16[4,3,56,128]{3,2,1,0:T(8,128)(2,1)S(1)} %lay_out.3.refs_3_), channel_id=1, source_target_pairs={{0,12},{1,13},{2,14},{3,15},{4,0},{5,1},{6,2},{7,3},{8,4},{9,5},{1... | collective-permute-start | bytes 516104 | tf_op jit(solution)/shard_map/ppermute | solution.py:15
  38.7 1.6 %collective-permute-start.17 = (bf16[1152,256]{1,0:T(8,128)(2,1)S(1)}, bf16[1152,256]{1,0:T(8,128)(2,1)S(1)}, u32[]{:S(2)}, u32[]{:S(2)}) collective-permute-start(bf16[1152,256]{1,0:T(8,128)(2,1)S(1)} %sort_weights.1.w_ref), channel_id=1, source_target_pairs={{0,16},{16,0},{1,17},{17,1},{2,18},{18,2},{3,19},{19,3},{4,20},{20... | collective-permute-start | bytes 1769480 | tf_op jit(solution)/shard_map/ppermute | solution.py:15
  40.2 3.6 %convolve.2.refs_0_ = bf16[1024,1152]{1,0:T(8,128)(2,1)S(1)} custom-call(s32[1]{0:T(128)} %bitcast.5.place_ref, f32[4,9,1536]{2,1,0:T(8,128)S(1)} %copy.7.packed_ref, bf16[4,5,56,128]{3,2,1,0:T(8,128)(2,1)S(1)} %collective-permute-done.9.refs_0_, bf16[4,5,56,128]{3,2,1,0:T(8,128)(2,1)S(1)} %lay_out.2.refs_1_.refs_2_, ...), custom_call_target="tpu_custom_call" | custom-call | flops 3221225472 | bytes 1 | tf_op jit(solution)/shard_map/convolve/pallas_call | solution.py:117
  44.8 3.6 %convolve.3.refs_0_.refs_1_ = bf16[1024,1152]{1,0:T(8,128)(2,1)S(1)} custom-call(s32[1]{0:T(128)} %bitcast.5.place_ref, f32[4,9,1536]{2,1,0:T(8,128)S(1)} %copy.8.packed_ref, bf16[4,5,56,128]{3,2,1,0:T(8,128)(2,1)S(1)} %collective-permute-done.9.refs_0_, bf16[4,3,56,128]{3,2,1,0:T(8,128)(2,1)S(1)} %collective-permute-done.13.refs_1_, ...), custom_call_target="tpu_custom_call" | custom-call | flops 3221225472 | bytes 1 | tf_op jit(solution)/shard_map/convolve/pallas_call | solution.py:117
  48.4 5.5 %collective-permute-done.17.w_ref = bf16[1152,256]{1,0:T(8,128)(2,1)S(1)} collective-permute-done((bf16[1152,256]{1,0:T(8,128)(2,1)S(1)}, bf16[1152,256]{1,0:T(8,128)(2,1)S(1)}, u32[]{:S(2)}, u32[]{:S(2)}) %collective-permute-start.17) | collective-permute-done | bytes 589856 | tf_op jit(solution)/shard_map/ppermute | solution.py:15
  53.9 1.5 %mix.5 = (f32[2,8,56,256]{3,2,1,0:T(8,128)S(1)}, bf16[2,8,56,256]{3,2,1,0:T(8,128)(2,1)S(1)}) custom-call(bf16[1152,256]{1,0:T(8,128)(2,1)S(1)} %collective-permute-done.17.w_ref, bf16[1024,1152]{1,0:T(8,128)(2,1)S(1)} %convolve.2.refs_0_, bf16[1024,1152]{1,0:T(8,128)(2,1)S(1)} %convolve.3.refs_0_.refs_1_), custom_call_target="tpu_custom_call" | custom-call | tf_op jit(solution)/shard_map/mix/pallas_call | solution.py:157
  57.0 1.6 %collective-permute-start.12 = (bf16[4,56,256]{2,1,0:T(8,128)(2,1)S(1)}, bf16[4,56,256]{2,1,0:T(8,128)(2,1)S(1)}, u32[]{:S(2)}, u32[]{:S(2)}) collective-permute-start(bf16[4,56,256]{2,1,0:T(8,128)(2,1)S(1)} %fusion.1), channel_id=1, source_target_pairs={{0,2},{1,3},{2,0},{3,1},{4,6},{5,7},{6,4},{7,5},{8,10},{9,11},{10,... | collective-permute-start | bytes 344072 | tf_op jit(solution)/shard_map/ppermute | solution.py:15
  59.2 1.6 %collective-permute-start.16 = (bf16[4,56,256]{2,1,0:T(8,128)(2,1)S(1)}, bf16[4,56,256]{2,1,0:T(8,128)(2,1)S(1)}, u32[]{:S(2)}, u32[]{:S(2)}) collective-permute-start(bf16[4,56,256]{2,1,0:T(8,128)(2,1)S(1)} %fusion.2), channel_id=1, source_target_pairs={{0,2},{1,3},{2,0},{3,1},{4,6},{5,7},{6,4},{7,5},{8,10},{9,11},{10,... | collective-permute-start | bytes 344072 | tf_op jit(solution)/shard_map/ppermute | solution.py:15
  60.8 2.2 %collective-permute-done.12.refs_2_ = bf16[4,56,256]{2,1,0:T(8,128)(2,1)S(1)} collective-permute-done((bf16[4,56,256]{2,1,0:T(8,128)(2,1)S(1)}, bf16[4,56,256]{2,1,0:T(8,128)(2,1)S(1)}, u32[]{:S(2)}, u32[]{:S(2)}) %collective-permute-start.12) | collective-permute-done | bytes 114720 | tf_op jit(solution)/shard_map/ppermute | solution.py:15
  63.1 6.4 %collective-permute-done.16.refs_5_ = bf16[4,56,256]{2,1,0:T(8,128)(2,1)S(1)} collective-permute-done((bf16[4,56,256]{2,1,0:T(8,128)(2,1)S(1)}, bf16[4,56,256]{2,1,0:T(8,128)(2,1)S(1)}, u32[]{:S(2)}, u32[]{:S(2)}) %collective-permute-start.16) | collective-permute-done | bytes 114720 | tf_op jit(solution)/shard_map/ppermute | solution.py:15
  69.5 1.2 %finish.1 = bf16[8,56,512]{2,1,0:T(8,128)(2,1)} custom-call(s32[1]{0:T(128)} %bitcast.turned_ref, f32[2,4,56,256]{3,2,1,0:T(8,128)S(1)} %get-tuple-element.11.refs_0_, bf16[2,4,56,256]{3,2,1,0:T(8,128)(2,1)S(1)} %collective-permute-done.11.refs_1_, bf16[4,56,256]{2,1,0:T(8,128)(2,1)S(1)} %collective-permute-done.12.refs_2_, ...), custom_call_target="tpu_custom_call" | custom-call | tf_op jit(solution)/shard_map/finish/pallas_call | solution.py:183
  (49 shorter events, 7.8 us)
Async XLA Ops:
  0.0 1.0 %copy-start = (bf16[288,512]{1,0:T(8,128)(2,1)S(1)}, bf16[288,512]{1,0:T(8,128)(2,1)}, u32[]{:S(2)}) copy-start(bf16[288,512]{1,0:T(8,128)(2,1)} %param.7) | copy-start | bytes 884740
  1.0 11.2 %collective-permute-start = (bf16[288,256]{1,0:T(8,128)(2,1)S(1)}, bf16[288,256]{1,0:T(8,128)(2,1)S(1)}, u32[]{:S(2)}, u32[]{:S(2)}) collective-permute-start(bf16[288,256]{1,0:T(8,128)(2,1)S(1)} %constant_dynamic-slice_fusion.4), channel_id=1, source_target_pairs={{0,8},{1,9},{2,10},{3,11},{4,12},{5,13},{6,14},{7,15},{8,0},{9,1},... | collective-permute-start | bytes 442376 | tf_op jit(solution)/shard_map/ppermute | solution.py:15
  5.1 12.4 %collective-permute-start.2 = (bf16[288,256]{1,0:T(8,128)(2,1)S(1)}, bf16[288,256]{1,0:T(8,128)(2,1)S(1)}, u32[]{:S(2)}, u32[]{:S(2)}) collective-permute-start(bf16[288,256]{1,0:T(8,128)(2,1)S(1)} %constant_dynamic-slice_fusion.4), channel_id=1, source_target_pairs={{0,4},{1,5},{2,6},{3,7},{4,0},{5,1},{6,2},{7,3},{8,12},{9,13},{10,... | collective-permute-start | bytes 442376 | tf_op jit(solution)/shard_map/ppermute | solution.py:15
  7.8 5.1 %collective-permute-start.6 = (bf16[8,56,128]{2,1,0:T(8,128)(2,1)S(1)}, bf16[8,56,128]{2,1,0:T(8,128)(2,1)S(1)}, u32[]{:S(2)}, u32[]{:S(2)}) collective-permute-start(bf16[8,56,128]{2,1,0:T(8,128)(2,1)S(1)} %get-tuple-element.30), channel_id=1, source_target_pairs={{0,1},{1,0},{2,3},{3,2},{4,5},{5,4},{6,7},{7,6},{8,9},{9,8},{10,11... | collective-permute-start | bytes 344072 | tf_op jit(solution)/shard_map/ppermute | solution.py:15
  7.9 6.0 %collective-permute-start.7 = (bf16[8,56,128]{2,1,0:T(8,128)(2,1)S(1)}, bf16[8,56,128]{2,1,0:T(8,128)(2,1)S(1)}, u32[]{:S(2)}, u32[]{:S(2)}) collective-permute-start(bf16[8,56,128]{2,1,0:T(8,128)(2,1)S(1)} %get-tuple-element.32), channel_id=1, source_target_pairs={{0,2},{1,3},{2,0},{3,1},{4,6},{5,7},{6,4},{7,5},{8,10},{9,11},{10,... | collective-permute-start | bytes 344072 | tf_op jit(solution)/shard_map/ppermute | solution.py:15
  9.4 6.0 %collective-permute-start.8 = (bf16[8,56,128]{2,1,0:T(8,128)(2,1)S(1)}, bf16[8,56,128]{2,1,0:T(8,128)(2,1)S(1)}, u32[]{:S(2)}, u32[]{:S(2)}) collective-permute-start(bf16[8,56,128]{2,1,0:T(8,128)(2,1)S(1)} %get-tuple-element.29), channel_id=1, source_target_pairs={{0,3},{1,2},{2,1},{3,0},{4,7},{5,6},{6,5},{7,4},{8,11},{9,10},{10,... | collective-permute-start | bytes 344072 | tf_op jit(solution)/shard_map/ppermute | solution.py:15
  12.2 5.5 %collective-permute-start.1 = (bf16[288,256]{1,0:T(8,128)(2,1)S(1)}, bf16[288,256]{1,0:T(8,128)(2,1)S(1)}, u32[]{:S(2)}, u32[]{:S(2)}) collective-permute-start(bf16[288,256]{1,0:T(8,128)(2,1)S(1)} %collective-permute-done), channel_id=1, source_target_pairs={{0,4},{1,5},{2,6},{3,7},{4,0},{5,1},{6,2},{7,3},{8,12},{9,13},{10,... | collective-permute-start | bytes 442376 | tf_op jit(solution)/shard_map/ppermute | solution.py:15
  15.4 24.8 %collective-permute-start.10 = (bf16[4,5,56,128]{3,2,1,0:T(8,128)(2,1)S(1)}, bf16[4,5,56,128]{3,2,1,0:T(8,128)(2,1)S(1)}, u32[]{:S(2)}, u32[]{:S(2)}) collective-permute-start(bf16[4,5,56,128]{3,2,1,0:T(8,128)(2,1)S(1)} %lay_out.2.refs_1_.refs_2_), channel_id=1, source_target_pairs={{0,12},{1,13},{2,14},{3,15},{4,0},{5,1},{6,2},{7,3},{8,4},{9,5},{1... | collective-permute-start | bytes 860168 | tf_op jit(solution)/shard_map/ppermute | solution.py:15
  15.8 24.4 %collective-permute-start.9 = (bf16[4,5,56,128]{3,2,1,0:T(8,128)(2,1)S(1)}, bf16[4,5,56,128]{3,2,1,0:T(8,128)(2,1)S(1)}, u32[]{:S(2)}, u32[]{:S(2)}) collective-permute-start(bf16[4,5,56,128]{3,2,1,0:T(8,128)(2,1)S(1)} %lay_out.2.refs_1_.refs_2_), channel_id=1, source_target_pairs={{0,4},{1,5},{2,6},{3,7},{4,8},{5,9},{6,10},{7,11},{8,12},{9,13},{1... | collective-permute-start | bytes 860168 | tf_op jit(solution)/shard_map/ppermute | solution.py:15
  18.0 2.2 %collective-permute-start.3 = (bf16[18,16,256]{2,1,0:T(8,128)(2,1)S(1)}, bf16[18,16,256]{2,1,0:T(8,128)(2,1)S(1)}, u32[]{:S(2)}, u32[]{:S(2)}) collective-permute-start(bf16[18,16,256]{2,1,0:T(8,128)(2,1)S(1)} %get-tuple-element.28), channel_id=1, source_target_pairs={{0,1},{1,0},{2,3},{3,2},{4,5},{5,4},{6,7},{7,6},{8,9},{9,8},{10,11... | collective-permute-start | bytes 442376 | tf_op jit(solution)/shard_map/ppermute | solution.py:15
  18.1 6.7 %collective-permute-start.4 = (bf16[18,16,256]{2,1,0:T(8,128)(2,1)S(1)}, bf16[18,16,256]{2,1,0:T(8,128)(2,1)S(1)}, u32[]{:S(2)}, u32[]{:S(2)}) collective-permute-start(bf16[18,16,256]{2,1,0:T(8,128)(2,1)S(1)} %get-tuple-element.27), channel_id=1, source_target_pairs={{0,2},{1,3},{2,0},{3,1},{4,6},{5,7},{6,4},{7,5},{8,10},{9,11},{10,... | collective-permute-start | bytes 442376 | tf_op jit(solution)/shard_map/ppermute | solution.py:15
  19.7 7.4 %collective-permute-start.5 = (bf16[18,16,256]{2,1,0:T(8,128)(2,1)S(1)}, bf16[18,16,256]{2,1,0:T(8,128)(2,1)S(1)}, u32[]{:S(2)}, u32[]{:S(2)}) collective-permute-start(bf16[18,16,256]{2,1,0:T(8,128)(2,1)S(1)} %get-tuple-element.26), channel_id=1, source_target_pairs={{0,3},{1,2},{2,1},{3,0},{4,7},{5,6},{6,5},{7,4},{8,11},{9,10},{10,... | collective-permute-start | bytes 442376 | tf_op jit(solution)/shard_map/ppermute | solution.py:15
  27.1 17.7 %collective-permute-start.13 = (bf16[4,3,56,128]{3,2,1,0:T(8,128)(2,1)S(1)}, bf16[4,3,56,128]{3,2,1,0:T(8,128)(2,1)S(1)}, u32[]{:S(2)}, u32[]{:S(2)}) collective-permute-start(bf16[4,3,56,128]{3,2,1,0:T(8,128)(2,1)S(1)} %lay_out.3.refs_3_), channel_id=1, source_target_pairs={{0,4},{1,5},{2,6},{3,7},{4,8},{5,9},{6,10},{7,11},{8,12},{9,13},{1... | collective-permute-start | bytes 516104 | tf_op jit(solution)/shard_map/ppermute | solution.py:15
  28.0 16.8 %collective-permute-start.14 = (bf16[4,3,56,128]{3,2,1,0:T(8,128)(2,1)S(1)}, bf16[4,3,56,128]{3,2,1,0:T(8,128)(2,1)S(1)}, u32[]{:S(2)}, u32[]{:S(2)}) collective-permute-start(bf16[4,3,56,128]{3,2,1,0:T(8,128)(2,1)S(1)} %lay_out.3.refs_3_), channel_id=1, source_target_pairs={{0,12},{1,13},{2,14},{3,15},{4,0},{5,1},{6,2},{7,3},{8,4},{9,5},{1... | collective-permute-start | bytes 516104 | tf_op jit(solution)/shard_map/ppermute | solution.py:15
  38.7 15.3 %collective-permute-start.17 = (bf16[1152,256]{1,0:T(8,128)(2,1)S(1)}, bf16[1152,256]{1,0:T(8,128)(2,1)S(1)}, u32[]{:S(2)}, u32[]{:S(2)}) collective-permute-start(bf16[1152,256]{1,0:T(8,128)(2,1)S(1)} %sort_weights.1.w_ref), channel_id=1, source_target_pairs={{0,16},{16,0},{1,17},{17,1},{2,18},{18,2},{3,19},{19,3},{4,20},{20... | collective-permute-start | bytes 1769480 | tf_op jit(solution)/shard_map/ppermute | solution.py:15
  44.7 12.3 %collective-permute-start.11 = (bf16[2,4,56,256]{3,2,1,0:T(8,128)(2,1)S(1)}, bf16[2,4,56,256]{3,2,1,0:T(8,128)(2,1)S(1)}, u32[]{:S(2)}, u32[]{:S(2)}) collective-permute-start(bf16[2,4,56,256]{3,2,1,0:T(8,128)(2,1)S(1)} %get-tuple-element.12), channel_id=1, source_target_pairs={{0,1},{1,0},{2,3},{3,2},{4,5},{5,4},{6,7},{7,6},{8,9},{9,8},{10,11... | collective-permute-start | bytes 688136 | tf_op jit(solution)/shard_map/ppermute | solution.py:15
  55.5 3.1 %collective-permute-start.18 = (bf16[2,8,56,256]{3,2,1,0:T(8,128)(2,1)S(1)}, bf16[2,8,56,256]{3,2,1,0:T(8,128)(2,1)S(1)}, u32[]{:S(2)}, u32[]{:S(2)}) collective-permute-start(bf16[2,8,56,256]{3,2,1,0:T(8,128)(2,1)S(1)} %get-tuple-element.16), channel_id=1, source_target_pairs={{0,1},{1,0},{2,3},{3,2},{4,5},{5,4},{6,7},{7,6},{8,9},{9,8},{10,11... | collective-permute-start | bytes 1376264 | tf_op jit(solution)/shard_map/ppermute | solution.py:15
  56.4 2.8 %collective-permute-start.15 = (bf16[2,4,56,256]{3,2,1,0:T(8,128)(2,1)S(1)}, bf16[2,4,56,256]{3,2,1,0:T(8,128)(2,1)S(1)}, u32[]{:S(2)}, u32[]{:S(2)}) collective-permute-start(bf16[2,4,56,256]{3,2,1,0:T(8,128)(2,1)S(1)} %get-tuple-element.14), channel_id=1, source_target_pairs={{0,1},{1,0},{2,3},{3,2},{4,5},{5,4},{6,7},{7,6},{8,9},{9,8},{10,11... | collective-permute-start | bytes 688136 | tf_op jit(solution)/shard_map/ppermute | solution.py:15
  57.0 6.1 %collective-permute-start.12 = (bf16[4,56,256]{2,1,0:T(8,128)(2,1)S(1)}, bf16[4,56,256]{2,1,0:T(8,128)(2,1)S(1)}, u32[]{:S(2)}, u32[]{:S(2)}) collective-permute-start(bf16[4,56,256]{2,1,0:T(8,128)(2,1)S(1)} %fusion.1), channel_id=1, source_target_pairs={{0,2},{1,3},{2,0},{3,1},{4,6},{5,7},{6,4},{7,5},{8,10},{9,11},{10,... | collective-permute-start | bytes 344072 | tf_op jit(solution)/shard_map/ppermute | solution.py:15
  58.6 10.9 %collective-permute-start.19 = (bf16[8,56,256]{2,1,0:T(8,128)(2,1)S(1)}, bf16[8,56,256]{2,1,0:T(8,128)(2,1)S(1)}, u32[]{:S(2)}, u32[]{:S(2)}) collective-permute-start(bf16[8,56,256]{2,1,0:T(8,128)(2,1)S(1)} %fusion), channel_id=1, source_target_pairs={{0,2},{1,3},{2,0},{3,1},{4,6},{5,7},{6,4},{7,5},{8,10},{9,11},{10,... | collective-permute-start | bytes 688136 | tf_op jit(solution)/shard_map/ppermute | solution.py:15
  59.2 10.3 %collective-permute-start.16 = (bf16[4,56,256]{2,1,0:T(8,128)(2,1)S(1)}, bf16[4,56,256]{2,1,0:T(8,128)(2,1)S(1)}, u32[]{:S(2)}, u32[]{:S(2)}) collective-permute-start(bf16[4,56,256]{2,1,0:T(8,128)(2,1)S(1)} %fusion.2), channel_id=1, source_target_pairs={{0,2},{1,3},{2,0},{3,1},{4,6},{5,7},{6,4},{7,5},{8,10},{9,11},{10,... | collective-permute-start | bytes 344072 | tf_op jit(solution)/shard_map/ppermute | solution.py:15

commit v3 on v2

--- a/solution.py
+++ b/solution.py
@@ -8,6 +8,7 @@
 MAXS = 4
 UNIT = 16
 VMEM = 28 << 20
+WORK = 4_500_000_000
 
 
 def send(value, axis, target_of):
@@ -64,13 +65,12 @@
         out_ref[start : start + pair.shape[0], :] = pair.astype(jnp.bfloat16)
 
 
-def convolve(place, packed, planes, first, bands):
+def convolve(place, packed, planes, slots, first, bands, ties):
     longitudes, chans = planes[0][0][1].shape[2:]
     count, filters, lanes = packed.shape
     rows = round_up(filters * longitudes, UNIT)
     segment = lanes // 3
     span = 3 * MAXS * longitudes
-    step = round_up(longitudes, UNIT)
     low, high = max(first - 1, 0), min(first + count + 1, bands)
     arrays, found = [], [{}, {}, {}]
     for t in range(3):
@@ -80,7 +80,7 @@
             arrays.append(array)
 
     def body(place_ref, packed_ref, *refs):
-        ins, (mixin, line, windows, toeplitz) = refs[: len(arrays)], refs[len(arrays) :]
+        ins, (mixin, line, windows, toeplitz) = refs[: len(arrays)], refs[len(arrays) + len(ties) :]
         here = place_ref[0]
         line[:, span:, :] = jnp.zeros((2, line.shape[1] - span, chans), jnp.float32)
         for b in range(low, high):
@@ -91,10 +91,10 @@
                     start = (t * MAXS + p) * longitudes
                     line[side, start : start + longitudes, :] = ins[which][p ^ here, at].astype(jnp.float32)
             start = (b - low) * segment
-            for r in range(MAXS):
+            for n, r in enumerate(slots):
                 begin = pl.multiple_of((r ^ here) * longitudes, 8)
                 part = line[side, pl.ds(begin, segment), :].astype(jnp.bfloat16)
-                windows[start : start + segment, r * chans : (r + 1) * chans] = part
+                windows[start : start + segment, n * chans : (n + 1) * chans] = part
         for c in range(count):
             i = first + c
             from_band, to_band = max(i - 1, 0), min(i + 2, bands)
@@ -103,81 +103,84 @@
             matrix = matrix[:, (from_band - i + 1) * segment : (to_band - i + 1) * segment]
             window = windows[(from_band - low) * segment : (to_band - low) * segment, :]
             conv = jnp.dot(matrix, window, preferred_element_type=jnp.float32)
-            for r in range(MAXS):
-                parts = [
-                    conv[k * longitudes : (k + 1) * longitudes, r * chans : (r + 1) * chans]
-                    for k in range(filters)
-                ]
-                part = jnp.concatenate(parts, 1)
-                fill = jnp.zeros((step - longitudes, part.shape[1]), jnp.float32)
-                start = (c * MAXS + r) * step
-                mixin[start : start + step, :] = jnp.concatenate([part, fill], 0).astype(jnp.bfloat16)
+            for pair in range(0, len(slots), 2):
+                rows_of = []
+                for n in (pair, pair + 1):
+                    parts = [
+                        conv[k * longitudes : (k + 1) * longitudes, n * chans : (n + 1) * chans]
+                        for k in range(filters)
+                    ]
+                    rows_of.append(jnp.concatenate(parts, 1))
+                start = (pair // 2 * count + c) * 2 * longitudes
+                mixin[start : start + 2 * longitudes, :] = jnp.concatenate(rows_of, 0).astype(jnp.bfloat16)
 
     vmem = pl.BlockSpec(memory_space=pltpu.VMEM)
     return pl.pallas_call(
         body,
-        in_specs=[pl.BlockSpec(memory_space=pltpu.SMEM)] + [vmem] * (1 + len(arrays)),
+        in_specs=[pl.BlockSpec(memory_space=pltpu.SMEM)]
+        + [vmem] * (1 + len(arrays))
+        + [pl.BlockSpec(memory_space=pl.ANY)] * len(ties),
         out_specs=vmem,
-        out_shape=jax.ShapeDtypeStruct((count * MAXS * step, filters * chans), jnp.bfloat16),
+        out_shape=jax.ShapeDtypeStruct((count * len(slots) * longitudes, filters * chans), jnp.bfloat16),
         scratch_shapes=[
             pltpu.VMEM((2, round_up((MAXS - 1) * longitudes + max(segment, span), 8), chans), jnp.float32),
-            pltpu.VMEM(((high - low) * segment, MAXS * chans), jnp.bfloat16),
+            pltpu.VMEM(((high - low) * segment, len(slots) * chans), jnp.bfloat16),
             pltpu.VMEM((2, rows, lanes), jnp.bfloat16),
         ],
         compiler_params=pltpu.CompilerParams(vmem_limit_bytes=VMEM),
         cost_estimate=pl.CostEstimate(
-            flops=2 * count * rows * lanes * MAXS * chans, bytes_accessed=1, transcendentals=0
+            flops=WORK, bytes_accessed=1, transcendentals=0
         ),
         name="convolve",
-    )(place, packed, *arrays)
-
-
-def mix(convolved, weights, longitudes):
-    step = round_up(longitudes, UNIT)
-    counts = [array.shape[0] // (MAXS * step) for array in convolved]
-    outs = weights.shape[1]
-
-    def body(w_ref, *refs):
-        ins, (kept_ref, sent_ref) = refs[:-2], refs[-2:]
-        first = 0
-        for ref, count in zip(ins, counts):
-            mixed = jnp.dot(ref[...], w_ref[...], preferred_element_type=jnp.float32)
-            for c in range(count):
-                for r in range(MAXS):
-                    start = (c * MAXS + r) * step
+    )(place, packed, *arrays, *ties)
+
+
+def mix(convolved, slots, weights, longitudes, ties):
+    pair = convolved.shape[0] // (MAXS // 2)
+    count = pair // (2 * longitudes)
+    half = len(slots) // 2
+    width = weights[0].shape[1]
+    begin = slots[0] // 2 * pair
+
+    def body(conv_ref, *refs):
+        kept_ref, sent_ref = refs[-2:]
+        block = conv_ref[begin : begin + half * pair, :]
+        for n in range(len(weights)):
+            mixed = jnp.dot(block, refs[n][...], preferred_element_type=jnp.float32)
+            for h in range(half):
+                for c in range(count):
+                    start = h * pair + c * 2 * longitudes
                     value = mixed[start : start + longitudes]
-                    if r % 2 == 0:
-                        kept_ref[r // 2, first + c] = value
-                    else:
-                        sent_ref[r // 2, first + c] = value.astype(jnp.bfloat16)
-            first += count
+                    kept_ref[h, c, :, n * width : (n + 1) * width] = value
+                    value = mixed[start + longitudes : start + 2 * longitudes].astype(jnp.bfloat16)
+                    sent_ref[h, c, :, n * width : (n + 1) * width] = value
 
     vmem = pl.BlockSpec(memory_space=pltpu.VMEM)
-    shape = (2, sum(counts), longitudes, outs)
+    shape = (half, count, longitudes, len(weights) * width)
     return pl.pallas_call(
         body,
-        in_specs=[vmem] * (1 + len(convolved)),
+        in_specs=[vmem] * (1 + len(weights)) + [pl.BlockSpec(memory_space=pl.ANY)] * len(ties),
         out_specs=[vmem, vmem],
         out_shape=[jax.ShapeDtypeStruct(shape, jnp.float32), jax.ShapeDtypeStruct(shape, jnp.bfloat16)],
         compiler_params=pltpu.CompilerParams(vmem_limit_bytes=VMEM),
         name="mix",
-    )(weights, *convolved)
-
-
-def finish(turned, sums, bands):
-    longitudes, width = sums[0][1].shape[2:]
+    )(convolved, *weights, *ties)
+
+
+def finish(turned, sums, width, bands):
+    longitudes = sums[0][2].shape[2]
 
     def body(turned_ref, *refs):
         out_ref = refs[-1]
-        reached = [0, 0]
-        for n, (half, kept, _, _) in enumerate(sums):
+        for n, (first, halves, kept, _, _) in enumerate(sums):
             kept_ref, core_ref, across_ref = refs[3 * n : 3 * n + 3]
-            column = pl.multiple_of((turned_ref[0] ^ half) * width, width)
-            for band in range(kept.shape[1]):
-                total = kept_ref[0, band] + core_ref[0, band].astype(jnp.float32)
-                total += across_ref[band].astype(jnp.float32)
-                out_ref[reached[half], :, pl.ds(column, width)] = jax.nn.gelu(total).astype(jnp.bfloat16)
-                reached[half] += 1
+            for m, half in enumerate(halves):
+                column = pl.multiple_of((turned_ref[0] ^ half) * width, width)
+                from_ = slice(m * width, (m + 1) * width)
+                for band in range(kept.shape[1]):
+                    total = kept_ref[0, band, :, from_] + core_ref[0, band, :, from_].astype(jnp.float32)
+                    total += across_ref[band, :, from_].astype(jnp.float32)
+                    out_ref[first + band, :, pl.ds(column, width)] = jax.nn.gelu(total).astype(jnp.bfloat16)
 
     vmem = pl.BlockSpec(memory_space=pltpu.VMEM)
     return pl.pallas_call(
@@ -187,7 +190,7 @@
         out_shape=jax.ShapeDtypeStruct((bands, longitudes, 2 * width), jnp.bfloat16),
         compiler_params=pltpu.CompilerParams(vmem_limit_bytes=VMEM),
         name="finish",
-    )(turned, *(array for entry in sums for array in entry[1:]))
+    )(turned, *(array for entry in sums for array in entry[2:]))
 
 
 def gather_weights(mixing, filters, channels):
@@ -264,7 +267,7 @@
     place = lax.axis_index("lon") % MAXS
     segment = round_up((2 * MAXS + 1) * longitudes, 128)
     packed = packed_basis(basis_table, support, longitudes, segment)
-    cuts = ((0, 4), (4, 8))
+    cuts = ((0, 6), (6, 8))
 
     def quarter(r):
         return lax.dynamic_slice_in_dim(inputs, (place ^ r) * chans, chans, 2)
@@ -287,20 +290,40 @@
     ours, theirs, turned = sort()
 
     here = place.reshape(1).astype(jnp.int32)
-    convolved = []
-    for index, (first, last) in enumerate(cuts):
+
+    def convolved(index, slots, ties):
+        first, last = cuts[index]
         low, high = max(first - 1, 0), min(last + 1, bands)
         needed = [[(s, a) for s, a in held if s < high and s + a.shape[1] > low] for held in planes]
-        convolved.append(convolve(here, packed[first:last], needed, first, bands))
-
-    def summed(half, arrays, weights):
-        kept, sent = mix(arrays, weights, longitudes)
-        core = send(sent, "lon", lambda s: s ^ 1)
-        across = (kept[1] + core[1].astype(jnp.float32)).astype(jnp.bfloat16)
-        return half, kept, core, send(across, "lon", lambda s: s ^ 2)
-
-    sums = [summed(0, [array], ours) for array in convolved] + [summed(1, convolved, theirs)]
-    return finish(turned.reshape(1).astype(jnp.int32), sums, bands)
+        return convolve(here, packed[first:last], needed, slots, first, bands, ties)
+
+    def over_core(sent):
+        return send(sent, "lon", lambda s: s ^ 1)
+
+    def added(kept, core):
+        return (kept + core.astype(jnp.float32)).astype(jnp.bfloat16)
+
+    def over_y(value):
+        return send(value, "lon", lambda s: s ^ 2)
+
+    every = tuple(range(MAXS))
+    sums = []
+    conv0 = convolved(0, every, [])
+    kept_a, sent_a = mix(conv0, every, [ours], longitudes, [planes[0][1][1], planes[2][1][1]])
+    core_a = over_core(sent_a)
+    part_a = added(kept_a[1], core_a[1])
+    across_a = over_y(part_a)
+    sums.append((cuts[0][0], (0,), kept_a, core_a, across_a))
+    kept_b, sent_b = mix(conv0, every, [theirs], longitudes, [])
+    core_b = over_core(sent_b)
+    part_b = added(kept_b[1], core_b[1])
+    across_b = over_y(part_b)
+    sums.append((cuts[0][0], (1,), kept_b, core_b, across_b))
+    conv1 = convolved(1, every, [])
+    kept, sent = mix(conv1, every, [ours, theirs], longitudes, [across_a])
+    core = over_core(sent)
+    sums.append((cuts[1][0], (0, 1), kept, core, over_y(added(kept[1], core[1]))))
+    return finish(turned.reshape(1).astype(jnp.int32), sums, ours.shape[1], bands)
 
 
 def solution(mesh):

time: 70.9 us -> 62.9 us (0.89)
  starting transfers between devices: 29.1 us -> 24.5 us
  waiting for transfers between devices: 24.4 us -> 21.4 us
    ppermute x20, starting transfers between devices: 29.1 us -> 24.5 us  [send(): return lax.ppermute(value, axis, [(s, target_of(s)) for s in range(count)])]
    ppermute x20, waiting for transfers between devices: 24.4 us -> 21.4 us  [send(): return lax.ppermute(value, axis, [(s, target_of(s)) for s in range(count)])]
  transfers between devices with their start and end apart: 20 -> 20, of which waited for: 9 -> 10; matrix products, arithmetic and copies ran while one was open for 5% -> 6% of each run, Pallas kernels for 16% -> 17%
where the time goes in v3:
time: 62.9 us; the launch traced here: 62.7 us
  starting transfers between devices  24.5 us (39%)
  waiting for transfers between devices  21.4 us (34%)
  Pallas kernels  11.9 us (19%)
  local copies, waits for them, and re-layouts  2.38 us (4%)
  other arithmetic  2.34 us (4%)
    ppermute x20, starting transfers between devices, send(): return lax.ppermute(value, axis, [(s, target_of(s)) for s in range(count)])  24.5 us
    ppermute x20, waiting for transfers between devices, send(): return lax.ppermute(value, axis, [(s, target_of(s)) for s in range(count)])  21.4 us
    pallas_call x2, Pallas kernels, convolve(): pl.pallas_call(body, in_specs=[pl.BlockSpec(memory_space=pltpu.SMEM)] + [...  7.17 us
    pallas_call x3, Pallas kernels, mix(): pl.pallas_call(body, in_specs=[vmem] * (1 + len(weights)) + [pl.BlockSpec...  2.87 us
  transfers between devices with their start and end apart: 20, of which 10 were waited for; matrix products, arithmetic and copies ran while one was open for 6% of the time, Pallas kernels for 17%

profile of v3, /device:TPU:0, one launch (start us, length us, event | category | flops | bytes accessed | tf_op | source)
XLA Modules:
  0.0 62.7 jit_solution(10191417188334851810)
XLA Ops:
  1.0 4.1 %collective-permute-start.5 = (bf16[288,256]{1,0:T(8,128)(2,1)S(1)}, bf16[288,256]{1,0:T(8,128)(2,1)S(1)}, u32[]{:S(2)}, u32[]{:S(2)}) collective-permute-start(bf16[288,256]{1,0:T(8,128)(2,1)S(1)} %constant_dynamic-slice_fusion), channel_id=1, source_target_pairs={{0,8},{1,9},{2,10},{3,11},{4,12},{5,13},{6,14},{7,15},{8,0},{9,1},... | collective-permute-start | bytes 442376 | tf_op jit(solution)/shard_map/ppermute | solution.py:16
  5.1 1.6 %collective-permute-start.7 = (bf16[288,256]{1,0:T(8,128)(2,1)S(1)}, bf16[288,256]{1,0:T(8,128)(2,1)S(1)}, u32[]{:S(2)}, u32[]{:S(2)}) collective-permute-start(bf16[288,256]{1,0:T(8,128)(2,1)S(1)} %constant_dynamic-slice_fusion), channel_id=1, source_target_pairs={{0,4},{1,5},{2,6},{3,7},{4,0},{5,1},{6,2},{7,3},{8,12},{9,13},{10,... | collective-permute-start | bytes 442376 | tf_op jit(solution)/shard_map/ppermute | solution.py:16
  6.7 1.1 %constant_dynamic-slice_fusion.1 = (bf16[8,56,128]{2,1,0:T(8,128)(2,1)S(1)}, bf16[8,56,128]{2,1,0:T(8,128)(2,1)S(1)}, bf16[8,56,128]{2,1,0:T(8,128)(2,1)S(1)}, bf16[8,56,128]{2,1,0:T(8,128)(2,1)S(1)}) fusion(bf16[8,56,512]{2,1,0:T(8,128)(2,1)} %param.4, s32[]{:T(128)S(6)} %select_n.237, s32[]{:T(128)S(6)} %select_n.235, s32[]{:T(128)S(6)} %select_n.234, ...), kind=kLoop, calls=%fused_computation.39 | loop fusion | bytes 917520 | tf_op jit(solution)/shard_map/dynamic_slice | solution.py:273
  7.9 1.6 %collective-permute-start.1 = (bf16[8,56,128]{2,1,0:T(8,128)(2,1)S(1)}, bf16[8,56,128]{2,1,0:T(8,128)(2,1)S(1)}, u32[]{:S(2)}, u32[]{:S(2)}) collective-permute-start(bf16[8,56,128]{2,1,0:T(8,128)(2,1)S(1)} %get-tuple-element.32), channel_id=1, source_target_pairs={{0,2},{1,3},{2,0},{3,1},{4,6},{5,7},{6,4},{7,5},{8,10},{9,11},{10,... | collective-permute-start | bytes 344072 | tf_op jit(solution)/shard_map/ppermute | solution.py:16
  12.8 1.0 %collective-permute-done.1.refs_2_ = bf16[8,56,128]{2,1,0:T(8,128)(2,1)S(1)} collective-permute-done((bf16[8,56,128]{2,1,0:T(8,128)(2,1)S(1)}, bf16[8,56,128]{2,1,0:T(8,128)(2,1)S(1)}, u32[]{:S(2)}, u32[]{:S(2)}) %collective-permute-start.1) | collective-permute-done | bytes 114720 | tf_op jit(solution)/shard_map/ppermute | solution.py:16
  13.9 1.6 %collective-permute-done.2.refs_3_ = bf16[8,56,128]{2,1,0:T(8,128)(2,1)S(1)} collective-permute-done((bf16[8,56,128]{2,1,0:T(8,128)(2,1)S(1)}, bf16[8,56,128]{2,1,0:T(8,128)(2,1)S(1)}, u32[]{:S(2)}, u32[]{:S(2)}) %collective-permute-start.2) | collective-permute-done | bytes 114720 | tf_op jit(solution)/shard_map/ppermute | solution.py:16
  15.9 3.4 %collective-permute-start.4 = (bf16[4,7,56,128]{3,2,1,0:T(8,128)(2,1)S(1)}, bf16[4,7,56,128]{3,2,1,0:T(8,128)(2,1)S(1)}, u32[]{:S(2)}, u32[]{:S(2)}) collective-permute-start(bf16[4,7,56,128]{3,2,1,0:T(8,128)(2,1)S(1)} %lay_out.2.refs_1_.refs_2_), channel_id=1, source_target_pairs={{0,12},{1,13},{2,14},{3,15},{4,0},{5,1},{6,2},{7,3},{8,4},{9,5},{1... | collective-permute-start | bytes 1204232 | tf_op jit(solution)/shard_map/ppermute | solution.py:16
  19.6 1.2 %collective-permute-start.10 = (bf16[18,16,256]{2,1,0:T(8,128)(2,1)S(1)}, bf16[18,16,256]{2,1,0:T(8,128)(2,1)S(1)}, u32[]{:S(2)}, u32[]{:S(2)}) collective-permute-start(bf16[18,16,256]{2,1,0:T(8,128)(2,1)S(1)} %get-tuple-element.26), channel_id=1, source_target_pairs={{0,3},{1,2},{2,1},{3,0},{4,7},{5,6},{6,5},{7,4},{8,11},{9,10},{10,... | collective-permute-start | bytes 442376 | tf_op jit(solution)/shard_map/ppermute | solution.py:16
  22.1 3.5 %collective-permute-done.10.refs_6_ = bf16[18,16,256]{2,1,0:T(8,128)(2,1)S(1)} collective-permute-done((bf16[18,16,256]{2,1,0:T(8,128)(2,1)S(1)}, bf16[18,16,256]{2,1,0:T(8,128)(2,1)S(1)}, u32[]{:S(2)}, u32[]{:S(2)}) %collective-permute-start.10) | collective-permute-done | bytes 147488 | tf_op jit(solution)/shard_map/ppermute | solution.py:16
  25.7 3.3 %collective-permute-done.9.refs_5_ = bf16[18,16,256]{2,1,0:T(8,128)(2,1)S(1)} collective-permute-done((bf16[18,16,256]{2,1,0:T(8,128)(2,1)S(1)}, bf16[18,16,256]{2,1,0:T(8,128)(2,1)S(1)}, u32[]{:S(2)}, u32[]{:S(2)}) %collective-permute-start.9) | collective-permute-done | bytes 147488 | tf_op jit(solution)/shard_map/ppermute | solution.py:16
  29.0 3.8 %collective-permute-start.12 = (bf16[4,1,56,128]{3,2,1,0:T(8,128)(2,1)S(1)}, bf16[4,1,56,128]{3,2,1,0:T(8,128)(2,1)S(1)}, u32[]{:S(2)}, u32[]{:S(2)}) collective-permute-start(bf16[4,1,56,128]{3,2,1,0:T(8,128)(2,1)S(1)} %lay_out.3.refs_3_), channel_id=1, source_target_pairs={{0,12},{1,13},{2,14},{3,15},{4,0},{5,1},{6,2},{7,3},{8,4},{9,5},{1... | collective-permute-start | bytes 172040 | tf_op jit(solution)/shard_map/ppermute | solution.py:16
  33.5 1.6 %collective-permute-start.15 = (bf16[1152,256]{1,0:T(8,128)(2,1)S(1)}, bf16[1152,256]{1,0:T(8,128)(2,1)S(1)}, u32[]{:S(2)}, u32[]{:S(2)}) collective-permute-start(bf16[1152,256]{1,0:T(8,128)(2,1)S(1)} %sort_weights.1.refs_0_), channel_id=1, source_target_pairs={{0,16},{16,0},{1,17},{17,1},{2,18},{18,2},{3,19},{19,3},{4,20},{20... | collective-permute-start | bytes 1769480 | tf_op jit(solution)/shard_map/ppermute | solution.py:16
  35.1 1.5 %collective-permute-done.4.refs_2_.refs_4_ = bf16[4,7,56,128]{3,2,1,0:T(8,128)(2,1)S(1)} collective-permute-done((bf16[4,7,56,128]{3,2,1,0:T(8,128)(2,1)S(1)}, bf16[4,7,56,128]{3,2,1,0:T(8,128)(2,1)S(1)}, u32[]{:S(2)}, u32[]{:S(2)}) %collective-permute-start.4) | collective-permute-done | bytes 401440 | tf_op jit(solution)/shard_map/ppermute | solution.py:16
  36.5 5.4 %convolve.2.conv_ref = bf16[1344,1152]{1,0:T(8,128)(2,1)S(1)} custom-call(s32[1]{0:T(128)} %bitcast.1.place_ref, f32[6,9,1536]{2,1,0:T(8,128)S(1)} %copy.7.packed_ref, bf16[4,7,56,128]{3,2,1,0:T(8,128)(2,1)S(1)} %collective-permute-done.3.refs_0_, bf16[4,7,56,128]{3,2,1,0:T(8,128)(2,1)S(1)} %lay_out.2.refs_1_.refs_2_, ...), custom_call_target="tpu_custom_call" | custom-call | flops 4499999744 | bytes 1 | tf_op jit(solution)/shard_map/convolve/pallas_call | solution.py:118
  42.0 1.1 %mix.3 = (f32[2,6,56,256]{3,2,1,0:T(8,128)S(1)}, bf16[2,6,56,256]{3,2,1,0:T(8,128)(2,1)S(1)}) custom-call(bf16[1344,1152]{1,0:T(8,128)(2,1)S(1)} %convolve.2.conv_ref, bf16[1152,256]{1,0:T(8,128)(2,1)S(1)} %sort_weights.1.refs_0_, bf16[4,1,56,128]{3,2,1,0:T(8,128)(2,1)S(1)} %collective-permute-done.11.refs_1_, ...), custom_call_target="tpu_custom_call" | custom-call | tf_op jit(solution)/shard_map/mix/pallas_call | solution.py:160
  43.2 1.5 %collective-permute-done.13.refs_1_ = bf16[2,6,56,256]{3,2,1,0:T(8,128)(2,1)S(1)} collective-permute-done((bf16[2,6,56,256]{3,2,1,0:T(8,128)(2,1)S(1)}, bf16[2,6,56,256]{3,2,1,0:T(8,128)(2,1)S(1)}, u32[]{:S(2)}, u32[]{:S(2)}) %collective-permute-start.13) | collective-permute-done | bytes 344096 | tf_op jit(solution)/shard_map/ppermute | solution.py:16
  44.8 1.6 %collective-permute-start.14 = (bf16[6,56,256]{2,1,0:T(8,128)(2,1)S(1)}, bf16[6,56,256]{2,1,0:T(8,128)(2,1)S(1)}, u32[]{:S(2)}, u32[]{:S(2)}) collective-permute-start(bf16[6,56,256]{2,1,0:T(8,128)(2,1)S(1)} %fusion), channel_id=1, source_target_pairs={{0,2},{1,3},{2,0},{3,1},{4,6},{5,7},{6,4},{7,5},{8,10},{9,11},{10,... | collective-permute-start | bytes 516104 | tf_op jit(solution)/shard_map/ppermute | solution.py:16
  46.4 1.8 %collective-permute-done.15.refs_0_.refs_1_ = bf16[1152,256]{1,0:T(8,128)(2,1)S(1)} collective-permute-done((bf16[1152,256]{1,0:T(8,128)(2,1)S(1)}, bf16[1152,256]{1,0:T(8,128)(2,1)S(1)}, u32[]{:S(2)}, u32[]{:S(2)}) %collective-permute-start.15) | collective-permute-done | bytes 589856 | tf_op jit(solution)/shard_map/ppermute | solution.py:16
  48.2 1.1 %mix.4 = (f32[2,6,56,256]{3,2,1,0:T(8,128)S(1)}, bf16[2,6,56,256]{3,2,1,0:T(8,128)(2,1)S(1)}) custom-call(bf16[1344,1152]{1,0:T(8,128)(2,1)S(1)} %convolve.2.conv_ref, bf16[1152,256]{1,0:T(8,128)(2,1)S(1)} %collective-permute-done.15.refs_0_.refs_1_), custom_call_target="tpu_custom_call" | custom-call | tf_op jit(solution)/shard_map/mix/pallas_call | solution.py:160
  49.3 1.8 %convolve.3.conv_ref = bf16[448,1152]{1,0:T(8,128)(2,1)S(1)} custom-call(s32[1]{0:T(128)} %bitcast.1.place_ref, f32[2,9,1536]{2,1,0:T(8,128)S(1)} %copy.8.packed_ref, bf16[4,7,56,128]{3,2,1,0:T(8,128)(2,1)S(1)} %collective-permute-done.3.refs_0_, bf16[4,1,56,128]{3,2,1,0:T(8,128)(2,1)S(1)} %collective-permute-done.11.refs_1_, ...), custom_call_target="tpu_custom_call" | custom-call | flops 4499999744 | bytes 1 | tf_op jit(solution)/shard_map/convolve/pallas_call | solution.py:118
  52.5 1.6 %collective-permute-start.17 = (bf16[6,56,256]{2,1,0:T(8,128)(2,1)S(1)}, bf16[6,56,256]{2,1,0:T(8,128)(2,1)S(1)}, u32[]{:S(2)}, u32[]{:S(2)}) collective-permute-start(bf16[6,56,256]{2,1,0:T(8,128)(2,1)S(1)} %fusion.1), channel_id=1, source_target_pairs={{0,2},{1,3},{2,0},{3,1},{4,6},{5,7},{6,4},{7,5},{8,10},{9,11},{10,... | collective-permute-start | bytes 516104 | tf_op jit(solution)/shard_map/ppermute | solution.py:16
  54.1 1.1 %collective-permute-start.19 = (bf16[2,56,512]{2,1,0:T(8,128)(2,1)S(1)}, bf16[2,56,512]{2,1,0:T(8,128)(2,1)S(1)}, u32[]{:S(2)}, u32[]{:S(2)}) collective-permute-start(bf16[2,56,512]{2,1,0:T(8,128)(2,1)S(1)} %fusion.2), channel_id=1, source_target_pairs={{0,2},{1,3},{2,0},{3,1},{4,6},{5,7},{6,4},{7,5},{8,10},{9,11},{10,... | collective-permute-start | bytes 344072 | tf_op jit(solution)/shard_map/ppermute | solution.py:16
  55.2 6.2 %collective-permute-done.19.refs_8_ = bf16[2,56,512]{2,1,0:T(8,128)(2,1)S(1)} collective-permute-done((bf16[2,56,512]{2,1,0:T(8,128)(2,1)S(1)}, bf16[2,56,512]{2,1,0:T(8,128)(2,1)S(1)}, u32[]{:S(2)}, u32[]{:S(2)}) %collective-permute-start.19) | collective-permute-done | bytes 114720 | tf_op jit(solution)/shard_map/ppermute | solution.py:16
  61.5 1.2 %finish.1 = bf16[8,56,512]{2,1,0:T(8,128)(2,1)} custom-call(s32[1]{0:T(128)} %bitcast.turned_ref, f32[2,6,56,256]{3,2,1,0:T(8,128)S(1)} %get-tuple-element.11.refs_0_, bf16[2,6,56,256]{3,2,1,0:T(8,128)(2,1)S(1)} %collective-permute-done.13.refs_1_, bf16[6,56,256]{2,1,0:T(8,128)(2,1)S(1)} %collective-permute-done.14.refs_2_, ...), custom_call_target="tpu_custom_call" | custom-call | tf_op jit(solution)/shard_map/finish/pallas_call | solution.py:186
  (49 shorter events, 8.9 us)
Async XLA Ops:
  0.0 1.0 %copy-start = (bf16[288,512]{1,0:T(8,128)(2,1)S(1)}, bf16[288,512]{1,0:T(8,128)(2,1)}, u32[]{:S(2)}) copy-start(bf16[288,512]{1,0:T(8,128)(2,1)} %param.7) | copy-start | bytes 884740
  1.0 11.2 %collective-permute-start.5 = (bf16[288,256]{1,0:T(8,128)(2,1)S(1)}, bf16[288,256]{1,0:T(8,128)(2,1)S(1)}, u32[]{:S(2)}, u32[]{:S(2)}) collective-permute-start(bf16[288,256]{1,0:T(8,128)(2,1)S(1)} %constant_dynamic-slice_fusion), channel_id=1, source_target_pairs={{0,8},{1,9},{2,10},{3,11},{4,12},{5,13},{6,14},{7,15},{8,0},{9,1},... | collective-permute-start | bytes 442376 | tf_op jit(solution)/shard_map/ppermute | solution.py:16
  5.1 14.2 %collective-permute-start.7 = (bf16[288,256]{1,0:T(8,128)(2,1)S(1)}, bf16[288,256]{1,0:T(8,128)(2,1)S(1)}, u32[]{:S(2)}, u32[]{:S(2)}) collective-permute-start(bf16[288,256]{1,0:T(8,128)(2,1)S(1)} %constant_dynamic-slice_fusion), channel_id=1, source_target_pairs={{0,4},{1,5},{2,6},{3,7},{4,0},{5,1},{6,2},{7,3},{8,12},{9,13},{10,... | collective-permute-start | bytes 442376 | tf_op jit(solution)/shard_map/ppermute | solution.py:16
  7.8 5.0 %collective-permute-start = (bf16[8,56,128]{2,1,0:T(8,128)(2,1)S(1)}, bf16[8,56,128]{2,1,0:T(8,128)(2,1)S(1)}, u32[]{:S(2)}, u32[]{:S(2)}) collective-permute-start(bf16[8,56,128]{2,1,0:T(8,128)(2,1)S(1)} %get-tuple-element.30), channel_id=1, source_target_pairs={{0,1},{1,0},{2,3},{3,2},{4,5},{5,4},{6,7},{7,6},{8,9},{9,8},{10,11... | collective-permute-start | bytes 344072 | tf_op jit(solution)/shard_map/ppermute | solution.py:16
  7.9 6.0 %collective-permute-start.1 = (bf16[8,56,128]{2,1,0:T(8,128)(2,1)S(1)}, bf16[8,56,128]{2,1,0:T(8,128)(2,1)S(1)}, u32[]{:S(2)}, u32[]{:S(2)}) collective-permute-start(bf16[8,56,128]{2,1,0:T(8,128)(2,1)S(1)} %get-tuple-element.32), channel_id=1, source_target_pairs={{0,2},{1,3},{2,0},{3,1},{4,6},{5,7},{6,4},{7,5},{8,10},{9,11},{10,... | collective-permute-start | bytes 344072 | tf_op jit(solution)/shard_map/ppermute | solution.py:16
  9.4 6.0 %collective-permute-start.2 = (bf16[8,56,128]{2,1,0:T(8,128)(2,1)S(1)}, bf16[8,56,128]{2,1,0:T(8,128)(2,1)S(1)}, u32[]{:S(2)}, u32[]{:S(2)}) collective-permute-start(bf16[8,56,128]{2,1,0:T(8,128)(2,1)S(1)} %get-tuple-element.29), channel_id=1, source_target_pairs={{0,3},{1,2},{2,1},{3,0},{4,7},{5,6},{6,5},{7,4},{8,11},{9,10},{10,... | collective-permute-start | bytes 344072 | tf_op jit(solution)/shard_map/ppermute | solution.py:16
  12.2 7.1 %collective-permute-start.6 = (bf16[288,256]{1,0:T(8,128)(2,1)S(1)}, bf16[288,256]{1,0:T(8,128)(2,1)S(1)}, u32[]{:S(2)}, u32[]{:S(2)}) collective-permute-start(bf16[288,256]{1,0:T(8,128)(2,1)S(1)} %collective-permute-done.5), channel_id=1, source_target_pairs={{0,4},{1,5},{2,6},{3,7},{4,0},{5,1},{6,2},{7,3},{8,12},{9,13},{10,... | collective-permute-start | bytes 442376 | tf_op jit(solution)/shard_map/ppermute | solution.py:16
  15.4 19.6 %collective-permute-start.3 = (bf16[4,7,56,128]{3,2,1,0:T(8,128)(2,1)S(1)}, bf16[4,7,56,128]{3,2,1,0:T(8,128)(2,1)S(1)}, u32[]{:S(2)}, u32[]{:S(2)}) collective-permute-start(bf16[4,7,56,128]{3,2,1,0:T(8,128)(2,1)S(1)} %lay_out.2.refs_1_.refs_2_), channel_id=1, source_target_pairs={{0,4},{1,5},{2,6},{3,7},{4,8},{5,9},{6,10},{7,11},{8,12},{9,13},{1... | collective-permute-start | bytes 1204232 | tf_op jit(solution)/shard_map/ppermute | solution.py:16
  15.9 20.6 %collective-permute-start.4 = (bf16[4,7,56,128]{3,2,1,0:T(8,128)(2,1)S(1)}, bf16[4,7,56,128]{3,2,1,0:T(8,128)(2,1)S(1)}, u32[]{:S(2)}, u32[]{:S(2)}) collective-permute-start(bf16[4,7,56,128]{3,2,1,0:T(8,128)(2,1)S(1)} %lay_out.2.refs_1_.refs_2_), channel_id=1, source_target_pairs={{0,12},{1,13},{2,14},{3,15},{4,0},{5,1},{6,2},{7,3},{8,4},{9,5},{1... | collective-permute-start | bytes 1204232 | tf_op jit(solution)/shard_map/ppermute | solution.py:16
  19.6 6.0 %collective-permute-start.10 = (bf16[18,16,256]{2,1,0:T(8,128)(2,1)S(1)}, bf16[18,16,256]{2,1,0:T(8,128)(2,1)S(1)}, u32[]{:S(2)}, u32[]{:S(2)}) collective-permute-start(bf16[18,16,256]{2,1,0:T(8,128)(2,1)S(1)} %get-tuple-element.26), channel_id=1, source_target_pairs={{0,3},{1,2},{2,1},{3,0},{4,7},{5,6},{6,5},{7,4},{8,11},{9,10},{10,... | collective-permute-start | bytes 442376 | tf_op jit(solution)/shard_map/ppermute | solution.py:16
  20.8 4.8 %collective-permute-start.8 = (bf16[18,16,256]{2,1,0:T(8,128)(2,1)S(1)}, bf16[18,16,256]{2,1,0:T(8,128)(2,1)S(1)}, u32[]{:S(2)}, u32[]{:S(2)}) collective-permute-start(bf16[18,16,256]{2,1,0:T(8,128)(2,1)S(1)} %get-tuple-element.28), channel_id=1, source_target_pairs={{0,1},{1,0},{2,3},{3,2},{4,5},{5,4},{6,7},{7,6},{8,9},{9,8},{10,11... | collective-permute-start | bytes 442376 | tf_op jit(solution)/shard_map/ppermute | solution.py:16
  21.3 7.7 %collective-permute-start.9 = (bf16[18,16,256]{2,1,0:T(8,128)(2,1)S(1)}, bf16[18,16,256]{2,1,0:T(8,128)(2,1)S(1)}, u32[]{:S(2)}, u32[]{:S(2)}) collective-permute-start(bf16[18,16,256]{2,1,0:T(8,128)(2,1)S(1)} %get-tuple-element.27), channel_id=1, source_target_pairs={{0,2},{1,3},{2,0},{3,1},{4,6},{5,7},{6,4},{7,5},{8,10},{9,11},{10,... | collective-permute-start | bytes 442376 | tf_op jit(solution)/shard_map/ppermute | solution.py:16
  29.0 12.9 %collective-permute-start.11 = (bf16[4,1,56,128]{3,2,1,0:T(8,128)(2,1)S(1)}, bf16[4,1,56,128]{3,2,1,0:T(8,128)(2,1)S(1)}, u32[]{:S(2)}, u32[]{:S(2)}) collective-permute-start(bf16[4,1,56,128]{3,2,1,0:T(8,128)(2,1)S(1)} %lay_out.3.refs_3_), channel_id=1, source_target_pairs={{0,4},{1,5},{2,6},{3,7},{4,8},{5,9},{6,10},{7,11},{8,12},{9,13},{1... | collective-permute-start | bytes 172040 | tf_op jit(solution)/shard_map/ppermute | solution.py:16
  29.0 12.9 %collective-permute-start.12 = (bf16[4,1,56,128]{3,2,1,0:T(8,128)(2,1)S(1)}, bf16[4,1,56,128]{3,2,1,0:T(8,128)(2,1)S(1)}, u32[]{:S(2)}, u32[]{:S(2)}) collective-permute-start(bf16[4,1,56,128]{3,2,1,0:T(8,128)(2,1)S(1)} %lay_out.3.refs_3_), channel_id=1, source_target_pairs={{0,12},{1,13},{2,14},{3,15},{4,0},{5,1},{6,2},{7,3},{8,4},{9,5},{1... | collective-permute-start | bytes 172040 | tf_op jit(solution)/shard_map/ppermute | solution.py:16
  33.5 14.7 %collective-permute-start.15 = (bf16[1152,256]{1,0:T(8,128)(2,1)S(1)}, bf16[1152,256]{1,0:T(8,128)(2,1)S(1)}, u32[]{:S(2)}, u32[]{:S(2)}) collective-permute-start(bf16[1152,256]{1,0:T(8,128)(2,1)S(1)} %sort_weights.1.refs_0_), channel_id=1, source_target_pairs={{0,16},{16,0},{1,17},{17,1},{2,18},{18,2},{3,19},{19,3},{4,20},{20... | collective-permute-start | bytes 1769480 | tf_op jit(solution)/shard_map/ppermute | solution.py:16
  43.0 1.7 %collective-permute-start.13 = (bf16[2,6,56,256]{3,2,1,0:T(8,128)(2,1)S(1)}, bf16[2,6,56,256]{3,2,1,0:T(8,128)(2,1)S(1)}, u32[]{:S(2)}, u32[]{:S(2)}) collective-permute-start(bf16[2,6,56,256]{3,2,1,0:T(8,128)(2,1)S(1)} %get-tuple-element.12), channel_id=1, source_target_pairs={{0,1},{1,0},{2,3},{3,2},{4,5},{5,4},{6,7},{7,6},{8,9},{9,8},{10,11... | collective-permute-start | bytes 1032200 | tf_op jit(solution)/shard_map/ppermute | solution.py:16
  44.8 6.5 %collective-permute-start.14 = (bf16[6,56,256]{2,1,0:T(8,128)(2,1)S(1)}, bf16[6,56,256]{2,1,0:T(8,128)(2,1)S(1)}, u32[]{:S(2)}, u32[]{:S(2)}) collective-permute-start(bf16[6,56,256]{2,1,0:T(8,128)(2,1)S(1)} %fusion), channel_id=1, source_target_pairs={{0,2},{1,3},{2,0},{3,1},{4,6},{5,7},{6,4},{7,5},{8,10},{9,11},{10,... | collective-permute-start | bytes 516104 | tf_op jit(solution)/shard_map/ppermute | solution.py:16
  49.3 3.2 %collective-permute-start.16 = (bf16[2,6,56,256]{3,2,1,0:T(8,128)(2,1)S(1)}, bf16[2,6,56,256]{3,2,1,0:T(8,128)(2,1)S(1)}, u32[]{:S(2)}, u32[]{:S(2)}) collective-permute-start(bf16[2,6,56,256]{3,2,1,0:T(8,128)(2,1)S(1)} %get-tuple-element.14), channel_id=1, source_target_pairs={{0,1},{1,0},{2,3},{3,2},{4,5},{5,4},{6,7},{7,6},{8,9},{9,8},{10,11... | collective-permute-start | bytes 1032200 | tf_op jit(solution)/shard_map/ppermute | solution.py:16
  52.1 2.1 %collective-permute-start.18 = (bf16[2,2,56,512]{3,2,1,0:T(8,128)(2,1)S(1)}, bf16[2,2,56,512]{3,2,1,0:T(8,128)(2,1)S(1)}, u32[]{:S(2)}, u32[]{:S(2)}) collective-permute-start(bf16[2,2,56,512]{3,2,1,0:T(8,128)(2,1)S(1)} %get-tuple-element.16), channel_id=1, source_target_pairs={{0,1},{1,0},{2,3},{3,2},{4,5},{5,4},{6,7},{7,6},{8,9},{9,8},{10,11... | collective-permute-start | bytes 688136 | tf_op jit(solution)/shard_map/ppermute | solution.py:16
  52.5 8.9 %collective-permute-start.17 = (bf16[6,56,256]{2,1,0:T(8,128)(2,1)S(1)}, bf16[6,56,256]{2,1,0:T(8,128)(2,1)S(1)}, u32[]{:S(2)}, u32[]{:S(2)}) collective-permute-start(bf16[6,56,256]{2,1,0:T(8,128)(2,1)S(1)} %fusion.1), channel_id=1, source_target_pairs={{0,2},{1,3},{2,0},{3,1},{4,6},{5,7},{6,4},{7,5},{8,10},{9,11},{10,... | collective-permute-start | bytes 516104 | tf_op jit(solution)/shard_map/ppermute | solution.py:16
  54.1 7.3 %collective-permute-start.19 = (bf16[2,56,512]{2,1,0:T(8,128)(2,1)S(1)}, bf16[2,56,512]{2,1,0:T(8,128)(2,1)S(1)}, u32[]{:S(2)}, u32[]{:S(2)}) collective-permute-start(bf16[2,56,512]{2,1,0:T(8,128)(2,1)S(1)} %fusion.2), channel_id=1, source_target_pairs={{0,2},{1,3},{2,0},{3,1},{4,6},{5,7},{6,4},{7,5},{8,10},{9,11},{10,... | collective-permute-start | bytes 344072 | tf_op jit(solution)/shard_map/ppermute | solution.py:16

commit v4 on v3

--- a/solution.py
+++ b/solution.py
@@ -8,7 +8,7 @@
 MAXS = 4
 UNIT = 16
 VMEM = 28 << 20
-WORK = 4_500_000_000
+WORK = 9_000_000_000
 
 
 def send(value, axis, target_of):
@@ -167,30 +167,60 @@
     )(convolved, *weights, *ties)
 
 
-def finish(turned, sums, width, bands):
+def gelu_of(kept, core, across):
+    def body(kept_ref, core_ref, across_ref, out_ref):
+        total = kept_ref[0] + core_ref[0].astype(jnp.float32) + across_ref[...].astype(jnp.float32)
+        out_ref[...] = jax.nn.gelu(total).astype(jnp.bfloat16)
+
+    vmem = pl.BlockSpec(memory_space=pltpu.VMEM)
+    return pl.pallas_call(
+        body,
+        in_specs=[vmem] * 3,
+        out_specs=vmem,
+        out_shape=jax.ShapeDtypeStruct(across.shape, jnp.bfloat16),
+        compiler_params=pltpu.CompilerParams(vmem_limit_bytes=VMEM),
+        name="gelu_of",
+    )(kept, core, across)
+
+
+def finish(turned, early, sums, width, bands):
     longitudes = sums[0][2].shape[2]
-
-    def body(turned_ref, *refs):
-        out_ref = refs[-1]
-        for n, (first, halves, kept, _, _) in enumerate(sums):
-            kept_ref, core_ref, across_ref = refs[3 * n : 3 * n + 3]
-            for m, half in enumerate(halves):
-                column = pl.multiple_of((turned_ref[0] ^ half) * width, width)
-                from_ = slice(m * width, (m + 1) * width)
-                for band in range(kept.shape[1]):
-                    total = kept_ref[0, band, :, from_] + core_ref[0, band, :, from_].astype(jnp.float32)
-                    total += across_ref[band, :, from_].astype(jnp.float32)
-                    out_ref[first + band, :, pl.ds(column, width)] = jax.nn.gelu(total).astype(jnp.bfloat16)
+    ready = early.shape[0]
+
+    def body(turned_ref, early_ref, *refs):
+        out_ref, held, sems = refs[-3:]
+        for band in range(bands):
+            if band < ready:
+                column = pl.multiple_of(turned_ref[0] * width, width)
+                held[band, :, pl.ds(column, width)] = early_ref[band]
+            for n, (first, halves, kept, _, _) in enumerate(sums):
+                at = band - first
+                if not 0 <= at < kept.shape[1]:
+                    continue
+                kept_ref, core_ref, across_ref = refs[3 * n : 3 * n + 3]
+                for m, half in enumerate(halves):
+                    column = pl.multiple_of((turned_ref[0] ^ half) * width, width)
+                    from_ = slice(m * width, (m + 1) * width)
+                    total = kept_ref[0, at, :, from_] + core_ref[0, at, :, from_].astype(jnp.float32)
+                    total += across_ref[at, :, from_].astype(jnp.float32)
+                    held[band, :, pl.ds(column, width)] = jax.nn.gelu(total).astype(jnp.bfloat16)
+            pltpu.make_async_copy(held.at[band], out_ref.at[band], sems.at[band]).start()
+        for band in range(bands):
+            pltpu.make_async_copy(held.at[band], out_ref.at[band], sems.at[band]).wait()
 
     vmem = pl.BlockSpec(memory_space=pltpu.VMEM)
     return pl.pallas_call(
         body,
-        in_specs=[pl.BlockSpec(memory_space=pltpu.SMEM)] + [vmem] * (3 * len(sums)),
-        out_specs=vmem,
+        in_specs=[pl.BlockSpec(memory_space=pltpu.SMEM)] + [vmem] * (1 + 3 * len(sums)),
+        out_specs=pl.BlockSpec(memory_space=pl.ANY),
         out_shape=jax.ShapeDtypeStruct((bands, longitudes, 2 * width), jnp.bfloat16),
+        scratch_shapes=[
+            pltpu.VMEM((bands, longitudes, 2 * width), jnp.bfloat16),
+            pltpu.SemaphoreType.DMA((bands,)),
+        ],
         compiler_params=pltpu.CompilerParams(vmem_limit_bytes=VMEM),
         name="finish",
-    )(turned, *(array for entry in sums for array in entry[2:]))
+    )(turned, early, *(array for entry in sums for array in entry[2:]))
 
 
 def gather_weights(mixing, filters, channels):
@@ -313,7 +343,7 @@
     core_a = over_core(sent_a)
     part_a = added(kept_a[1], core_a[1])
     across_a = over_y(part_a)
-    sums.append((cuts[0][0], (0,), kept_a, core_a, across_a))
+    early = gelu_of(kept_a, core_a, across_a)
     kept_b, sent_b = mix(conv0, every, [theirs], longitudes, [])
     core_b = over_core(sent_b)
     part_b = added(kept_b[1], core_b[1])
@@ -323,7 +353,7 @@
     kept, sent = mix(conv1, every, [ours, theirs], longitudes, [across_a])
     core = over_core(sent)
     sums.append((cuts[1][0], (0, 1), kept, core, over_y(added(kept[1], core[1]))))
-    return finish(turned.reshape(1).astype(jnp.int32), sums, ours.shape[1], bands)
+    return finish(turned.reshape(1).astype(jnp.int32), early, sums, ours.shape[1], bands)
 
 
 def solution(mesh):

time: 62.9 us -> 62.7 us (level)
  no operation moved by 1% of the time
where the time goes in v4:
time: 62.7 us; the launch traced here: 62.5 us
  starting transfers between devices  24.5 us (39%)
  waiting for transfers between devices  21.2 us (34%)
  Pallas kernels  11.8 us (19%)
  local copies, waits for them, and re-layouts  2.38 us (4%)
  other arithmetic  2.34 us (4%)
    ppermute x20, starting transfers between devices, send(): return lax.ppermute(value, axis, [(s, target_of(s)) for s in range(count)])  24.5 us
    ppermute x20, waiting for transfers between devices, send(): return lax.ppermute(value, axis, [(s, target_of(s)) for s in range(count)])  21.2 us
    pallas_call x2, Pallas kernels, convolve(): pl.pallas_call(body, in_specs=[pl.BlockSpec(memory_space=pltpu.SMEM)] + [...  7.17 us
    pallas_call x3, Pallas kernels, mix(): pl.pallas_call(body, in_specs=[vmem] * (1 + len(weights)) + [pl.BlockSpec...  2.88 us
  transfers between devices with their start and end apart: 20, of which 10 were waited for; matrix products, arithmetic and copies ran while one was open for 6% of the time, Pallas kernels for 17%

profile of v4, /device:TPU:0, one launch (start us, length us, event | category | flops | bytes accessed | tf_op | source)
XLA Modules:
  0.0 62.5 jit_solution(4915731088768517322)
XLA Ops:
  1.0 4.1 %collective-permute-start.5 = (bf16[288,256]{1,0:T(8,128)(2,1)S(1)}, bf16[288,256]{1,0:T(8,128)(2,1)S(1)}, u32[]{:S(2)}, u32[]{:S(2)}) collective-permute-start(bf16[288,256]{1,0:T(8,128)(2,1)S(1)} %constant_dynamic-slice_fusion), channel_id=1, source_target_pairs={{0,8},{1,9},{2,10},{3,11},{4,12},{5,13},{6,14},{7,15},{8,0},{9,1},... | collective-permute-start | bytes 442376 | tf_op jit(solution)/shard_map/ppermute | solution.py:16
  5.1 1.6 %collective-permute-start.7 = (bf16[288,256]{1,0:T(8,128)(2,1)S(1)}, bf16[288,256]{1,0:T(8,128)(2,1)S(1)}, u32[]{:S(2)}, u32[]{:S(2)}) collective-permute-start(bf16[288,256]{1,0:T(8,128)(2,1)S(1)} %constant_dynamic-slice_fusion), channel_id=1, source_target_pairs={{0,4},{1,5},{2,6},{3,7},{4,0},{5,1},{6,2},{7,3},{8,12},{9,13},{10,... | collective-permute-start | bytes 442376 | tf_op jit(solution)/shard_map/ppermute | solution.py:16
  6.7 1.1 %constant_dynamic-slice_fusion.1 = (bf16[8,56,128]{2,1,0:T(8,128)(2,1)S(1)}, bf16[8,56,128]{2,1,0:T(8,128)(2,1)S(1)}, bf16[8,56,128]{2,1,0:T(8,128)(2,1)S(1)}, bf16[8,56,128]{2,1,0:T(8,128)(2,1)S(1)}) fusion(bf16[8,56,512]{2,1,0:T(8,128)(2,1)} %param.4, s32[]{:T(128)S(6)} %select_n.237, s32[]{:T(128)S(6)} %select_n.235, s32[]{:T(128)S(6)} %select_n.234, ...), kind=kLoop, calls=%fused_computation.39 | loop fusion | bytes 917520 | tf_op jit(solution)/shard_map/dynamic_slice | solution.py:303
  7.9 1.6 %collective-permute-start.1 = (bf16[8,56,128]{2,1,0:T(8,128)(2,1)S(1)}, bf16[8,56,128]{2,1,0:T(8,128)(2,1)S(1)}, u32[]{:S(2)}, u32[]{:S(2)}) collective-permute-start(bf16[8,56,128]{2,1,0:T(8,128)(2,1)S(1)} %get-tuple-element.32), channel_id=1, source_target_pairs={{0,2},{1,3},{2,0},{3,1},{4,6},{5,7},{6,4},{7,5},{8,10},{9,11},{10,... | collective-permute-start | bytes 344072 | tf_op jit(solution)/shard_map/ppermute | solution.py:16
  12.8 1.0 %collective-permute-done.1.refs_2_ = bf16[8,56,128]{2,1,0:T(8,128)(2,1)S(1)} collective-permute-done((bf16[8,56,128]{2,1,0:T(8,128)(2,1)S(1)}, bf16[8,56,128]{2,1,0:T(8,128)(2,1)S(1)}, u32[]{:S(2)}, u32[]{:S(2)}) %collective-permute-start.1) | collective-permute-done | bytes 114720 | tf_op jit(solution)/shard_map/ppermute | solution.py:16
  13.9 1.6 %collective-permute-done.2.refs_3_ = bf16[8,56,128]{2,1,0:T(8,128)(2,1)S(1)} collective-permute-done((bf16[8,56,128]{2,1,0:T(8,128)(2,1)S(1)}, bf16[8,56,128]{2,1,0:T(8,128)(2,1)S(1)}, u32[]{:S(2)}, u32[]{:S(2)}) %collective-permute-start.2) | collective-permute-done | bytes 114720 | tf_op jit(solution)/shard_map/ppermute | solution.py:16
  15.9 3.4 %collective-permute-start.4 = (bf16[4,7,56,128]{3,2,1,0:T(8,128)(2,1)S(1)}, bf16[4,7,56,128]{3,2,1,0:T(8,128)(2,1)S(1)}, u32[]{:S(2)}, u32[]{:S(2)}) collective-permute-start(bf16[4,7,56,128]{3,2,1,0:T(8,128)(2,1)S(1)} %lay_out.2.refs_1_.refs_2_), channel_id=1, source_target_pairs={{0,12},{1,13},{2,14},{3,15},{4,0},{5,1},{6,2},{7,3},{8,4},{9,5},{1... | collective-permute-start | bytes 1204232 | tf_op jit(solution)/shard_map/ppermute | solution.py:16
  19.6 1.2 %collective-permute-start.10 = (bf16[18,16,256]{2,1,0:T(8,128)(2,1)S(1)}, bf16[18,16,256]{2,1,0:T(8,128)(2,1)S(1)}, u32[]{:S(2)}, u32[]{:S(2)}) collective-permute-start(bf16[18,16,256]{2,1,0:T(8,128)(2,1)S(1)} %get-tuple-element.26), channel_id=1, source_target_pairs={{0,3},{1,2},{2,1},{3,0},{4,7},{5,6},{6,5},{7,4},{8,11},{9,10},{10,... | collective-permute-start | bytes 442376 | tf_op jit(solution)/shard_map/ppermute | solution.py:16
  22.1 3.5 %collective-permute-done.10.refs_6_ = bf16[18,16,256]{2,1,0:T(8,128)(2,1)S(1)} collective-permute-done((bf16[18,16,256]{2,1,0:T(8,128)(2,1)S(1)}, bf16[18,16,256]{2,1,0:T(8,128)(2,1)S(1)}, u32[]{:S(2)}, u32[]{:S(2)}) %collective-permute-start.10) | collective-permute-done | bytes 147488 | tf_op jit(solution)/shard_map/ppermute | solution.py:16
  25.7 3.3 %collective-permute-done.9.refs_5_ = bf16[18,16,256]{2,1,0:T(8,128)(2,1)S(1)} collective-permute-done((bf16[18,16,256]{2,1,0:T(8,128)(2,1)S(1)}, bf16[18,16,256]{2,1,0:T(8,128)(2,1)S(1)}, u32[]{:S(2)}, u32[]{:S(2)}) %collective-permute-start.9) | collective-permute-done | bytes 147488 | tf_op jit(solution)/shard_map/ppermute | solution.py:16
  29.0 3.8 %collective-permute-start.12 = (bf16[4,1,56,128]{3,2,1,0:T(8,128)(2,1)S(1)}, bf16[4,1,56,128]{3,2,1,0:T(8,128)(2,1)S(1)}, u32[]{:S(2)}, u32[]{:S(2)}) collective-permute-start(bf16[4,1,56,128]{3,2,1,0:T(8,128)(2,1)S(1)} %lay_out.3.refs_3_), channel_id=1, source_target_pairs={{0,12},{1,13},{2,14},{3,15},{4,0},{5,1},{6,2},{7,3},{8,4},{9,5},{1... | collective-permute-start | bytes 172040 | tf_op jit(solution)/shard_map/ppermute | solution.py:16
  33.5 1.6 %collective-permute-start.15 = (bf16[1152,256]{1,0:T(8,128)(2,1)S(1)}, bf16[1152,256]{1,0:T(8,128)(2,1)S(1)}, u32[]{:S(2)}, u32[]{:S(2)}) collective-permute-start(bf16[1152,256]{1,0:T(8,128)(2,1)S(1)} %sort_weights.1.refs_0_), channel_id=1, source_target_pairs={{0,16},{16,0},{1,17},{17,1},{2,18},{18,2},{3,19},{19,3},{4,20},{20... | collective-permute-start | bytes 1769480 | tf_op jit(solution)/shard_map/ppermute | solution.py:16
  35.1 1.5 %collective-permute-done.4.refs_2_.refs_4_ = bf16[4,7,56,128]{3,2,1,0:T(8,128)(2,1)S(1)} collective-permute-done((bf16[4,7,56,128]{3,2,1,0:T(8,128)(2,1)S(1)}, bf16[4,7,56,128]{3,2,1,0:T(8,128)(2,1)S(1)}, u32[]{:S(2)}, u32[]{:S(2)}) %collective-permute-start.4) | collective-permute-done | bytes 401440 | tf_op jit(solution)/shard_map/ppermute | solution.py:16
  36.5 5.4 %convolve.2.conv_ref = bf16[1344,1152]{1,0:T(8,128)(2,1)S(1)} custom-call(s32[1]{0:T(128)} %bitcast.1.place_ref, f32[6,9,1536]{2,1,0:T(8,128)S(1)} %copy.7.packed_ref, bf16[4,7,56,128]{3,2,1,0:T(8,128)(2,1)S(1)} %collective-permute-done.3.refs_0_, bf16[4,7,56,128]{3,2,1,0:T(8,128)(2,1)S(1)} %lay_out.2.refs_1_.refs_2_, ...), custom_call_target="tpu_custom_call" | custom-call | flops 8999999488 | bytes 1 | tf_op jit(solution)/shard_map/convolve/pallas_call | solution.py:118
  42.0 1.1 %mix.3 = (f32[2,6,56,256]{3,2,1,0:T(8,128)S(1)}, bf16[2,6,56,256]{3,2,1,0:T(8,128)(2,1)S(1)}) custom-call(bf16[1344,1152]{1,0:T(8,128)(2,1)S(1)} %convolve.2.conv_ref, bf16[1152,256]{1,0:T(8,128)(2,1)S(1)} %sort_weights.1.refs_0_, bf16[4,1,56,128]{3,2,1,0:T(8,128)(2,1)S(1)} %collective-permute-done.11.refs_1_, ...), custom_call_target="tpu_custom_call" | custom-call | tf_op jit(solution)/shard_map/mix/pallas_call | solution.py:160
  43.2 1.5 %collective-permute-done.13.core_ref = bf16[2,6,56,256]{3,2,1,0:T(8,128)(2,1)S(1)} collective-permute-done((bf16[2,6,56,256]{3,2,1,0:T(8,128)(2,1)S(1)}, bf16[2,6,56,256]{3,2,1,0:T(8,128)(2,1)S(1)}, u32[]{:S(2)}, u32[]{:S(2)}) %collective-permute-start.13) | collective-permute-done | bytes 344096 | tf_op jit(solution)/shard_map/ppermute | solution.py:16
  44.8 1.6 %collective-permute-start.14 = (bf16[6,56,256]{2,1,0:T(8,128)(2,1)S(1)}, bf16[6,56,256]{2,1,0:T(8,128)(2,1)S(1)}, u32[]{:S(2)}, u32[]{:S(2)}) collective-permute-start(bf16[6,56,256]{2,1,0:T(8,128)(2,1)S(1)} %fusion), channel_id=1, source_target_pairs={{0,2},{1,3},{2,0},{3,1},{4,6},{5,7},{6,4},{7,5},{8,10},{9,11},{10,... | collective-permute-start | bytes 516104 | tf_op jit(solution)/shard_map/ppermute | solution.py:16
  46.4 1.8 %collective-permute-done.15.refs_0_.refs_1_ = bf16[1152,256]{1,0:T(8,128)(2,1)S(1)} collective-permute-done((bf16[1152,256]{1,0:T(8,128)(2,1)S(1)}, bf16[1152,256]{1,0:T(8,128)(2,1)S(1)}, u32[]{:S(2)}, u32[]{:S(2)}) %collective-permute-start.15) | collective-permute-done | bytes 589856 | tf_op jit(solution)/shard_map/ppermute | solution.py:16
  48.2 1.1 %mix.4 = (f32[2,6,56,256]{3,2,1,0:T(8,128)S(1)}, bf16[2,6,56,256]{3,2,1,0:T(8,128)(2,1)S(1)}) custom-call(bf16[1344,1152]{1,0:T(8,128)(2,1)S(1)} %convolve.2.conv_ref, bf16[1152,256]{1,0:T(8,128)(2,1)S(1)} %collective-permute-done.15.refs_0_.refs_1_), custom_call_target="tpu_custom_call" | custom-call | tf_op jit(solution)/shard_map/mix/pallas_call | solution.py:160
  49.3 1.8 %convolve.3.conv_ref = bf16[448,1152]{1,0:T(8,128)(2,1)S(1)} custom-call(s32[1]{0:T(128)} %bitcast.1.place_ref, f32[2,9,1536]{2,1,0:T(8,128)S(1)} %copy.8.packed_ref, bf16[4,7,56,128]{3,2,1,0:T(8,128)(2,1)S(1)} %collective-permute-done.3.refs_0_, bf16[4,1,56,128]{3,2,1,0:T(8,128)(2,1)S(1)} %collective-permute-done.11.refs_1_, ...), custom_call_target="tpu_custom_call" | custom-call | flops 8999999488 | bytes 1 | tf_op jit(solution)/shard_map/convolve/pallas_call | solution.py:118
  52.5 1.6 %collective-permute-start.17 = (bf16[6,56,256]{2,1,0:T(8,128)(2,1)S(1)}, bf16[6,56,256]{2,1,0:T(8,128)(2,1)S(1)}, u32[]{:S(2)}, u32[]{:S(2)}) collective-permute-start(bf16[6,56,256]{2,1,0:T(8,128)(2,1)S(1)} %fusion.1), channel_id=1, source_target_pairs={{0,2},{1,3},{2,0},{3,1},{4,6},{5,7},{6,4},{7,5},{8,10},{9,11},{10,... | collective-permute-start | bytes 516104 | tf_op jit(solution)/shard_map/ppermute | solution.py:16
  54.1 1.1 %collective-permute-start.19 = (bf16[2,56,512]{2,1,0:T(8,128)(2,1)S(1)}, bf16[2,56,512]{2,1,0:T(8,128)(2,1)S(1)}, u32[]{:S(2)}, u32[]{:S(2)}) collective-permute-start(bf16[2,56,512]{2,1,0:T(8,128)(2,1)S(1)} %fusion.2), channel_id=1, source_target_pairs={{0,2},{1,3},{2,0},{3,1},{4,6},{5,7},{6,4},{7,5},{8,10},{9,11},{10,... | collective-permute-start | bytes 344072 | tf_op jit(solution)/shard_map/ppermute | solution.py:16
  55.4 6.1 %collective-permute-done.19.refs_5_ = bf16[2,56,512]{2,1,0:T(8,128)(2,1)S(1)} collective-permute-done((bf16[2,56,512]{2,1,0:T(8,128)(2,1)S(1)}, bf16[2,56,512]{2,1,0:T(8,128)(2,1)S(1)}, u32[]{:S(2)}, u32[]{:S(2)}) %collective-permute-start.19) | collective-permute-done | bytes 114720 | tf_op jit(solution)/shard_map/ppermute | solution.py:16
  61.5 1.0 %finish.1 = bf16[8,56,512]{2,1,0:T(8,128)(2,1)} custom-call(s32[1]{0:T(128)} %bitcast.turned_ref, bf16[6,56,256]{2,1,0:T(8,128)(2,1)S(1)} %gelu_of.1.early_ref, f32[2,6,56,256]{3,2,1,0:T(8,128)S(1)} %get-tuple-element.13.refs_0_, bf16[2,6,56,256]{3,2,1,0:T(8,128)(2,1)S(1)} %collective-permute-done.16.refs_1_, ...), custom_call_target="tpu_custom_call" | custom-call | tf_op jit(solution)/shard_map/finish/pallas_call | solution.py:212
  (50 shorter events, 9.1 us)
Async XLA Ops:
  0.0 1.0 %copy-start = (bf16[288,512]{1,0:T(8,128)(2,1)S(1)}, bf16[288,512]{1,0:T(8,128)(2,1)}, u32[]{:S(2)}) copy-start(bf16[288,512]{1,0:T(8,128)(2,1)} %param.7) | copy-start | bytes 884740
  1.0 11.2 %collective-permute-start.5 = (bf16[288,256]{1,0:T(8,128)(2,1)S(1)}, bf16[288,256]{1,0:T(8,128)(2,1)S(1)}, u32[]{:S(2)}, u32[]{:S(2)}) collective-permute-start(bf16[288,256]{1,0:T(8,128)(2,1)S(1)} %constant_dynamic-slice_fusion), channel_id=1, source_target_pairs={{0,8},{1,9},{2,10},{3,11},{4,12},{5,13},{6,14},{7,15},{8,0},{9,1},... | collective-permute-start | bytes 442376 | tf_op jit(solution)/shard_map/ppermute | solution.py:16
  5.1 14.2 %collective-permute-start.7 = (bf16[288,256]{1,0:T(8,128)(2,1)S(1)}, bf16[288,256]{1,0:T(8,128)(2,1)S(1)}, u32[]{:S(2)}, u32[]{:S(2)}) collective-permute-start(bf16[288,256]{1,0:T(8,128)(2,1)S(1)} %constant_dynamic-slice_fusion), channel_id=1, source_target_pairs={{0,4},{1,5},{2,6},{3,7},{4,0},{5,1},{6,2},{7,3},{8,12},{9,13},{10,... | collective-permute-start | bytes 442376 | tf_op jit(solution)/shard_map/ppermute | solution.py:16
  7.8 5.0 %collective-permute-start = (bf16[8,56,128]{2,1,0:T(8,128)(2,1)S(1)}, bf16[8,56,128]{2,1,0:T(8,128)(2,1)S(1)}, u32[]{:S(2)}, u32[]{:S(2)}) collective-permute-start(bf16[8,56,128]{2,1,0:T(8,128)(2,1)S(1)} %get-tuple-element.30), channel_id=1, source_target_pairs={{0,1},{1,0},{2,3},{3,2},{4,5},{5,4},{6,7},{7,6},{8,9},{9,8},{10,11... | collective-permute-start | bytes 344072 | tf_op jit(solution)/shard_map/ppermute | solution.py:16
  7.9 6.0 %collective-permute-start.1 = (bf16[8,56,128]{2,1,0:T(8,128)(2,1)S(1)}, bf16[8,56,128]{2,1,0:T(8,128)(2,1)S(1)}, u32[]{:S(2)}, u32[]{:S(2)}) collective-permute-start(bf16[8,56,128]{2,1,0:T(8,128)(2,1)S(1)} %get-tuple-element.32), channel_id=1, source_target_pairs={{0,2},{1,3},{2,0},{3,1},{4,6},{5,7},{6,4},{7,5},{8,10},{9,11},{10,... | collective-permute-start | bytes 344072 | tf_op jit(solution)/shard_map/ppermute | solution.py:16
  9.4 6.0 %collective-permute-start.2 = (bf16[8,56,128]{2,1,0:T(8,128)(2,1)S(1)}, bf16[8,56,128]{2,1,0:T(8,128)(2,1)S(1)}, u32[]{:S(2)}, u32[]{:S(2)}) collective-permute-start(bf16[8,56,128]{2,1,0:T(8,128)(2,1)S(1)} %get-tuple-element.29), channel_id=1, source_target_pairs={{0,3},{1,2},{2,1},{3,0},{4,7},{5,6},{6,5},{7,4},{8,11},{9,10},{10,... | collective-permute-start | bytes 344072 | tf_op jit(solution)/shard_map/ppermute | solution.py:16
  12.2 7.1 %collective-permute-start.6 = (bf16[288,256]{1,0:T(8,128)(2,1)S(1)}, bf16[288,256]{1,0:T(8,128)(2,1)S(1)}, u32[]{:S(2)}, u32[]{:S(2)}) collective-permute-start(bf16[288,256]{1,0:T(8,128)(2,1)S(1)} %collective-permute-done.5), channel_id=1, source_target_pairs={{0,4},{1,5},{2,6},{3,7},{4,0},{5,1},{6,2},{7,3},{8,12},{9,13},{10,... | collective-permute-start | bytes 442376 | tf_op jit(solution)/shard_map/ppermute | solution.py:16
  15.4 19.6 %collective-permute-start.3 = (bf16[4,7,56,128]{3,2,1,0:T(8,128)(2,1)S(1)}, bf16[4,7,56,128]{3,2,1,0:T(8,128)(2,1)S(1)}, u32[]{:S(2)}, u32[]{:S(2)}) collective-permute-start(bf16[4,7,56,128]{3,2,1,0:T(8,128)(2,1)S(1)} %lay_out.2.refs_1_.refs_2_), channel_id=1, source_target_pairs={{0,4},{1,5},{2,6},{3,7},{4,8},{5,9},{6,10},{7,11},{8,12},{9,13},{1... | collective-permute-start | bytes 1204232 | tf_op jit(solution)/shard_map/ppermute | solution.py:16
  15.9 20.6 %collective-permute-start.4 = (bf16[4,7,56,128]{3,2,1,0:T(8,128)(2,1)S(1)}, bf16[4,7,56,128]{3,2,1,0:T(8,128)(2,1)S(1)}, u32[]{:S(2)}, u32[]{:S(2)}) collective-permute-start(bf16[4,7,56,128]{3,2,1,0:T(8,128)(2,1)S(1)} %lay_out.2.refs_1_.refs_2_), channel_id=1, source_target_pairs={{0,12},{1,13},{2,14},{3,15},{4,0},{5,1},{6,2},{7,3},{8,4},{9,5},{1... | collective-permute-start | bytes 1204232 | tf_op jit(solution)/shard_map/ppermute | solution.py:16
  19.6 6.0 %collective-permute-start.10 = (bf16[18,16,256]{2,1,0:T(8,128)(2,1)S(1)}, bf16[18,16,256]{2,1,0:T(8,128)(2,1)S(1)}, u32[]{:S(2)}, u32[]{:S(2)}) collective-permute-start(bf16[18,16,256]{2,1,0:T(8,128)(2,1)S(1)} %get-tuple-element.26), channel_id=1, source_target_pairs={{0,3},{1,2},{2,1},{3,0},{4,7},{5,6},{6,5},{7,4},{8,11},{9,10},{10,... | collective-permute-start | bytes 442376 | tf_op jit(solution)/shard_map/ppermute | solution.py:16
  20.8 4.8 %collective-permute-start.8 = (bf16[18,16,256]{2,1,0:T(8,128)(2,1)S(1)}, bf16[18,16,256]{2,1,0:T(8,128)(2,1)S(1)}, u32[]{:S(2)}, u32[]{:S(2)}) collective-permute-start(bf16[18,16,256]{2,1,0:T(8,128)(2,1)S(1)} %get-tuple-element.28), channel_id=1, source_target_pairs={{0,1},{1,0},{2,3},{3,2},{4,5},{5,4},{6,7},{7,6},{8,9},{9,8},{10,11... | collective-permute-start | bytes 442376 | tf_op jit(solution)/shard_map/ppermute | solution.py:16
  21.3 7.7 %collective-permute-start.9 = (bf16[18,16,256]{2,1,0:T(8,128)(2,1)S(1)}, bf16[18,16,256]{2,1,0:T(8,128)(2,1)S(1)}, u32[]{:S(2)}, u32[]{:S(2)}) collective-permute-start(bf16[18,16,256]{2,1,0:T(8,128)(2,1)S(1)} %get-tuple-element.27), channel_id=1, source_target_pairs={{0,2},{1,3},{2,0},{3,1},{4,6},{5,7},{6,4},{7,5},{8,10},{9,11},{10,... | collective-permute-start | bytes 442376 | tf_op jit(solution)/shard_map/ppermute | solution.py:16
  29.0 12.9 %collective-permute-start.11 = (bf16[4,1,56,128]{3,2,1,0:T(8,128)(2,1)S(1)}, bf16[4,1,56,128]{3,2,1,0:T(8,128)(2,1)S(1)}, u32[]{:S(2)}, u32[]{:S(2)}) collective-permute-start(bf16[4,1,56,128]{3,2,1,0:T(8,128)(2,1)S(1)} %lay_out.3.refs_3_), channel_id=1, source_target_pairs={{0,4},{1,5},{2,6},{3,7},{4,8},{5,9},{6,10},{7,11},{8,12},{9,13},{1... | collective-permute-start | bytes 172040 | tf_op jit(solution)/shard_map/ppermute | solution.py:16
  29.0 12.9 %collective-permute-start.12 = (bf16[4,1,56,128]{3,2,1,0:T(8,128)(2,1)S(1)}, bf16[4,1,56,128]{3,2,1,0:T(8,128)(2,1)S(1)}, u32[]{:S(2)}, u32[]{:S(2)}) collective-permute-start(bf16[4,1,56,128]{3,2,1,0:T(8,128)(2,1)S(1)} %lay_out.3.refs_3_), channel_id=1, source_target_pairs={{0,12},{1,13},{2,14},{3,15},{4,0},{5,1},{6,2},{7,3},{8,4},{9,5},{1... | collective-permute-start | bytes 172040 | tf_op jit(solution)/shard_map/ppermute | solution.py:16
  33.5 14.7 %collective-permute-start.15 = (bf16[1152,256]{1,0:T(8,128)(2,1)S(1)}, bf16[1152,256]{1,0:T(8,128)(2,1)S(1)}, u32[]{:S(2)}, u32[]{:S(2)}) collective-permute-start(bf16[1152,256]{1,0:T(8,128)(2,1)S(1)} %sort_weights.1.refs_0_), channel_id=1, source_target_pairs={{0,16},{16,0},{1,17},{17,1},{2,18},{18,2},{3,19},{19,3},{4,20},{20... | collective-permute-start | bytes 1769480 | tf_op jit(solution)/shard_map/ppermute | solution.py:16
  43.0 1.7 %collective-permute-start.13 = (bf16[2,6,56,256]{3,2,1,0:T(8,128)(2,1)S(1)}, bf16[2,6,56,256]{3,2,1,0:T(8,128)(2,1)S(1)}, u32[]{:S(2)}, u32[]{:S(2)}) collective-permute-start(bf16[2,6,56,256]{3,2,1,0:T(8,128)(2,1)S(1)} %get-tuple-element.12), channel_id=1, source_target_pairs={{0,1},{1,0},{2,3},{3,2},{4,5},{5,4},{6,7},{7,6},{8,9},{9,8},{10,11... | collective-permute-start | bytes 1032200 | tf_op jit(solution)/shard_map/ppermute | solution.py:16
  44.8 6.5 %collective-permute-start.14 = (bf16[6,56,256]{2,1,0:T(8,128)(2,1)S(1)}, bf16[6,56,256]{2,1,0:T(8,128)(2,1)S(1)}, u32[]{:S(2)}, u32[]{:S(2)}) collective-permute-start(bf16[6,56,256]{2,1,0:T(8,128)(2,1)S(1)} %fusion), channel_id=1, source_target_pairs={{0,2},{1,3},{2,0},{3,1},{4,6},{5,7},{6,4},{7,5},{8,10},{9,11},{10,... | collective-permute-start | bytes 516104 | tf_op jit(solution)/shard_map/ppermute | solution.py:16
  49.3 3.2 %collective-permute-start.16 = (bf16[2,6,56,256]{3,2,1,0:T(8,128)(2,1)S(1)}, bf16[2,6,56,256]{3,2,1,0:T(8,128)(2,1)S(1)}, u32[]{:S(2)}, u32[]{:S(2)}) collective-permute-start(bf16[2,6,56,256]{3,2,1,0:T(8,128)(2,1)S(1)} %get-tuple-element.14), channel_id=1, source_target_pairs={{0,1},{1,0},{2,3},{3,2},{4,5},{5,4},{6,7},{7,6},{8,9},{9,8},{10,11... | collective-permute-start | bytes 1032200 | tf_op jit(solution)/shard_map/ppermute | solution.py:16
  52.1 2.1 %collective-permute-start.18 = (bf16[2,2,56,512]{3,2,1,0:T(8,128)(2,1)S(1)}, bf16[2,2,56,512]{3,2,1,0:T(8,128)(2,1)S(1)}, u32[]{:S(2)}, u32[]{:S(2)}) collective-permute-start(bf16[2,2,56,512]{3,2,1,0:T(8,128)(2,1)S(1)} %get-tuple-element.16), channel_id=1, source_target_pairs={{0,1},{1,0},{2,3},{3,2},{4,5},{5,4},{6,7},{7,6},{8,9},{9,8},{10,11... | collective-permute-start | bytes 688136 | tf_op jit(solution)/shard_map/ppermute | solution.py:16
  52.5 8.9 %collective-permute-start.17 = (bf16[6,56,256]{2,1,0:T(8,128)(2,1)S(1)}, bf16[6,56,256]{2,1,0:T(8,128)(2,1)S(1)}, u32[]{:S(2)}, u32[]{:S(2)}) collective-permute-start(bf16[6,56,256]{2,1,0:T(8,128)(2,1)S(1)} %fusion.1), channel_id=1, source_target_pairs={{0,2},{1,3},{2,0},{3,1},{4,6},{5,7},{6,4},{7,5},{8,10},{9,11},{10,... | collective-permute-start | bytes 516104 | tf_op jit(solution)/shard_map/ppermute | solution.py:16
  54.1 7.3 %collective-permute-start.19 = (bf16[2,56,512]{2,1,0:T(8,128)(2,1)S(1)}, bf16[2,56,512]{2,1,0:T(8,128)(2,1)S(1)}, u32[]{:S(2)}, u32[]{:S(2)}) collective-permute-start(bf16[2,56,512]{2,1,0:T(8,128)(2,1)S(1)} %fusion.2), channel_id=1, source_target_pairs={{0,2},{1,3},{2,0},{3,1},{4,6},{5,7},{6,4},{7,5},{8,10},{9,11},{10,... | collective-permute-start | bytes 344072 | tf_op jit(solution)/shard_map/ppermute | solution.py:16

commit v5 on v4

--- a/solution.py
+++ b/solution.py
@@ -185,14 +185,16 @@
 
 def finish(turned, early, sums, width, bands):
     longitudes = sums[0][2].shape[2]
-    ready = early.shape[0]
-
-    def body(turned_ref, early_ref, *refs):
+    ready = early[0].shape[0]
+
+    def body(turned_ref, *refs):
+        early_refs, refs = refs[: len(early)], refs[len(early) :]
         out_ref, held, sems = refs[-3:]
         for band in range(bands):
             if band < ready:
-                column = pl.multiple_of(turned_ref[0] * width, width)
-                held[band, :, pl.ds(column, width)] = early_ref[band]
+                for half, early_ref in enumerate(early_refs):
+                    column = pl.multiple_of((turned_ref[0] ^ half) * width, width)
+                    held[band, :, pl.ds(column, width)] = early_ref[band]
             for n, (first, halves, kept, _, _) in enumerate(sums):
                 at = band - first
                 if not 0 <= at < kept.shape[1]:
@@ -211,7 +213,7 @@
     vmem = pl.BlockSpec(memory_space=pltpu.VMEM)
     return pl.pallas_call(
         body,
-        in_specs=[pl.BlockSpec(memory_space=pltpu.SMEM)] + [vmem] * (1 + 3 * len(sums)),
+        in_specs=[pl.BlockSpec(memory_space=pltpu.SMEM)] + [vmem] * (len(early) + 3 * len(sums)),
         out_specs=pl.BlockSpec(memory_space=pl.ANY),
         out_shape=jax.ShapeDtypeStruct((bands, longitudes, 2 * width), jnp.bfloat16),
         scratch_shapes=[
@@ -220,7 +222,7 @@
         ],
         compiler_params=pltpu.CompilerParams(vmem_limit_bytes=VMEM),
         name="finish",
-    )(turned, early, *(array for entry in sums for array in entry[2:]))
+    )(turned, *early, *(array for entry in sums for array in entry[2:]))
 
 
 def gather_weights(mixing, filters, channels):
@@ -343,12 +345,12 @@
     core_a = over_core(sent_a)
     part_a = added(kept_a[1], core_a[1])
     across_a = over_y(part_a)
-    early = gelu_of(kept_a, core_a, across_a)
+    early = [gelu_of(kept_a, core_a, across_a)]
     kept_b, sent_b = mix(conv0, every, [theirs], longitudes, [])
     core_b = over_core(sent_b)
     part_b = added(kept_b[1], core_b[1])
     across_b = over_y(part_b)
-    sums.append((cuts[0][0], (1,), kept_b, core_b, across_b))
+    early.append(gelu_of(kept_b, core_b, across_b))
     conv1 = convolved(1, every, [])
     kept, sent = mix(conv1, every, [ours, theirs], longitudes, [across_a])
     core = over_core(sent)

time: 62.7 us -> 62.5 us (level)
  transfers between devices with their start and end apart: 20 -> 20, of which waited for: 10 -> 11; matrix products, arithmetic and copies ran while one was open for 6% -> 6% of each run, Pallas kernels for 17% -> 18%
where the time goes in v5:
time: 62.5 us; the launch traced here: 62.3 us
  starting transfers between devices  24.5 us (39%)
  waiting for transfers between devices  21 us (34%)
  Pallas kernels  11.9 us (19%)
  local copies, waits for them, and re-layouts  2.38 us (4%)
  other arithmetic  2.34 us (4%)
    ppermute x20, starting transfers between devices, send(): return lax.ppermute(value, axis, [(s, target_of(s)) for s in range(count)])  24.5 us
    ppermute x20, waiting for transfers between devices, send(): return lax.ppermute(value, axis, [(s, target_of(s)) for s in range(count)])  21 us
    pallas_call x2, Pallas kernels, convolve(): pl.pallas_call(body, in_specs=[pl.BlockSpec(memory_space=pltpu.SMEM)] + [...  7.17 us
    pallas_call x3, Pallas kernels, mix(): pl.pallas_call(body, in_specs=[vmem] * (1 + len(weights)) + [pl.BlockSpec...  2.88 us
  transfers between devices with their start and end apart: 20, of which 11 were waited for; matrix products, arithmetic and copies ran while one was open for 6% of the time, Pallas kernels for 18%

profile of v5, /device:TPU:0, one launch (start us, length us, event | category | flops | bytes accessed | tf_op | source)
XLA Modules:
  0.0 62.3 jit_solution(13754680380385296741)
XLA Ops:
  1.0 4.1 %collective-permute-start.5 = (bf16[288,256]{1,0:T(8,128)(2,1)S(1)}, bf16[288,256]{1,0:T(8,128)(2,1)S(1)}, u32[]{:S(2)}, u32[]{:S(2)}) collective-permute-start(bf16[288,256]{1,0:T(8,128)(2,1)S(1)} %constant_dynamic-slice_fusion), channel_id=1, source_target_pairs={{0,8},{1,9},{2,10},{3,11},{4,12},{5,13},{6,14},{7,15},{8,0},{9,1},... | collective-permute-start | bytes 442376 | tf_op jit(solution)/shard_map/ppermute | solution.py:16
  5.1 1.6 %collective-permute-start.7 = (bf16[288,256]{1,0:T(8,128)(2,1)S(1)}, bf16[288,256]{1,0:T(8,128)(2,1)S(1)}, u32[]{:S(2)}, u32[]{:S(2)}) collective-permute-start(bf16[288,256]{1,0:T(8,128)(2,1)S(1)} %constant_dynamic-slice_fusion), channel_id=1, source_target_pairs={{0,4},{1,5},{2,6},{3,7},{4,0},{5,1},{6,2},{7,3},{8,12},{9,13},{10,... | collective-permute-start | bytes 442376 | tf_op jit(solution)/shard_map/ppermute | solution.py:16
  6.7 1.1 %constant_dynamic-slice_fusion.1 = (bf16[8,56,128]{2,1,0:T(8,128)(2,1)S(1)}, bf16[8,56,128]{2,1,0:T(8,128)(2,1)S(1)}, bf16[8,56,128]{2,1,0:T(8,128)(2,1)S(1)}, bf16[8,56,128]{2,1,0:T(8,128)(2,1)S(1)}) fusion(bf16[8,56,512]{2,1,0:T(8,128)(2,1)} %param.4, s32[]{:T(128)S(6)} %select_n.237, s32[]{:T(128)S(6)} %select_n.235, s32[]{:T(128)S(6)} %select_n.234, ...), kind=kLoop, calls=%fused_computation.39 | loop fusion | bytes 917520 | tf_op jit(solution)/shard_map/dynamic_slice | solution.py:305
  7.9 1.6 %collective-permute-start.1 = (bf16[8,56,128]{2,1,0:T(8,128)(2,1)S(1)}, bf16[8,56,128]{2,1,0:T(8,128)(2,1)S(1)}, u32[]{:S(2)}, u32[]{:S(2)}) collective-permute-start(bf16[8,56,128]{2,1,0:T(8,128)(2,1)S(1)} %get-tuple-element.32), channel_id=1, source_target_pairs={{0,2},{1,3},{2,0},{3,1},{4,6},{5,7},{6,4},{7,5},{8,10},{9,11},{10,... | collective-permute-start | bytes 344072 | tf_op jit(solution)/shard_map/ppermute | solution.py:16
  12.8 1.0 %collective-permute-done.1.refs_2_ = bf16[8,56,128]{2,1,0:T(8,128)(2,1)S(1)} collective-permute-done((bf16[8,56,128]{2,1,0:T(8,128)(2,1)S(1)}, bf16[8,56,128]{2,1,0:T(8,128)(2,1)S(1)}, u32[]{:S(2)}, u32[]{:S(2)}) %collective-permute-start.1) | collective-permute-done | bytes 114720 | tf_op jit(solution)/shard_map/ppermute | solution.py:16
  13.9 1.6 %collective-permute-done.2.refs_3_ = bf16[8,56,128]{2,1,0:T(8,128)(2,1)S(1)} collective-permute-done((bf16[8,56,128]{2,1,0:T(8,128)(2,1)S(1)}, bf16[8,56,128]{2,1,0:T(8,128)(2,1)S(1)}, u32[]{:S(2)}, u32[]{:S(2)}) %collective-permute-start.2) | collective-permute-done | bytes 114720 | tf_op jit(solution)/shard_map/ppermute | solution.py:16
  15.9 3.4 %collective-permute-start.4 = (bf16[4,7,56,128]{3,2,1,0:T(8,128)(2,1)S(1)}, bf16[4,7,56,128]{3,2,1,0:T(8,128)(2,1)S(1)}, u32[]{:S(2)}, u32[]{:S(2)}) collective-permute-start(bf16[4,7,56,128]{3,2,1,0:T(8,128)(2,1)S(1)} %lay_out.2.refs_1_.refs_2_), channel_id=1, source_target_pairs={{0,12},{1,13},{2,14},{3,15},{4,0},{5,1},{6,2},{7,3},{8,4},{9,5},{1... | collective-permute-start | bytes 1204232 | tf_op jit(solution)/shard_map/ppermute | solution.py:16
  19.6 1.2 %collective-permute-start.10 = (bf16[18,16,256]{2,1,0:T(8,128)(2,1)S(1)}, bf16[18,16,256]{2,1,0:T(8,128)(2,1)S(1)}, u32[]{:S(2)}, u32[]{:S(2)}) collective-permute-start(bf16[18,16,256]{2,1,0:T(8,128)(2,1)S(1)} %get-tuple-element.26), channel_id=1, source_target_pairs={{0,3},{1,2},{2,1},{3,0},{4,7},{5,6},{6,5},{7,4},{8,11},{9,10},{10,... | collective-permute-start | bytes 442376 | tf_op jit(solution)/shard_map/ppermute | solution.py:16
  22.1 3.5 %collective-permute-done.10.refs_6_ = bf16[18,16,256]{2,1,0:T(8,128)(2,1)S(1)} collective-permute-done((bf16[18,16,256]{2,1,0:T(8,128)(2,1)S(1)}, bf16[18,16,256]{2,1,0:T(8,128)(2,1)S(1)}, u32[]{:S(2)}, u32[]{:S(2)}) %collective-permute-start.10) | collective-permute-done | bytes 147488 | tf_op jit(solution)/shard_map/ppermute | solution.py:16
  25.7 3.3 %collective-permute-done.9.refs_5_ = bf16[18,16,256]{2,1,0:T(8,128)(2,1)S(1)} collective-permute-done((bf16[18,16,256]{2,1,0:T(8,128)(2,1)S(1)}, bf16[18,16,256]{2,1,0:T(8,128)(2,1)S(1)}, u32[]{:S(2)}, u32[]{:S(2)}) %collective-permute-start.9) | collective-permute-done | bytes 147488 | tf_op jit(solution)/shard_map/ppermute | solution.py:16
  29.0 3.8 %collective-permute-start.12 = (bf16[4,1,56,128]{3,2,1,0:T(8,128)(2,1)S(1)}, bf16[4,1,56,128]{3,2,1,0:T(8,128)(2,1)S(1)}, u32[]{:S(2)}, u32[]{:S(2)}) collective-permute-start(bf16[4,1,56,128]{3,2,1,0:T(8,128)(2,1)S(1)} %lay_out.3.refs_3_), channel_id=1, source_target_pairs={{0,12},{1,13},{2,14},{3,15},{4,0},{5,1},{6,2},{7,3},{8,4},{9,5},{1... | collective-permute-start | bytes 172040 | tf_op jit(solution)/shard_map/ppermute | solution.py:16
  33.5 1.6 %collective-permute-start.15 = (bf16[1152,256]{1,0:T(8,128)(2,1)S(1)}, bf16[1152,256]{1,0:T(8,128)(2,1)S(1)}, u32[]{:S(2)}, u32[]{:S(2)}) collective-permute-start(bf16[1152,256]{1,0:T(8,128)(2,1)S(1)} %sort_weights.1.refs_0_), channel_id=1, source_target_pairs={{0,16},{16,0},{1,17},{17,1},{2,18},{18,2},{3,19},{19,3},{4,20},{20... | collective-permute-start | bytes 1769480 | tf_op jit(solution)/shard_map/ppermute | solution.py:16
  35.1 1.5 %collective-permute-done.4.refs_2_.refs_4_ = bf16[4,7,56,128]{3,2,1,0:T(8,128)(2,1)S(1)} collective-permute-done((bf16[4,7,56,128]{3,2,1,0:T(8,128)(2,1)S(1)}, bf16[4,7,56,128]{3,2,1,0:T(8,128)(2,1)S(1)}, u32[]{:S(2)}, u32[]{:S(2)}) %collective-permute-start.4) | collective-permute-done | bytes 401440 | tf_op jit(solution)/shard_map/ppermute | solution.py:16
  36.5 5.4 %convolve.2.conv_ref = bf16[1344,1152]{1,0:T(8,128)(2,1)S(1)} custom-call(s32[1]{0:T(128)} %bitcast.1.place_ref, f32[6,9,1536]{2,1,0:T(8,128)S(1)} %copy.7.packed_ref, bf16[4,7,56,128]{3,2,1,0:T(8,128)(2,1)S(1)} %collective-permute-done.3.refs_0_, bf16[4,7,56,128]{3,2,1,0:T(8,128)(2,1)S(1)} %lay_out.2.refs_1_.refs_2_, ...), custom_call_target="tpu_custom_call" | custom-call | flops 8999999488 | bytes 1 | tf_op jit(solution)/shard_map/convolve/pallas_call | solution.py:118
  42.0 1.1 %mix.3 = (f32[2,6,56,256]{3,2,1,0:T(8,128)S(1)}, bf16[2,6,56,256]{3,2,1,0:T(8,128)(2,1)S(1)}) custom-call(bf16[1344,1152]{1,0:T(8,128)(2,1)S(1)} %convolve.2.conv_ref, bf16[1152,256]{1,0:T(8,128)(2,1)S(1)} %sort_weights.1.refs_0_, bf16[4,1,56,128]{3,2,1,0:T(8,128)(2,1)S(1)} %collective-permute-done.11.refs_1_, ...), custom_call_target="tpu_custom_call" | custom-call | tf_op jit(solution)/shard_map/mix/pallas_call | solution.py:160
  43.2 1.5 %collective-permute-done.13.core_ref = bf16[2,6,56,256]{3,2,1,0:T(8,128)(2,1)S(1)} collective-permute-done((bf16[2,6,56,256]{3,2,1,0:T(8,128)(2,1)S(1)}, bf16[2,6,56,256]{3,2,1,0:T(8,128)(2,1)S(1)}, u32[]{:S(2)}, u32[]{:S(2)}) %collective-permute-start.13) | collective-permute-done | bytes 344096 | tf_op jit(solution)/shard_map/ppermute | solution.py:16
  44.8 1.6 %collective-permute-start.14 = (bf16[6,56,256]{2,1,0:T(8,128)(2,1)S(1)}, bf16[6,56,256]{2,1,0:T(8,128)(2,1)S(1)}, u32[]{:S(2)}, u32[]{:S(2)}) collective-permute-start(bf16[6,56,256]{2,1,0:T(8,128)(2,1)S(1)} %fusion), channel_id=1, source_target_pairs={{0,2},{1,3},{2,0},{3,1},{4,6},{5,7},{6,4},{7,5},{8,10},{9,11},{10,... | collective-permute-start | bytes 516104 | tf_op jit(solution)/shard_map/ppermute | solution.py:16
  46.4 1.8 %collective-permute-done.15.refs_0_.refs_1_ = bf16[1152,256]{1,0:T(8,128)(2,1)S(1)} collective-permute-done((bf16[1152,256]{1,0:T(8,128)(2,1)S(1)}, bf16[1152,256]{1,0:T(8,128)(2,1)S(1)}, u32[]{:S(2)}, u32[]{:S(2)}) %collective-permute-start.15) | collective-permute-done | bytes 589856 | tf_op jit(solution)/shard_map/ppermute | solution.py:16
  48.2 1.1 %mix.4 = (f32[2,6,56,256]{3,2,1,0:T(8,128)S(1)}, bf16[2,6,56,256]{3,2,1,0:T(8,128)(2,1)S(1)}) custom-call(bf16[1344,1152]{1,0:T(8,128)(2,1)S(1)} %convolve.2.conv_ref, bf16[1152,256]{1,0:T(8,128)(2,1)S(1)} %collective-permute-done.15.refs_0_.refs_1_), custom_call_target="tpu_custom_call" | custom-call | tf_op jit(solution)/shard_map/mix/pallas_call | solution.py:160
  49.3 1.8 %convolve.3.conv_ref = bf16[448,1152]{1,0:T(8,128)(2,1)S(1)} custom-call(s32[1]{0:T(128)} %bitcast.1.place_ref, f32[2,9,1536]{2,1,0:T(8,128)S(1)} %copy.8.packed_ref, bf16[4,7,56,128]{3,2,1,0:T(8,128)(2,1)S(1)} %collective-permute-done.3.refs_0_, bf16[4,1,56,128]{3,2,1,0:T(8,128)(2,1)S(1)} %collective-permute-done.11.refs_1_, ...), custom_call_target="tpu_custom_call" | custom-call | flops 8999999488 | bytes 1 | tf_op jit(solution)/shard_map/convolve/pallas_call | solution.py:118
  52.5 1.6 %collective-permute-start.17 = (bf16[6,56,256]{2,1,0:T(8,128)(2,1)S(1)}, bf16[6,56,256]{2,1,0:T(8,128)(2,1)S(1)}, u32[]{:S(2)}, u32[]{:S(2)}) collective-permute-start(bf16[6,56,256]{2,1,0:T(8,128)(2,1)S(1)} %fusion.1), channel_id=1, source_target_pairs={{0,2},{1,3},{2,0},{3,1},{4,6},{5,7},{6,4},{7,5},{8,10},{9,11},{10,... | collective-permute-start | bytes 516104 | tf_op jit(solution)/shard_map/ppermute | solution.py:16
  54.2 1.1 %collective-permute-start.19 = (bf16[2,56,512]{2,1,0:T(8,128)(2,1)S(1)}, bf16[2,56,512]{2,1,0:T(8,128)(2,1)S(1)}, u32[]{:S(2)}, u32[]{:S(2)}) collective-permute-start(bf16[2,56,512]{2,1,0:T(8,128)(2,1)S(1)} %fusion.2), channel_id=1, source_target_pairs={{0,2},{1,3},{2,0},{3,1},{4,6},{5,7},{6,4},{7,5},{8,10},{9,11},{10,... | collective-permute-start | bytes 344072 | tf_op jit(solution)/shard_map/ppermute | solution.py:16
  55.4 4.4 %collective-permute-done.17.across_ref = bf16[6,56,256]{2,1,0:T(8,128)(2,1)S(1)} collective-permute-done((bf16[6,56,256]{2,1,0:T(8,128)(2,1)S(1)}, bf16[6,56,256]{2,1,0:T(8,128)(2,1)S(1)}, u32[]{:S(2)}, u32[]{:S(2)}) %collective-permute-start.17) | collective-permute-done | bytes 172064 | tf_op jit(solution)/shard_map/ppermute | solution.py:16
  60.0 1.5 %collective-permute-done.19.refs_4_ = bf16[2,56,512]{2,1,0:T(8,128)(2,1)S(1)} collective-permute-done((bf16[2,56,512]{2,1,0:T(8,128)(2,1)S(1)}, bf16[2,56,512]{2,1,0:T(8,128)(2,1)S(1)}, u32[]{:S(2)}, u32[]{:S(2)}) %collective-permute-start.19) | collective-permute-done | bytes 114720 | tf_op jit(solution)/shard_map/ppermute | solution.py:16
  (51 shorter events, 10.1 us)
Async XLA Ops:
  0.0 1.0 %copy-start = (bf16[288,512]{1,0:T(8,128)(2,1)S(1)}, bf16[288,512]{1,0:T(8,128)(2,1)}, u32[]{:S(2)}) copy-start(bf16[288,512]{1,0:T(8,128)(2,1)} %param.7) | copy-start | bytes 884740
  1.0 11.2 %collective-permute-start.5 = (bf16[288,256]{1,0:T(8,128)(2,1)S(1)}, bf16[288,256]{1,0:T(8,128)(2,1)S(1)}, u32[]{:S(2)}, u32[]{:S(2)}) collective-permute-start(bf16[288,256]{1,0:T(8,128)(2,1)S(1)} %constant_dynamic-slice_fusion), channel_id=1, source_target_pairs={{0,8},{1,9},{2,10},{3,11},{4,12},{5,13},{6,14},{7,15},{8,0},{9,1},... | collective-permute-start | bytes 442376 | tf_op jit(solution)/shard_map/ppermute | solution.py:16
  5.1 14.2 %collective-permute-start.7 = (bf16[288,256]{1,0:T(8,128)(2,1)S(1)}, bf16[288,256]{1,0:T(8,128)(2,1)S(1)}, u32[]{:S(2)}, u32[]{:S(2)}) collective-permute-start(bf16[288,256]{1,0:T(8,128)(2,1)S(1)} %constant_dynamic-slice_fusion), channel_id=1, source_target_pairs={{0,4},{1,5},{2,6},{3,7},{4,0},{5,1},{6,2},{7,3},{8,12},{9,13},{10,... | collective-permute-start | bytes 442376 | tf_op jit(solution)/shard_map/ppermute | solution.py:16
  7.8 5.0 %collective-permute-start = (bf16[8,56,128]{2,1,0:T(8,128)(2,1)S(1)}, bf16[8,56,128]{2,1,0:T(8,128)(2,1)S(1)}, u32[]{:S(2)}, u32[]{:S(2)}) collective-permute-start(bf16[8,56,128]{2,1,0:T(8,128)(2,1)S(1)} %get-tuple-element.30), channel_id=1, source_target_pairs={{0,1},{1,0},{2,3},{3,2},{4,5},{5,4},{6,7},{7,6},{8,9},{9,8},{10,11... | collective-permute-start | bytes 344072 | tf_op jit(solution)/shard_map/ppermute | solution.py:16
  7.9 6.0 %collective-permute-start.1 = (bf16[8,56,128]{2,1,0:T(8,128)(2,1)S(1)}, bf16[8,56,128]{2,1,0:T(8,128)(2,1)S(1)}, u32[]{:S(2)}, u32[]{:S(2)}) collective-permute-start(bf16[8,56,128]{2,1,0:T(8,128)(2,1)S(1)} %get-tuple-element.32), channel_id=1, source_target_pairs={{0,2},{1,3},{2,0},{3,1},{4,6},{5,7},{6,4},{7,5},{8,10},{9,11},{10,... | collective-permute-start | bytes 344072 | tf_op jit(solution)/shard_map/ppermute | solution.py:16
  9.4 6.0 %collective-permute-start.2 = (bf16[8,56,128]{2,1,0:T(8,128)(2,1)S(1)}, bf16[8,56,128]{2,1,0:T(8,128)(2,1)S(1)}, u32[]{:S(2)}, u32[]{:S(2)}) collective-permute-start(bf16[8,56,128]{2,1,0:T(8,128)(2,1)S(1)} %get-tuple-element.29), channel_id=1, source_target_pairs={{0,3},{1,2},{2,1},{3,0},{4,7},{5,6},{6,5},{7,4},{8,11},{9,10},{10,... | collective-permute-start | bytes 344072 | tf_op jit(solution)/shard_map/ppermute | solution.py:16
  12.2 7.1 %collective-permute-start.6 = (bf16[288,256]{1,0:T(8,128)(2,1)S(1)}, bf16[288,256]{1,0:T(8,128)(2,1)S(1)}, u32[]{:S(2)}, u32[]{:S(2)}) collective-permute-start(bf16[288,256]{1,0:T(8,128)(2,1)S(1)} %collective-permute-done.5), channel_id=1, source_target_pairs={{0,4},{1,5},{2,6},{3,7},{4,0},{5,1},{6,2},{7,3},{8,12},{9,13},{10,... | collective-permute-start | bytes 442376 | tf_op jit(solution)/shard_map/ppermute | solution.py:16
  15.4 19.6 %collective-permute-start.3 = (bf16[4,7,56,128]{3,2,1,0:T(8,128)(2,1)S(1)}, bf16[4,7,56,128]{3,2,1,0:T(8,128)(2,1)S(1)}, u32[]{:S(2)}, u32[]{:S(2)}) collective-permute-start(bf16[4,7,56,128]{3,2,1,0:T(8,128)(2,1)S(1)} %lay_out.2.refs_1_.refs_2_), channel_id=1, source_target_pairs={{0,4},{1,5},{2,6},{3,7},{4,8},{5,9},{6,10},{7,11},{8,12},{9,13},{1... | collective-permute-start | bytes 1204232 | tf_op jit(solution)/shard_map/ppermute | solution.py:16
  15.9 20.6 %collective-permute-start.4 = (bf16[4,7,56,128]{3,2,1,0:T(8,128)(2,1)S(1)}, bf16[4,7,56,128]{3,2,1,0:T(8,128)(2,1)S(1)}, u32[]{:S(2)}, u32[]{:S(2)}) collective-permute-start(bf16[4,7,56,128]{3,2,1,0:T(8,128)(2,1)S(1)} %lay_out.2.refs_1_.refs_2_), channel_id=1, source_target_pairs={{0,12},{1,13},{2,14},{3,15},{4,0},{5,1},{6,2},{7,3},{8,4},{9,5},{1... | collective-permute-start | bytes 1204232 | tf_op jit(solution)/shard_map/ppermute | solution.py:16
  19.6 6.0 %collective-permute-start.10 = (bf16[18,16,256]{2,1,0:T(8,128)(2,1)S(1)}, bf16[18,16,256]{2,1,0:T(8,128)(2,1)S(1)}, u32[]{:S(2)}, u32[]{:S(2)}) collective-permute-start(bf16[18,16,256]{2,1,0:T(8,128)(2,1)S(1)} %get-tuple-element.26), channel_id=1, source_target_pairs={{0,3},{1,2},{2,1},{3,0},{4,7},{5,6},{6,5},{7,4},{8,11},{9,10},{10,... | collective-permute-start | bytes 442376 | tf_op jit(solution)/shard_map/ppermute | solution.py:16
  20.8 4.8 %collective-permute-start.8 = (bf16[18,16,256]{2,1,0:T(8,128)(2,1)S(1)}, bf16[18,16,256]{2,1,0:T(8,128)(2,1)S(1)}, u32[]{:S(2)}, u32[]{:S(2)}) collective-permute-start(bf16[18,16,256]{2,1,0:T(8,128)(2,1)S(1)} %get-tuple-element.28), channel_id=1, source_target_pairs={{0,1},{1,0},{2,3},{3,2},{4,5},{5,4},{6,7},{7,6},{8,9},{9,8},{10,11... | collective-permute-start | bytes 442376 | tf_op jit(solution)/shard_map/ppermute | solution.py:16
  21.3 7.7 %collective-permute-start.9 = (bf16[18,16,256]{2,1,0:T(8,128)(2,1)S(1)}, bf16[18,16,256]{2,1,0:T(8,128)(2,1)S(1)}, u32[]{:S(2)}, u32[]{:S(2)}) collective-permute-start(bf16[18,16,256]{2,1,0:T(8,128)(2,1)S(1)} %get-tuple-element.27), channel_id=1, source_target_pairs={{0,2},{1,3},{2,0},{3,1},{4,6},{5,7},{6,4},{7,5},{8,10},{9,11},{10,... | collective-permute-start | bytes 442376 | tf_op jit(solution)/shard_map/ppermute | solution.py:16
  29.0 12.9 %collective-permute-start.11 = (bf16[4,1,56,128]{3,2,1,0:T(8,128)(2,1)S(1)}, bf16[4,1,56,128]{3,2,1,0:T(8,128)(2,1)S(1)}, u32[]{:S(2)}, u32[]{:S(2)}) collective-permute-start(bf16[4,1,56,128]{3,2,1,0:T(8,128)(2,1)S(1)} %lay_out.3.refs_3_), channel_id=1, source_target_pairs={{0,4},{1,5},{2,6},{3,7},{4,8},{5,9},{6,10},{7,11},{8,12},{9,13},{1... | collective-permute-start | bytes 172040 | tf_op jit(solution)/shard_map/ppermute | solution.py:16
  29.0 12.9 %collective-permute-start.12 = (bf16[4,1,56,128]{3,2,1,0:T(8,128)(2,1)S(1)}, bf16[4,1,56,128]{3,2,1,0:T(8,128)(2,1)S(1)}, u32[]{:S(2)}, u32[]{:S(2)}) collective-permute-start(bf16[4,1,56,128]{3,2,1,0:T(8,128)(2,1)S(1)} %lay_out.3.refs_3_), channel_id=1, source_target_pairs={{0,12},{1,13},{2,14},{3,15},{4,0},{5,1},{6,2},{7,3},{8,4},{9,5},{1... | collective-permute-start | bytes 172040 | tf_op jit(solution)/shard_map/ppermute | solution.py:16
  33.5 14.7 %collective-permute-start.15 = (bf16[1152,256]{1,0:T(8,128)(2,1)S(1)}, bf16[1152,256]{1,0:T(8,128)(2,1)S(1)}, u32[]{:S(2)}, u32[]{:S(2)}) collective-permute-start(bf16[1152,256]{1,0:T(8,128)(2,1)S(1)} %sort_weights.1.refs_0_), channel_id=1, source_target_pairs={{0,16},{16,0},{1,17},{17,1},{2,18},{18,2},{3,19},{19,3},{4,20},{20... | collective-permute-start | bytes 1769480 | tf_op jit(solution)/shard_map/ppermute | solution.py:16
  43.0 1.7 %collective-permute-start.13 = (bf16[2,6,56,256]{3,2,1,0:T(8,128)(2,1)S(1)}, bf16[2,6,56,256]{3,2,1,0:T(8,128)(2,1)S(1)}, u32[]{:S(2)}, u32[]{:S(2)}) collective-permute-start(bf16[2,6,56,256]{3,2,1,0:T(8,128)(2,1)S(1)} %get-tuple-element.12), channel_id=1, source_target_pairs={{0,1},{1,0},{2,3},{3,2},{4,5},{5,4},{6,7},{7,6},{8,9},{9,8},{10,11... | collective-permute-start | bytes 1032200 | tf_op jit(solution)/shard_map/ppermute | solution.py:16
  44.8 6.5 %collective-permute-start.14 = (bf16[6,56,256]{2,1,0:T(8,128)(2,1)S(1)}, bf16[6,56,256]{2,1,0:T(8,128)(2,1)S(1)}, u32[]{:S(2)}, u32[]{:S(2)}) collective-permute-start(bf16[6,56,256]{2,1,0:T(8,128)(2,1)S(1)} %fusion), channel_id=1, source_target_pairs={{0,2},{1,3},{2,0},{3,1},{4,6},{5,7},{6,4},{7,5},{8,10},{9,11},{10,... | collective-permute-start | bytes 516104 | tf_op jit(solution)/shard_map/ppermute | solution.py:16
  49.3 3.2 %collective-permute-start.16 = (bf16[2,6,56,256]{3,2,1,0:T(8,128)(2,1)S(1)}, bf16[2,6,56,256]{3,2,1,0:T(8,128)(2,1)S(1)}, u32[]{:S(2)}, u32[]{:S(2)}) collective-permute-start(bf16[2,6,56,256]{3,2,1,0:T(8,128)(2,1)S(1)} %get-tuple-element.14), channel_id=1, source_target_pairs={{0,1},{1,0},{2,3},{3,2},{4,5},{5,4},{6,7},{7,6},{8,9},{9,8},{10,11... | collective-permute-start | bytes 1032200 | tf_op jit(solution)/shard_map/ppermute | solution.py:16
  52.0 2.1 %collective-permute-start.18 = (bf16[2,2,56,512]{3,2,1,0:T(8,128)(2,1)S(1)}, bf16[2,2,56,512]{3,2,1,0:T(8,128)(2,1)S(1)}, u32[]{:S(2)}, u32[]{:S(2)}) collective-permute-start(bf16[2,2,56,512]{3,2,1,0:T(8,128)(2,1)S(1)} %get-tuple-element.16), channel_id=1, source_target_pairs={{0,1},{1,0},{2,3},{3,2},{4,5},{5,4},{6,7},{7,6},{8,9},{9,8},{10,11... | collective-permute-start | bytes 688136 | tf_op jit(solution)/shard_map/ppermute | solution.py:16
  52.5 7.3 %collective-permute-start.17 = (bf16[6,56,256]{2,1,0:T(8,128)(2,1)S(1)}, bf16[6,56,256]{2,1,0:T(8,128)(2,1)S(1)}, u32[]{:S(2)}, u32[]{:S(2)}) collective-permute-start(bf16[6,56,256]{2,1,0:T(8,128)(2,1)S(1)} %fusion.1), channel_id=1, source_target_pairs={{0,2},{1,3},{2,0},{3,1},{4,6},{5,7},{6,4},{7,5},{8,10},{9,11},{10,... | collective-permute-start | bytes 516104 | tf_op jit(solution)/shard_map/ppermute | solution.py:16
  54.2 7.3 %collective-permute-start.19 = (bf16[2,56,512]{2,1,0:T(8,128)(2,1)S(1)}, bf16[2,56,512]{2,1,0:T(8,128)(2,1)S(1)}, u32[]{:S(2)}, u32[]{:S(2)}) collective-permute-start(bf16[2,56,512]{2,1,0:T(8,128)(2,1)S(1)} %fusion.2), channel_id=1, source_target_pairs={{0,2},{1,3},{2,0},{3,1},{4,6},{5,7},{6,4},{7,5},{8,10},{9,11},{10,... | collective-permute-start | bytes 344072 | tf_op jit(solution)/shard_map/ppermute | solution.py:16
